TPU v7x, 32 devices: a whole 2x2x4 slice. The times are simulated.
32 devices in a mesh: rep: 2 (over x), fsdp: 16 (over z, y, core).
Axes of the slice: x: 2, y: 2, z: 4, core: 2. Of those that a mesh axis runs over, the one named last changes fastest.
Arguments:
- tokens: bfloat16 [16, 1024, 512], P('fsdp', 'rep'), may hold values from -6 to 6
- cotangent: bfloat16 [16, 1024, 512], P('fsdp', 'rep'), may hold values from -6 to 6
- tags: int32 [16], P('fsdp'), may hold values from 0 to 1
- lengths: int32 [16], P('fsdp'), may hold values from 513 to 1024, as said below
- key_mask: int32 [16, 1024], P('fsdp'), may hold values 0 or 1
- master_qkv: float32 [2, 512, 1536], P(None, 'fsdp'), may hold values from -0.25 to 0.25
- master_out: float32 [2, 512, 512], P(None, 'fsdp'), may hold values from -1 to 1
- master_in: float32 [2, 512, 2048], P(None, 'fsdp'), may hold values from -0.25 to 0.25
- master_feed_output: float32 [2, 2048, 512], P(None, 'fsdp'), may hold values from -0.1875 to 0.1875
- master_vec: float32 [2, 14, 512], P(None, None, 'fsdp'), may hold values from -3 to 3
- first_qkv: float32 [2, 512, 1536], P(None, 'fsdp'), may hold values from -512 to 512
- first_out: float32 [2, 512, 512], P(None, 'fsdp'), may hold values from -48 to 48
- first_in: float32 [2, 512, 2048], P(None, 'fsdp'), may hold values from -224 to 224
- first_ffo: float32 [2, 2048, 512], P(None, 'fsdp'), may hold values from -320 to 320
- first_vec: float32 [2, 14, 512], P(None, None, 'fsdp'), may hold values from -448 to 448
- second_qkv: float32 [2, 512, 1536], P(None, 'fsdp'), may hold values from 8028.16 to 32112.64
- second_out: float32 [2, 512, 512], P(None, 'fsdp'), may hold values from 64 to 256
- second_in: float32 [2, 512, 2048], P(None, 'fsdp'), may hold values from 1474.56 to 5898.24
- second_ffo: float32 [2, 2048, 512], P(None, 'fsdp'), may hold values from 2621.44 to 10485.76
- second_moment_vector: float32 [2, 14, 512], P(None, None, 'fsdp'), may hold values from 5898.24 to 23592.96
Outputs:
- out_tokens: bfloat16 [16, 1024, 512], P('fsdp', 'rep')
- input_grad: float32 [16, 1024, 512], P('fsdp', 'rep')
- new_master_qkv: float32 [2, 512, 1536], P(None, 'fsdp')
- new_master_out: float32 [2, 512, 512], P(None, 'fsdp')
- new_master_in: float32 [2, 512, 2048], P(None, 'fsdp')
- new_master_ffo: float32 [2, 2048, 512], P(None, 'fsdp')
- new_master_vec: float32 [2, 14, 512], P(None, None, 'fsdp')
- new_first_qkv: float32 [2, 512, 1536], P(None, 'fsdp')
- new_first_out: float32 [2, 512, 512], P(None, 'fsdp')
- new_first_in: float32 [2, 512, 2048], P(None, 'fsdp')
- new_first_ffo: float32 [2, 2048, 512], P(None, 'fsdp')
- new_first_vec: float32 [2, 14, 512], P(None, None, 'fsdp')
- new_second_qkv: float32 [2, 512, 1536], P(None, 'fsdp')
- updated_second_output: float32 [2, 512, 512], P(None, 'fsdp')
- new_second_in: float32 [2, 512, 2048], P(None, 'fsdp')
- new_second_ffo: float32 [2, 2048, 512], P(None, 'fsdp')
- new_second_vec: float32 [2, 14, 512], P(None, None, 'fsdp')
Inputs may be any that keep to these rules, and one draw needn't show every extreme that they name: `lengths`: every sequence is longer than 512; one sequence of each draw has all 1024 positions.
All inputs are finite; a program needn't handle non-finite values. No bound on the sum of `key_mask` on one device may be relied on, other than what follows from the above.
Results may differ from a plain program's by a relative error of at most 0.018.
Values may be sent and summed in bfloat16 or wider, within the bound.
A program may use at most 192 MiB of HBM per device.

v0:
```python
import jax
import jax.numpy as jnp
from jax import lax
from jax.sharding import PartitionSpec as P

D = 512
H = 8
FF = 2048
STEP = 10


beta_decay = 0.5
epsilon_adam = 1e-08
weight_decay = 0.01
norm_epsilon = 1e-05
masked_score = -1000000000.0
vector_rate = 0.15
matrix_rate = 0.5


def layer_norm(pre_norm, gain_row, offset_row):
    centre_mean = jnp.mean(pre_norm, axis=-1, keepdims=True)
    centred = pre_norm - centre_mean
    variance = jnp.mean(centred * centred, axis=-1, keepdims=True)
    return centred * lax.rsqrt(variance + norm_epsilon) * gain_row + offset_row


def tanh_gelu_activation(inner_act):
    return jax.nn.gelu(inner_act, approximate=True)


def adamw(master, first, second, grad, rate, decay):
    first_new = beta_decay * first + (1.0 - beta_decay) * grad
    second_new = beta_decay * second + (1.0 - beta_decay) * grad * grad
    correction = 1.0 - beta_decay**STEP
    direction = first_new / correction / (jnp.sqrt(second_new / correction) + epsilon_adam)
    master_new = master - rate * (direction + decay * master)
    return (master_new, first_new, second_new)


def score_block(query_heads, key_heads, key_bias, score_scale):
    scores = jnp.einsum("qhd,khd->hqk", query_heads, key_heads, preferred_element_type=jnp.float32)
    return scores * score_scale + key_bias[None, None, :]


def forward_layer(input_rows, weights, tag_value, key_bias):
    w_qkv, w_out, w_in, w_ffo, vectors_low = weights
    vectors = vectors_low.astype(jnp.float32)
    model_width = w_out.shape[0]
    row_count = input_rows.shape[0]
    head_size = model_width // H
    score_scale = head_size ** (-0.5)
    direction = jnp.where(tag_value == 0, vectors[0], vectors[1])
    summed = input_rows + direction[None, :]
    summed_low = summed.astype(jnp.bfloat16)
    projected = jnp.dot(summed_low, w_qkv, preferred_element_type=jnp.float32)
    queries = (projected[:, :model_width] + vectors[2]).astype(jnp.bfloat16)
    keys_local = projected[:, model_width : 2 * model_width].astype(jnp.bfloat16)
    local_values = (projected[:, 2 * model_width :] + vectors[3]).astype(jnp.bfloat16)
    keys_all, values_all = (
        lax.all_gather(keys_local, "rep", axis=0, tiled=True),
        lax.all_gather(local_values, "rep", axis=0, tiled=True),
    )
    key_count = keys_all.shape[0]
    query_heads = queries.reshape(row_count, H, head_size)
    key_heads = keys_all.reshape(key_count, H, head_size)
    value_heads = values_all.reshape(key_count, H, head_size)
    scores = score_block(query_heads, key_heads, key_bias, score_scale)
    row_top = jnp.max(scores, axis=-1, keepdims=True)
    exponent_terms = jnp.exp(scores - row_top)
    totals = jnp.sum(exponent_terms, axis=-1, keepdims=True)
    soft_weights = exponent_terms / totals
    log_total = row_top + jnp.log(totals)
    context = jnp.einsum(
        "hqk,khd->qhd",
        soft_weights.astype(jnp.bfloat16),
        value_heads,
        preferred_element_type=jnp.float32,
    )
    context_low = context.reshape(row_count, model_width).astype(jnp.bfloat16)
    branch = jnp.dot(context_low, w_out, preferred_element_type=jnp.float32) + vectors[4]
    hidden, norm_first = jax.vjp(layer_norm, summed + branch, vectors[5], vectors[6])
    hidden_low = hidden.astype(jnp.bfloat16)
    inner_act = jnp.dot(hidden_low, w_in, preferred_element_type=jnp.float32) + vectors[
        10:
    ].reshape(-1)
    activated, gelu_pull = jax.vjp(tanh_gelu_activation, inner_act)
    activated_low = activated.astype(jnp.bfloat16)
    feed_out = jnp.dot(activated_low, w_ffo, preferred_element_type=jnp.float32) + vectors[7]
    result, norm_second = jax.vjp(layer_norm, hidden + feed_out, vectors[8], vectors[9])
    saved_state = (
        summed_low,
        query_heads,
        key_heads,
        value_heads,
        log_total,
        context_low,
        norm_first,
        hidden_low,
        gelu_pull,
        activated_low,
        norm_second,
    )
    return (result, saved_state)


def attention_grads(
    query_heads, key_heads, value_heads, log_total, context_heads, key_bias, score_scale
):
    row_count = query_heads.shape[0]
    model_width = query_heads.shape[1] * query_heads.shape[2]
    scores = score_block(query_heads, key_heads, key_bias, score_scale)
    soft_weights = jnp.exp(scores - log_total)
    grad_soft = jnp.einsum(
        "qhd,khd->hqk", context_heads, value_heads, preferred_element_type=jnp.float32
    )
    row_inner = jnp.sum(soft_weights * grad_soft, axis=-1, keepdims=True)
    grad_scores = (soft_weights * (grad_soft - row_inner) * score_scale).astype(jnp.bfloat16)
    grad_queries = jnp.einsum(
        "hqk,khd->qhd", grad_scores, key_heads, preferred_element_type=jnp.float32
    ).reshape(row_count, model_width)
    key_terms = jnp.einsum(
        "hqk,qhd->khd", grad_scores, query_heads, preferred_element_type=jnp.float32
    ).reshape(-1, model_width)
    value_terms = jnp.einsum(
        "hqk,qhd->khd",
        soft_weights.astype(jnp.bfloat16),
        context_heads,
        preferred_element_type=jnp.float32,
    ).reshape(-1, model_width)
    grad_keys, grad_values = (
        lax.psum_scatter(
            key_terms.astype(jnp.bfloat16), "rep", scatter_dimension=0, tiled=True
        ).astype(jnp.float32),
        lax.psum_scatter(
            value_terms.astype(jnp.bfloat16), "rep", scatter_dimension=0, tiled=True
        ).astype(jnp.float32),
    )
    return (grad_queries, grad_keys, grad_values)


def backward_layer(grad_result, saved_state, weights, tag_value, key_bias):
    w_qkv, w_out, w_in, w_ffo, vectors_low = weights
    (
        summed_low,
        query_heads,
        key_heads,
        value_heads,
        log_total,
        context_low,
        norm_first,
        hidden_low,
        gelu_pull,
        activated_low,
        norm_second,
    ) = saved_state
    model_width = w_out.shape[0]
    row_count = summed_low.shape[0]
    head_size = model_width // H
    score_scale = head_size ** (-0.5)
    grad_pre_two, grad_gain_two, grad_shift_two = norm_second(grad_result)
    grad_feed = grad_pre_two.astype(jnp.bfloat16)
    grad_bias_feed = jnp.sum(grad_feed.astype(jnp.float32), axis=0)
    grad_ffo = jnp.einsum("tf,td->fd", activated_low, grad_feed, preferred_element_type=jnp.float32)
    grad_activated = jnp.einsum("td,fd->tf", grad_feed, w_ffo, preferred_element_type=jnp.float32)
    grad_inner = gelu_pull(grad_activated)[0].astype(jnp.bfloat16)
    grad_bias_inner = jnp.sum(grad_inner.astype(jnp.float32), axis=0)
    grad_in = jnp.einsum("td,tf->df", hidden_low, grad_inner, preferred_element_type=jnp.float32)
    grad_hidden = grad_pre_two + jnp.einsum(
        "tf,df->td", grad_inner, w_in, preferred_element_type=jnp.float32
    )
    grad_pre_one, grad_gain_one, grad_shift_one = norm_first(grad_hidden)
    grad_branch = grad_pre_one.astype(jnp.bfloat16)
    grad_bias_out = jnp.sum(grad_branch.astype(jnp.float32), axis=0)
    grad_out_matrix = jnp.einsum(
        "te,td->ed", context_low, grad_branch, preferred_element_type=jnp.float32
    )
    grad_context = jnp.einsum(
        "td,ed->te", grad_branch, w_out, preferred_element_type=jnp.float32
    ).astype(jnp.bfloat16)
    context_heads = grad_context.reshape(row_count, H, head_size)
    grad_queries, grad_keys, grad_values = attention_grads(
        query_heads, key_heads, value_heads, log_total, context_heads, key_bias, score_scale
    )
    grad_joined = jnp.concatenate(
        [
            grad_queries.astype(jnp.bfloat16),
            grad_keys.astype(jnp.bfloat16),
            grad_values.astype(jnp.bfloat16),
        ],
        axis=1,
    )
    grad_qkv = jnp.einsum("td,te->de", summed_low, grad_joined, preferred_element_type=jnp.float32)
    grad_summed = grad_pre_one + jnp.einsum(
        "te,de->td", grad_joined, w_qkv, preferred_element_type=jnp.float32
    )
    column_sums = jnp.sum(grad_joined.astype(jnp.float32), axis=0)
    grad_direction = jnp.sum(grad_summed, axis=0)
    zero_row = jnp.zeros_like(grad_direction)
    grad_rows = jnp.stack(
        [
            jnp.where(tag_value == 0, grad_direction, zero_row),
            jnp.where(tag_value == 1, grad_direction, zero_row),
            column_sums[:model_width],
            column_sums[2 * model_width :],
            grad_bias_out,
            grad_gain_one,
            grad_shift_one,
            grad_bias_feed,
            grad_gain_two,
            grad_shift_two,
        ],
        axis=0,
    )
    grad_vectors = jnp.concatenate([grad_rows, grad_bias_inner.reshape(-1, model_width)], axis=0)
    return (grad_summed, (grad_qkv, grad_out_matrix, grad_in, grad_ffo, grad_vectors))


def reduce_layer(grads):
    shards = (
        lax.psum_scatter(grads[0], "fsdp", scatter_dimension=0, tiled=True),
        lax.psum_scatter(grads[1], "fsdp", scatter_dimension=0, tiled=True),
        lax.psum_scatter(grads[2], "fsdp", scatter_dimension=0, tiled=True),
        lax.psum_scatter(grads[3], "fsdp", scatter_dimension=0, tiled=True),
        lax.psum_scatter(grads[4], "fsdp", scatter_dimension=1, tiled=True),
    )
    return (
        lax.psum(shards[0].astype(jnp.bfloat16), "rep").astype(jnp.float32),
        lax.psum(shards[1].astype(jnp.bfloat16), "rep").astype(jnp.float32),
        lax.psum(shards[2].astype(jnp.bfloat16), "rep").astype(jnp.float32),
        lax.psum(shards[3].astype(jnp.bfloat16), "rep").astype(jnp.float32),
        lax.psum(shards[4].astype(jnp.bfloat16), "rep").astype(jnp.float32),
    )


def body(
    tokens,
    cotangent,
    tags,
    lengths,
    key_mask,
    master_qkv,
    master_out,
    master_in,
    master_feed_output,
    master_vec,
    first_qkv,
    first_out,
    first_in,
    first_ffo,
    first_vec,
    second_qkv,
    second_out,
    second_in,
    second_ffo,
    second_moment_vector,
):
    row_count = tokens.shape[1]
    key_count = key_mask.shape[1]
    start_row = lax.axis_index("rep") * row_count
    query_pos = start_row + jnp.arange(row_count, dtype=jnp.int32)
    key_pos = jnp.arange(key_count, dtype=jnp.int32)
    seq_length = lengths[0]
    tag_value = tags[0]
    key_valid = (key_pos < seq_length) & ((key_mask[0] == 1) | (key_pos == 0))
    key_bias = jnp.where(key_valid, 0.0, masked_score).astype(jnp.float32)
    query_valid = (query_pos < seq_length).astype(jnp.float32)
    masters = (master_qkv, master_out, master_in, master_feed_output, master_vec)
    firsts = (first_qkv, first_out, first_in, first_ffo, first_vec)
    seconds = (second_qkv, second_out, second_in, second_ffo, second_moment_vector)
    shared = (
        lax.all_gather(master_qkv[0].astype(jnp.bfloat16), "fsdp", axis=0, tiled=True),
        lax.all_gather(master_out[0].astype(jnp.bfloat16), "fsdp", axis=0, tiled=True),
        lax.all_gather(master_in[0].astype(jnp.bfloat16), "fsdp", axis=0, tiled=True),
        lax.all_gather(master_feed_output[0].astype(jnp.bfloat16), "fsdp", axis=0, tiled=True),
        lax.all_gather(master_vec[0].astype(jnp.bfloat16), "fsdp", axis=1, tiled=True),
    )
    shared_out, saved_shared = forward_layer(
        tokens[0].astype(jnp.float32), shared, tag_value, key_bias
    )
    unique = (
        lax.all_gather(master_qkv[1].astype(jnp.bfloat16), "fsdp", axis=0, tiled=True),
        lax.all_gather(master_out[1].astype(jnp.bfloat16), "fsdp", axis=0, tiled=True),
        lax.all_gather(master_in[1].astype(jnp.bfloat16), "fsdp", axis=0, tiled=True),
        lax.all_gather(master_feed_output[1].astype(jnp.bfloat16), "fsdp", axis=0, tiled=True),
        lax.all_gather(master_vec[1].astype(jnp.bfloat16), "fsdp", axis=1, tiled=True),
    )
    final_out, saved_unique = forward_layer(shared_out, unique, tag_value, key_bias)
    grad_final = cotangent[0].astype(jnp.float32) * query_valid[:, None]
    unique_back = (
        lax.all_gather(master_qkv[1].astype(jnp.bfloat16), "fsdp", axis=0, tiled=True),
        lax.all_gather(master_out[1].astype(jnp.bfloat16), "fsdp", axis=0, tiled=True),
        lax.all_gather(master_in[1].astype(jnp.bfloat16), "fsdp", axis=0, tiled=True),
        lax.all_gather(master_feed_output[1].astype(jnp.bfloat16), "fsdp", axis=0, tiled=True),
        lax.all_gather(master_vec[1].astype(jnp.bfloat16), "fsdp", axis=1, tiled=True),
    )
    grad_middle, unique_grads = backward_layer(
        grad_final, saved_unique, unique_back, tag_value, key_bias
    )
    reduced_unique = reduce_layer(unique_grads)
    grad_inputs, shared_grads = backward_layer(
        grad_middle, saved_shared, shared, tag_value, key_bias
    )
    reduced_shared = reduce_layer(shared_grads)
    rates = (
        matrix_rate * D ** (-0.5),
        matrix_rate * (D // 16) ** (-0.5),
        matrix_rate * D ** (-0.5),
        matrix_rate * (FF // 2) ** (-0.5),
        vector_rate,
    )
    decays = (weight_decay, weight_decay, weight_decay, weight_decay, 0.0)
    updated = []
    for kind_index in range(5):
        grad_stack = jnp.stack([reduced_shared[kind_index], reduced_unique[kind_index]], axis=0)
        updated.append(
            adamw(
                masters[kind_index],
                firsts[kind_index],
                seconds[kind_index],
                grad_stack,
                rates[kind_index],
                decays[kind_index],
            )
        )
    return (
        final_out.astype(jnp.bfloat16)[None],
        grad_inputs[None],
        updated[0][0],
        updated[1][0],
        updated[2][0],
        updated[3][0],
        updated[4][0],
        updated[0][1],
        updated[1][1],
        updated[2][1],
        updated[3][1],
        updated[4][1],
        updated[0][2],
        updated[1][2],
        updated[2][2],
        updated[3][2],
        updated[4][2],
    )


def solution(mesh):
    placed = (
        P("fsdp", "rep", None),
        P("fsdp", "rep", None),
        P("fsdp"),
        P("fsdp"),
        P("fsdp", None),
        P(None, "fsdp", None),
        P(None, "fsdp", None),
        P(None, "fsdp", None),
        P(None, "fsdp", None),
        P(None, None, "fsdp"),
        P(None, "fsdp", None),
        P(None, "fsdp", None),
        P(None, "fsdp", None),
        P(None, "fsdp", None),
        P(None, None, "fsdp"),
        P(None, "fsdp", None),
        P(None, "fsdp", None),
        P(None, "fsdp", None),
        P(None, "fsdp", None),
        P(None, None, "fsdp"),
    )
    return jax.shard_map(
        body,
        mesh=mesh,
        in_specs=placed,
        out_specs=(
            P("fsdp", "rep", None),
            P("fsdp", "rep", None),
            P(None, "fsdp", None),
            P(None, "fsdp", None),
            P(None, "fsdp", None),
            P(None, "fsdp", None),
            P(None, None, "fsdp"),
            P(None, "fsdp", None),
            P(None, "fsdp", None),
            P(None, "fsdp", None),
            P(None, "fsdp", None),
            P(None, None, "fsdp"),
            P(None, "fsdp", None),
            P(None, "fsdp", None),
            P(None, "fsdp", None),
            P(None, "fsdp", None),
            P(None, None, "fsdp"),
        ),
        check_vma=False,
    )
```

profile of v0, /device:TPU:0, one launch (start us, length us, event | category | flops | bytes accessed | tf_op | source)
XLA Modules:
  0.0 1294.2 jit_solution(14532192392042811786)
XLA Ops:
  10.5 23.9 %all-gather = bf16[1,14,512]{1,0,2:T(2,128)(2,1)S(1)} all-gather(bf16[1,14,32]{1,0,2:T(2,128)(2,1)S(1)} %get-tuple-element.170), channel_id=2, replica_groups=mesh['rep'=2,'fsdp'=16] {'fsdp'}, dimensions={2}, use_global_device_ids=true | all-gather | bytes 15232 | tf_op jit(solution)/shard_map/all_gather | solution.py:276
  36.0 15.3 %slice_reduce_fusion.9 = (f32[512]{0:T(512)S(1)}, f32[512]{0:T(512)S(1)}, f32[512]{0:T(512)S(1)}, f32[512]{0:T(512)S(1)}, f32[512]{0:T(512)S(1)}, /*index=5*/f32...) fusion(f32[1,14,512]{1,0,2:T(1,128)S(1)} %convert_element_type.376, pred[]{:T(512)} %bitcast.1), kind=kLoop, calls=%fused_computation.189 | loop fusion | flops 512 | bytes 38913 | tf_op jit(solution)/shard_map/slice | solution.py:90
  51.3 2.2 all-gather.29.cloned.1.call-done
  53.5 2.5 fusion.84
  58.6 2.6 fusion.134
  64.9 20.2 %all-gather.5 = bf16[1,14,512]{1,0,2:T(2,128)(2,1)S(1)} all-gather(bf16[1,14,32]{1,0,2:T(2,128)(2,1)S(1)} %get-tuple-element.169), channel_id=7, replica_groups=mesh['rep'=2,'fsdp'=16] {'fsdp'}, dimensions={2}, use_global_device_ids=true | all-gather | bytes 15232 | tf_op jit(solution)/shard_map/all_gather | solution.py:286
  85.6 15.3 %slice_reduce_fusion.1 = (f32[512]{0:T(512)S(1)}, f32[512]{0:T(512)S(1)}, f32[512]{0:T(512)S(1)}, f32[512]{0:T(512)S(1)}, f32[512]{0:T(512)S(1)}, /*index=5*/f32...) fusion(f32[1,14,512]{1,0,2:T(1,128)S(1)} %convert_element_type.377, pred[]{:T(512)} %bitcast.1), kind=kLoop, calls=%fused_computation.181 | loop fusion | flops 512 | bytes 38913 | tf_op jit(solution)/shard_map/slice | solution.py:90
  100.9 19.7 %all-gather.2 = bf16[1,512,512]{2,1,0:T(8,128)(2,1)S(1)} all-gather(bf16[1,32,512]{2,1,0:T(8,128)(2,1)S(1)} %get-tuple-element.168), channel_id=4, replica_groups=mesh['rep'=2,'fsdp'=16] {'fsdp'}, dimensions={1}, use_global_device_ids=true | all-gather | bytes 557056 | tf_op jit(solution)/shard_map/all_gather | solution.py:273
  122.5 2.6 fusion.207
  125.1 5.8 copy-done
  130.9 3.7 fusion.8
  136.2 8.0 fusion.131
  144.9 1.9 all-gather.31.cloned.1.call-done
  146.8 5.0 fusion.72
  151.8 37.8 %all-gather.33.cloned.1.call-done = bf16[1,2048,512]{2,1,0:T(8,128)(2,1)} async-done(((bf16[1,128,512]{2,1,0:T(8,128)(2,1)}), bf16[1,2048,512]{2,1,0:T(8,128)(2,1)}) %all-gather.33.cloned.1.call-update) | async-done | bytes 2097168 | tf_op jit(solution)/shard_map/all_gather | solution.py:275
  189.6 5.0 fusion.209
  194.9 35.9 %all-gather.35.cloned.1.call-done = bf16[1,512,1536]{2,1,0:T(8,128)(2,1)} async-done(((bf16[1,32,1536]{2,1,0:T(8,128)(2,1)}), bf16[1,512,1536]{2,1,0:T(8,128)(2,1)}) %all-gather.35.cloned.1.call-update) | async-done | bytes 1572880 | tf_op jit(solution)/shard_map/all_gather | solution.py:282
  230.8 2.6 fusion.80
  236.0 2.6 fusion.132
  240.7 22.4 %all-gather.7 = bf16[1,512,512]{2,1,0:T(8,128)(2,1)} all-gather(bf16[1,32,512]{2,1,0:T(8,128)(2,1)S(1)} %get-tuple-element.167), channel_id=9, replica_groups=mesh['rep'=2,'fsdp'=16] {'fsdp'}, dimensions={1}, use_global_device_ids=true | all-gather | bytes 557056 | tf_op jit(solution)/shard_map/all_gather | solution.py:283
  265.3 2.6 fusion.210
  267.9 5.7 copy-done.1
  273.6 3.7 fusion.9
  277.3 2.4 all-gather.25.cloned.1.call-done
  281.3 7.9 fusion.130
  290.2 33.7 %all-gather.37.cloned.1.call-done = bf16[1,512,2048]{2,1,0:T(8,128)(2,1)} async-done(((bf16[1,32,2048]{2,1,0:T(8,128)(2,1)}), bf16[1,512,2048]{2,1,0:T(8,128)(2,1)}) %all-gather.37.cloned.1.call-update) | async-done | bytes 2097168 | tf_op jit(solution)/shard_map/all_gather | solution.py:284
  323.9 4.9 fusion.64
  328.9 37.8 %all-gather.39.cloned.1.call-done = bf16[1,2048,512]{2,1,0:T(8,128)(2,1)} async-done(((bf16[1,128,512]{2,1,0:T(8,128)(2,1)}), bf16[1,2048,512]{2,1,0:T(8,128)(2,1)}) %all-gather.39.cloned.1.call-update) | async-done | bytes 2097168 | tf_op jit(solution)/shard_map/all_gather | solution.py:285
  366.7 5.2 fusion.212
  374.2 4.0 convert_reduce_fusion
  381.8 3.8 fusion.92
  385.6 9.3 fusion.214
  395.0 30.8 %fusion.89 = bf16[8,64,1024]{2,1,0:T(8,128)(2,1)} fusion(bf16[512,8,64]{0,2,1:T(8,128)(2,1)} %bitcast.240, f32[8,512,1024]{2,1,0:T(8,128)} %fusion.214, f32[8,512,1024]{2,1,0:T(8,128)} %copy-done.1, f32[8,512]{1,0:T(8,128)S(1)} %log_add_fusion.1), kind=kOutput, calls=%fused_computation.93 | convolution fusion | flops 566760448 | bytes 35143680 | tf_op jit(solution)/shard_map/hqk,qhd->khd/dot_general | solution.py:122
  425.9 37.5 %fusion.127 = bf16[8,64,512]{2,1,0:T(8,128)(2,1)} fusion(bf16[1024,8,64]{0,2,1:T(8,128)(2,1)S(1)} %bitcast.234, f32[8,512,1024]{2,1,0:T(8,128)} %fusion.214, f32[8,512,1024]{2,1,0:T(8,128)} %copy-done.1, f32[8,512]{1,0:T(8,128)S(1)} %log_add_fusion.1), kind=kOutput, calls=%fused_computation.109 | convolution fusion | flops 566498304 | bytes 35143680 | tf_op jit(solution)/shard_map/hqk,khd->qhd/dot_general | solution.py:119
  463.4 3.9 multiply_reduce_fusion.3
  467.9 1.8 copy-done.15
  469.7 3.8 convert_reduce_fusion.1
  478.0 3.8 fusion.95
  481.9 9.3 fusion.215
  491.2 30.9 %fusion.86 = bf16[8,64,1024]{2,1,0:T(8,128)(2,1)} fusion(bf16[512,8,64]{0,2,1:T(8,128)(2,1)} %bitcast.238, f32[8,512,1024]{2,1,0:T(8,128)} %fusion.215, f32[8,512,1024]{2,1,0:T(8,128)} %copy-done, f32[8,512]{1,0:T(8,128)S(1)} %log_add_fusion), kind=kOutput, calls=%fused_computation.92 | convolution fusion | flops 566760448 | bytes 35143680 | tf_op jit(solution)/shard_map/hqk,qhd->khd/dot_general | solution.py:122
  522.2 2.5 fusion.217
  527.5 2.5 fusion.216
  530.1 30.0 %fusion.124 = bf16[8,64,512]{2,1,0:T(8,128)(2,1)} fusion(bf16[1024,8,64]{0,2,1:T(8,128)(2,1)} %bitcast.232, f32[8,512,1024]{2,1,0:T(8,128)} %fusion.215, f32[8,512,1024]{2,1,0:T(8,128)} %copy-done, f32[8,512]{1,0:T(8,128)S(1)} %log_add_fusion), kind=kOutput, calls=%fused_computation.108 | convolution fusion | flops 566498304 | bytes 35143680 | tf_op jit(solution)/shard_map/hqk,khd->qhd/dot_general | solution.py:119
  561.8 3.9 fusion.213
  566.7 6.3 fusion.191
  573.1 5.0 fusion.181
  579.3 3.8 fusion.180
  583.3 6.4 fusion.190
  591.3 3.3 fusion.184
  596.1 2.7 fusion.157
  599.0 3.6 reduce-scatter.33.cloned.1.call-done
  604.0 57.2 %reduce-scatter.45.cloned.1.call-done = f32[32,14]{1,0:T(8,128)} async-done(((f32[512,14]{1,0:T(8,128)}), f32[32,14]{1,0:T(8,128)}) %reduce-scatter.45.cloned.1.call-update) | async-done | bytes 1808
  662.7 59.0 %reduce-scatter.31.cloned.1.call-done = f32[32,512]{1,0:T(8,128)} async-done(((f32[512,512]{1,0:T(8,128)}), f32[32,512]{1,0:T(8,128)}) %reduce-scatter.31.cloned.1.call-update) | async-done | bytes 65552 | tf_op jit(solution)/shard_map/reduce_scatter | solution.py:222
  723.1 56.8 %reduce-scatter.43.cloned.1.call-done = f32[32,14]{1,0:T(8,128)} async-done(((f32[512,14]{1,0:T(8,128)}), f32[32,14]{1,0:T(8,128)}) %reduce-scatter.43.cloned.1.call-update) | async-done | bytes 1808
  781.3 73.9 %reduce-scatter.41.cloned.1.call-done = f32[128,512]{1,0:T(8,128)} async-done(((f32[2048,512]{1,0:T(8,128)}), f32[128,512]{1,0:T(8,128)}) %reduce-scatter.41.cloned.1.call-update) | async-done | bytes 262160 | tf_op jit(solution)/shard_map/reduce_scatter | solution.py:224
  856.9 74.0 %reduce-scatter.37.cloned.1.call-done = f32[32,2048]{1,0:T(8,128)} async-done(((f32[512,2048]{1,0:T(8,128)}), f32[32,2048]{1,0:T(8,128)}) %reduce-scatter.37.cloned.1.call-update) | async-done | bytes 262160 | tf_op jit(solution)/shard_map/reduce_scatter | solution.py:223
  932.5 67.4 %reduce-scatter.29.cloned.1.call-done = f32[32,1536]{1,0:T(8,128)} async-done(((f32[512,1536]{1,0:T(8,128)}), f32[32,1536]{1,0:T(8,128)}) %reduce-scatter.29.cloned.1.call-update) | async-done | bytes 196624 | tf_op jit(solution)/shard_map/reduce_scatter | solution.py:221
  1001.5 73.8 %reduce-scatter.39.cloned.1.call-done = f32[128,512]{1,0:T(8,128)} async-done(((f32[2048,512]{1,0:T(8,128)}), f32[128,512]{1,0:T(8,128)}) %reduce-scatter.39.cloned.1.call-update) | async-done | bytes 262160 | tf_op jit(solution)/shard_map/reduce_scatter | solution.py:224
  1076.9 74.2 %reduce-scatter.35.cloned.1.call-done = f32[32,2048]{1,0:T(8,128)} async-done(((f32[512,2048]{1,0:T(8,128)}), f32[32,2048]{1,0:T(8,128)}) %reduce-scatter.35.cloned.1.call-update) | async-done | bytes 262160 | tf_op jit(solution)/shard_map/reduce_scatter | solution.py:223
  1152.7 67.2 %reduce-scatter.27.cloned.1.call-done = f32[32,1536]{1,0:T(8,128)} async-done(((f32[512,1536]{1,0:T(8,128)}), f32[32,1536]{1,0:T(8,128)}) %reduce-scatter.27.cloned.1.call-update) | async-done | bytes 196624 | tf_op jit(solution)/shard_map/reduce_scatter | solution.py:221
  1223.8 19.7 %all-reduce.5.cloned.1.call-done = (bf16[1,32,512]{2,1,0:T(8,128)(2,1)}, bf16[1,32,512]{2,1,0:T(8,128)(2,1)}, bf16[1,14,32]{2,1,0:T(8,128)(2,1)}, bf16[1,14,32]{2,1,0:T(8,128)(2,1)}) async-done(((bf16[1,32,512]{2,1,0:T(8,128)(2,1)}, bf16[1,32,512]{2,1,0:T(8,128)(2,1)}, bf16[1,14,32]{2,1,0:T(8,128)(2,1)}, bf16[1,14,32]{2,1,0:T(8,128)(2,1)}), (bf16[1,32,512]{2,1,0:T(8,128)(2,1)}, ...) | async-done | bytes 67344 | tf_op jit(solution)/shard_map/psum | solution.py:229
  1247.9 33.2 %all-reduce.7.cloned.1.call-done = (bf16[1,32,1536]{2,1,0:T(8,128)(2,1)}, bf16[1,32,1536]{2,1,0:T(8,128)(2,1)}, bf16[1,32,2048]{2,1,0:T(8,128)(2,1)}, bf16[1,32,...) async-done(((bf16[1,32,1536]{2,1,0:T(8,128)(2,1)}, bf16[1,32,1536]{2,1,0:T(8,128)(2,1)}, bf16[1,32,2048]{2,1,0:T(8,128)(2,1)}, ...) | async-done | bytes 720912 | tf_op jit(solution)/shard_map/psum | solution.py:228
  1281.2 2.3 multiply_subtract_fusion.2
  1283.5 2.6 multiply_subtract_fusion.1
  (312 shorter events, 68.2 us)
Async XLA Ops:
  7.2 46.3 %all-gather.29.cloned.1.call-start = ((), (), s32[]{:S(2)}) async-start(), calls=%async_computation.30 | async-start | bytes 1671168 | tf_op jit(solution)/shard_map/all_gather | solution.py:272
  9.0 111.9 %all-gather.23.cloned.1.call-start = ((), (), s32[]{:S(2)}) async-start(), calls=%async_computation.15 | async-start | bytes 1572864 | tf_op jit(solution)/shard_map/all_gather | solution.py:61
  36.0 108.2 %copy-start.51 = (bf16[1,512,512]{1,2,0:T(8,128)(2,1)}, bf16[1,512,512]{1,2,0:T(8,128)(2,1)S(1)}, u32[]{:S(2)}) copy-start(bf16[1,512,512]{1,2,0:T(8,128)(2,1)S(1)} %copy.106) | copy-start | bytes 1572868
  51.3 92.9 %copy-start.67 = (f32[512]{0:T(512)}, f32[512]{0:T(512)S(1)}, u32[]{:S(2)}) copy-start(f32[512]{0:T(512)S(1)} %get-tuple-element.115) | copy-start | bytes 6148
  51.3 138.3 %copy-start.63 = (f32[512]{0:T(512)}, f32[512]{0:T(512)S(1)}, u32[]{:S(2)}) copy-start(f32[512]{0:T(512)S(1)} %get-tuple-element.110) | copy-start | bytes 6148
  57.7 7.2 copy-start.66
  57.7 7.2 copy-start.53
  58.6 76.1 %all-gather.21.cloned.1.call-start = ((), (), s32[]{:S(2)}) async-start(), calls=%async_computation.14 | async-start | bytes 1572864 | tf_op jit(solution)/shard_map/all_gather | solution.py:62
  61.3 85.5 %all-gather.31.cloned.1.call-start = ((), (), s32[]{:S(2)}) async-start(), calls=%async_computation.31 | async-start | bytes 2228224 | tf_op jit(solution)/shard_map/all_gather | solution.py:274
  62.1 127.5 %all-gather.33.cloned.1.call-start = ((), (), s32[]{:S(2)}) async-start(), calls=%async_computation.32 | async-start | bytes 2228224 | tf_op jit(solution)/shard_map/all_gather | solution.py:275
  63.0 167.8 %all-gather.35.cloned.1.call-start = ((), (), s32[]{:S(2)}) async-start(), calls=%async_computation.33 | async-start | bytes 1671168 | tf_op jit(solution)/shard_map/all_gather | solution.py:282
  63.5 200.1 %all-gather.27.cloned.1.call-start = ((), (), s32[]{:S(2)}) async-start(), calls=%async_computation.17 | async-start | bytes 1572864 | tf_op jit(solution)/shard_map/all_gather | solution.py:61
  120.6 23.6 %copy-start.28 = (bf16[1,512,512]{2,1,0:T(8,128)(2,1)}, bf16[1,512,512]{2,1,0:T(8,128)(2,1)S(1)}, u32[]{:S(2)}) copy-start(bf16[1,512,512]{2,1,0:T(8,128)(2,1)S(1)} %all-gather.2) | copy-start | bytes 1572868
  125.1 5.8 copy-start
  136.2 8.0 copy-start.2
  144.1 7.7 copy-start.58
  194.7 38.7 %copy-start.17 = (f32[512,512]{0,1:T(8,128)}, f32[512,512]{0,1:T(8,128)S(1)}, u32[]{:S(2)}) copy-start(f32[512,512]{0,1:T(8,128)S(1)} %get-tuple-element.186) | copy-start | bytes 3145732
  235.0 28.1 %copy-start.50 = (bf16[1,512,512]{2,1,0:T(8,128)(2,1)S(1)}, bf16[1,512,512]{2,1,0:T(8,128)(2,1)}, u32[]{:S(2)}) copy-start(bf16[1,512,512]{2,1,0:T(8,128)(2,1)} %param.21) | copy-start | bytes 1572868
  235.9 43.8 %all-gather.25.cloned.1.call-start = ((), (), s32[]{:S(2)}) async-start(), calls=%async_computation.16 | async-start | bytes 1572864 | tf_op jit(solution)/shard_map/all_gather | solution.py:62
  238.6 85.3 %all-gather.37.cloned.1.call-start = ((), (), s32[]{:S(2)}) async-start(), calls=%async_computation.34 | async-start | bytes 2228224 | tf_op jit(solution)/shard_map/all_gather | solution.py:284
  239.4 127.3 %all-gather.39.cloned.1.call-start = ((), (), s32[]{:S(2)}) async-start(), calls=%async_computation.35 | async-start | bytes 2228224 | tf_op jit(solution)/shard_map/all_gather | solution.py:285
  239.9 223.5 %reduce-scatter.21.cloned.1.call-start = ((), (), s32[]{:S(2)}) async-start(), calls=%async_computation.19 | async-start | bytes 1572864 | tf_op jit(solution)/shard_map/reduce_scatter | solution.py:135
  267.9 5.7 copy-start.1
  281.2 7.9 copy-start.4
  281.2 7.9 copy-start.18
  281.3 7.9 copy-start.31
  366.7 7.5 copy-start.70
  374.2 6.9 slice-start.4
  374.2 6.9 slice-start.5
  374.2 6.9 slice-start.6
  385.6 77.8 %reduce-scatter.19.cloned.1.call-start = ((), (), s32[]{:S(2)}) async-start(), calls=%async_computation.18 | async-start | bytes 1572864 | tf_op jit(solution)/shard_map/reduce_scatter | solution.py:132
  395.0 30.9 %copy-start.14 = (bf16[1024,512]{0,1:T(8,128)(2,1)S(1)}, bf16[1024,512]{0,1:T(8,128)(2,1)}, u32[]{:S(2)}) copy-start(bf16[1024,512]{0,1:T(8,128)(2,1)} %copy-done.13) | copy-start | bytes 3145732
  425.8 134.3 %reduce-scatter.25.cloned.1.call-start = ((), (), s32[]{:S(2)}) async-start(), calls=%async_computation.21 | async-start | bytes 1572864 | tf_op jit(solution)/shard_map/reduce_scatter | solution.py:135
  469.7 8.2 slice-start
  469.7 8.2 slice-start.1
  469.7 8.3 slice-start.2
  475.6 6.3 copy-start.21
  475.7 6.1 copy-start.10
  481.8 78.3 %reduce-scatter.23.cloned.1.call-start = ((), (), s32[]{:S(2)}) async-start(), calls=%async_computation.20 | async-start | bytes 1572864 | tf_op jit(solution)/shard_map/reduce_scatter | solution.py:132
  491.2 31.0 %copy-start.9 = (bf16[512,512]{0,1:T(8,128)(2,1)S(1)}, bf16[512,512]{0,1:T(8,128)(2,1)}, u32[]{:S(2)}) copy-start(bf16[512,512]{0,1:T(8,128)(2,1)} %copy-done.8) | copy-start | bytes 1572868
  522.2 80.4 %reduce-scatter.33.cloned.1.call-start = ((), (), s32[]{:S(2)}) async-start(), calls=%async_computation.25 | async-start | bytes 1114112 | tf_op jit(solution)/shard_map/reduce_scatter | solution.py:222
  524.8 136.5 %reduce-scatter.45.cloned.1.call-start = ((), (), s32[]{:S(2)}) async-start(), calls=%async_computation.37 | async-start | bytes 278528
  527.5 194.1 %reduce-scatter.31.cloned.1.call-start = ((), (), s32[]{:S(2)}) async-start(), calls=%async_computation.24 | async-start | bytes 1114112 | tf_op jit(solution)/shard_map/reduce_scatter | solution.py:222
  530.0 249.9 %reduce-scatter.43.cloned.1.call-start = ((), (), s32[]{:S(2)}) async-start(), calls=%async_computation.36 | async-start | bytes 278528
  530.1 31.7 %copy-start.22 = (f32[512,512]{0,1:T(8,128)S(1)}, f32[512,512]{0,1:T(8,128)}, u32[]{:S(2)}) copy-start(f32[512,512]{0,1:T(8,128)} %copy-done.21) | copy-start | bytes 3145732
  566.6 288.6 %reduce-scatter.41.cloned.1.call-start = ((), (), s32[]{:S(2)}) async-start(), calls=%async_computation.29 | async-start | bytes 4456448 | tf_op jit(solution)/shard_map/reduce_scatter | solution.py:224
  573.0 357.9 %reduce-scatter.37.cloned.1.call-start = ((), (), s32[]{:S(2)}) async-start(), calls=%async_computation.27 | async-start | bytes 4456448 | tf_op jit(solution)/shard_map/reduce_scatter | solution.py:223
  578.1 421.8 %reduce-scatter.29.cloned.1.call-start = ((), (), s32[]{:S(2)}) async-start(), calls=%async_computation.23 | async-start | bytes 3342336 | tf_op jit(solution)/shard_map/reduce_scatter | solution.py:221
  583.1 492.2 %reduce-scatter.39.cloned.1.call-start = ((), (), s32[]{:S(2)}) async-start(), calls=%async_computation.28 | async-start | bytes 4456448 | tf_op jit(solution)/shard_map/reduce_scatter | solution.py:224
  589.8 561.3 %reduce-scatter.35.cloned.1.call-start = ((), (), s32[]{:S(2)}) async-start(), calls=%async_computation.26 | async-start | bytes 4456448 | tf_op jit(solution)/shard_map/reduce_scatter | solution.py:223
  594.7 625.2 %reduce-scatter.27.cloned.1.call-start = ((), (), s32[]{:S(2)}) async-start(), calls=%async_computation.22 | async-start | bytes 3342336 | tf_op jit(solution)/shard_map/reduce_scatter | solution.py:221
  598.9 622.6 %copy-start.26 = (bf16[1,512,512]{1,2,0:T(8,128)(2,1)S(1)}, bf16[1,512,512]{1,2,0:T(8,128)(2,1)}, u32[]{:S(2)}) copy-start(bf16[1,512,512]{1,2,0:T(8,128)(2,1)} %get-tuple-element.160) | copy-start | bytes 1572868
  598.9 623.6 %copy-start.42 = (f32[512,512]{0,1:T(8,128)S(1)}, f32[512,512]{0,1:T(8,128)}, u32[]{:S(2)}) copy-start(f32[512,512]{0,1:T(8,128)} %get-tuple-element.199) | copy-start | bytes 3145732
  598.9 644.7 %copy-start.65 = (f32[2,14,32]{2,0,1:T(2,128)S(1)}, f32[2,14,32]{2,0,1:T(2,128)}, u32[]{:S(2)}) copy-start(f32[2,14,32]{2,0,1:T(2,128)} %param.29) | copy-start | bytes 10756
  598.9 647.2 %copy-start.54 = (f32[2,32,512]{2,1,0:T(8,128)S(1)}, f32[2,32,512]{2,1,0:T(8,128)}, u32[]{:S(2)}) copy-start(f32[2,32,512]{2,1,0:T(8,128)} %param.26) | copy-start | bytes 393220
  598.9 682.3 %copy-start.41 = (f32[2,32,1536]{2,1,0:T(8,128)S(1)}, f32[2,32,1536]{2,1,0:T(8,128)}, u32[]{:S(2)}) copy-start(f32[2,32,1536]{2,1,0:T(8,128)} %param.25) | copy-start | bytes 1179652
  598.9 682.3 %copy-start.60 = (f32[2,32,1536]{2,1,0:T(8,128)S(1)}, f32[2,32,1536]{2,1,0:T(8,128)}, u32[]{:S(2)}) copy-start(f32[2,32,1536]{2,1,0:T(8,128)} %param.30) | copy-start | bytes 1179652
  598.9 644.6 %all-reduce.5.cloned.1.call-start = ((), (), s32[]{:S(2)}) async-start(), calls=%async_computation.38 | async-start | bytes 147456 | tf_op jit(solution)/shard_map/psum | solution.py:229
  781.3 499.9 %all-reduce.7.cloned.1.call-start = ((), (), s32[]{:S(2)}) async-start(), calls=%async_computation.39 | async-start | bytes 1441792 | tf_op jit(solution)/shard_map/psum | solution.py:228
  1076.9 206.6 %copy-start.33 = (f32[2,32,2048]{2,1,0:T(8,128)S(1)}, f32[2,32,2048]{2,1,0:T(8,128)}, u32[]{:S(2)}) copy-start(f32[2,32,2048]{2,1,0:T(8,128)} %param.27) | copy-start | bytes 1572868
  1076.9 206.6 %copy-start.55 = (f32[2,32,2048]{2,1,0:T(8,128)S(1)}, f32[2,32,2048]{2,1,0:T(8,128)}, u32[]{:S(2)}) copy-start(f32[2,32,2048]{2,1,0:T(8,128)} %param.32) | copy-start | bytes 1572868
  1222.5 63.5 %copy-start.35 = (f32[2,128,512]{2,1,0:T(8,128)S(1)}, f32[2,128,512]{2,1,0:T(8,128)}, u32[]{:S(2)}) copy-start(f32[2,128,512]{2,1,0:T(8,128)} %param.28) | copy-start | bytes 1572868
  1223.8 62.2 %copy-start.56 = (f32[2,128,512]{2,1,0:T(8,128)S(1)}, f32[2,128,512]{2,1,0:T(8,128)}, u32[]{:S(2)}) copy-start(f32[2,128,512]{2,1,0:T(8,128)} %param.33) | copy-start | bytes 1572868
  1223.8 62.2 %copy-start.57 = (f32[2,128,512]{2,1,0:T(8,128)S(1)}, f32[2,128,512]{2,1,0:T(8,128)}, u32[]{:S(2)}) copy-start(f32[2,128,512]{2,1,0:T(8,128)} %param.38) | copy-start | bytes 1572868
  (41 other events, 132.4 us)
Sparse Core Ops, SparseCore 0:
  10.9 42.5 all-gather.28
  58.7 20.1 all-gather.22
  81.1 21.2 all-gather.20
  105.0 41.7 all-gather.30
  149.4 40.1 all-gather.32
  192.3 38.4 all-gather.34
  236.1 20.1 all-gather.26
  258.4 21.2 all-gather.24
  282.5 41.3 all-gather.36
  326.5 40.1 all-gather.38
  385.7 19.1 reduce-scatter.20
  425.9 19.0 reduce-scatter.18
  482.0 19.1 reduce-scatter.24
  522.3 19.0 reduce-scatter.22
  544.9 57.6 reduce-scatter.32
  606.9 54.2 reduce-scatter.44
  665.2 56.4 reduce-scatter.30
  725.6 54.2 reduce-scatter.42
  783.7 71.4 reduce-scatter.40
  859.5 71.4 reduce-scatter.36
  934.7 65.1 reduce-scatter.28
  1003.8 71.4 reduce-scatter.38
  1079.6 71.4 reduce-scatter.34
  1154.7 65.1 reduce-scatter.26
  1223.5 20.0 all-reduce.4
  1247.2 33.9 all-reduce.6
where the time goes:
time: 1300 us; the launch traced here: 1290 us
  waiting for transfers between devices  814 us (63%)
  matrix products  255 us (20%)
  blocking collectives  86.2 us (7%)
  other arithmetic  74 us (6%)
  local copies, waits for them, and re-layouts  46.7 us (4%)
  between operations  16.8 us (1%)
    reduce_scatter x2, waiting for transfers between devices, reduce_layer(): lax.psum_scatter(grads[2], 'fsdp', scatter_dimension=0, tiled=True)  148 us
    reduce_scatter x2, waiting for transfers between devices, reduce_layer(): lax.psum_scatter(grads[3], 'fsdp', scatter_dimension=0, tiled=True)  148 us
    reduce_scatter x2, waiting for transfers between devices, reduce_layer(): lax.psum_scatter(grads[0], 'fsdp', scatter_dimension=0, tiled=True)  135 us
    unnamed x28, waiting for transfers between devices  116 us
    dot_general x2, matrix products, attention_grads(): jnp.einsum('hqk,khd->qhd', grad_scores, key_heads, preferred_element_type...  67.6 us
    reduce_scatter x2, waiting for transfers between devices, reduce_layer(): lax.psum_scatter(grads[1], 'fsdp', scatter_dimension=0, tiled=True)  62.5 us
    dot_general x2, matrix products, attention_grads(): jnp.einsum('hqk,qhd->khd', grad_scores, query_heads, preferred_element_ty...  61.8 us
    all_gather x1, waiting for transfers between devices, body(): lax.all_gather(master_feed_output[1].astype(jnp.bfloat16), 'fsdp', axis=0...  37.8 us
  transfers between devices with their start and end apart: 26, of which 19 were waited for; matrix products, arithmetic and copies ran while one was open for 24% of the time, Pallas kernels for 0%

commit v1 on v0

--- a/solution.py
+++ b/solution.py
@@ -1,6 +1,12 @@
+import functools
+from types import SimpleNamespace
+from typing import NamedTuple
+
 import jax
 import jax.numpy as jnp
 from jax import lax
+from jax.experimental import pallas as pl
+from jax.experimental.pallas import tpu as pltpu
 from jax.sharding import PartitionSpec as P
 
 D = 512
@@ -344,6 +350,1272 @@
     )
 
 
+BF = jnp.bfloat16
+F32 = jnp.float32
+MESH = pl.DeviceIdType.MESH
+KIND_K, KIND_V, KIND_Q, KIND_O, KIND_I, KIND_F = KINDS = tuple(range(6))
+VMEM_BYTES = 60 << 20
+
+
+def nt_dot(left, right):
+    return lax.dot_general(left, right, (((1,), (1,)), ((), ())), preferred_element_type=F32)
+
+
+def nn_dot(left, right):
+    return jnp.dot(left, right, preferred_element_type=F32)
+
+
+def remote(src, dst, send_sem, recv_sem, device):
+    return pltpu.make_async_remote_copy(
+        src_ref=src,
+        dst_ref=dst,
+        send_sem=send_sem,
+        recv_sem=recv_sem,
+        device_id=device,
+        device_id_type=MESH,
+    )
+
+
+class ForwardIn(NamedTuple):
+    tok: object
+    cot: object
+    meta: object
+    vecb: object
+    masters: object
+
+
+class Saved(NamedTuple):
+    w_o: object
+    vec_o: object
+    meta_o: object
+    cot_o: object
+    y_o: object
+    at_o: object
+    q_o: object
+    k_o: object
+    v_o: object
+    lse_o: object
+    ct_o: object
+    ctp_o: object
+    n1_o: object
+    r1_o: object
+    ht_o: object
+    g_o: object
+    gp_o: object
+    n2_o: object
+    r2_o: object
+
+
+class ForwardScratch(NamedTuple):
+    w: object
+    stages: object
+    vecg: object
+    vec: object
+    metab: object
+    msel: object
+    tokb: object
+    A32: object
+    Ab: object
+    ATp: object
+    Q: object
+    K: object
+    V: object
+    lse: object
+    CT: object
+    CTp: object
+    C: object
+    N1: object
+    r1: object
+    H32: object
+    Hb: object
+    HTp: object
+    G: object
+    Gp: object
+    N2: object
+    r2: object
+    X: object
+    Yb: object
+    msem: object
+    xsem: object
+    osem: object
+    gs: object
+    gr: object
+    vs: object
+    vr: object
+    xs: object
+    xr: object
+    ks: object
+    kr: object
+
+
+class BackwardOut(NamedTuple):
+    fin: object
+    vec_g: object
+    yo: object
+    dxo: object
+
+
+class BackwardScratch(NamedTuple):
+    g: object
+    landing: object
+    half_y: object
+    half_x: object
+    quarter_x: object
+    quarter_y: object
+    level: object
+    total: object
+    w: object
+    AT: object
+    Q: object
+    K: object
+    V: object
+    lse: object
+    CT: object
+    CTp: object
+    N1: object
+    r1: object
+    HT: object
+    G: object
+    Gp: object
+    N2: object
+    r2: object
+    vec: object
+    msel: object
+    cotb: object
+    dy: object
+    dpre: object
+    dF: object
+    dFT: object
+    dU: object
+    dZ: object
+    delta: object
+    dQT: object
+    dvb: object
+    dkp: object
+    dvp: object
+    dkr: object
+    dvr: object
+    vg: object
+    va: object
+    vrecv: object
+    vb: object
+    vt: object
+    lsem: object
+    ssem: object
+    fsem: object
+    gs: object
+    gr: object
+    xs: object
+    xr: object
+    ks: object
+    kr: object
+    vs: object
+    vr: object
+
+
+class UpdateIn(NamedTuple):
+    fin: object
+    fvec: object
+    y: object
+    dx: object
+    masters: object
+    firsts: object
+    seconds: object
+
+
+class UpdateOut(NamedTuple):
+    out: object
+    grad: object
+    new_masters: object
+    new_firsts: object
+    new_seconds: object
+
+
+def named(parts, refs):
+    fields, at = {}, 0
+    for part in parts:
+        leaves, tree = jax.tree.flatten(part)
+        fields.update(tree.unflatten(refs[at : at + len(leaves)])._asdict())
+        at += len(leaves)
+    return SimpleNamespace(**fields)
+
+
+def call_kernel(kernel, args, outs, scratch, spec, **options):
+    leaves, _ = jax.tree.flatten(args)
+    out_leaves, out_tree = jax.tree.flatten(outs)
+    parts = (args, outs) if scratch is None else (args, outs, scratch)
+    empty = jax.tree.map(lambda leaf: 0, parts)
+    results = pl.pallas_call(
+        functools.partial(kernel, empty),
+        out_shape=out_leaves,
+        in_specs=[spec] * len(leaves),
+        out_specs=[spec] * len(out_leaves),
+        scratch_shapes=() if scratch is None else jax.tree.leaves(scratch),
+        compiler_params=pltpu.CompilerParams(**options),
+    )(*leaves)
+    return out_tree.unflatten(results)
+
+
+class Place:
+    def __init__(self):
+        self.r = lax.axis_index("rep")
+        self.f = lax.axis_index("fsdp")
+        self.z = lax.div(self.f, 4)
+        self.y = lax.rem(lax.div(self.f, 2), 2)
+        self.c = lax.rem(self.f, 2)
+        self.xn = (1 - self.r, self.f)
+        self.yn = (self.r, self.f + 2 - 4 * self.y)
+        self.cn = (self.r, self.f + 1 - 2 * self.c)
+        self.dn = (1 - self.r, self.f + 1 - 2 * self.c)
+
+    def zn(self, step, levels):
+        other = lax.rem(self.z + step, levels)
+        return other, (self.r, other * 4 + 2 * self.y + self.c)
+
+
+def parity_rows(rows, shards):
+    blocks = rows.reshape(shards // 2, 2, rows.shape[0] // shards, rows.shape[1])
+    half = rows.shape[0] // 2
+    return blocks[:, 0].reshape(half, rows.shape[1]), blocks[:, 1].reshape(half, rows.shape[1])
+
+
+def lane_masks():
+    lane = lax.broadcasted_iota(jnp.int32, (16, 128), 1)
+    low = (lane < 64).astype(F32)
+    spots = (lax.rem(lane, 64) == 0).astype(F32)
+    return low[:1].astype(BF), (1.0 - low[:1]).astype(BF), spots[:1].astype(BF)
+
+
+def sizes_of(mesh_n, width, inner):
+    shard = width // mesh_n
+    rows = [shard // 2] * 6
+    rows[KIND_F] = inner // mesh_n // 2
+    cols = [width] * 6
+    cols[KIND_I] = inner
+    return rows, cols
+
+
+def forward_kernel(parts, levels, eps, *refs):
+    R = named(parts, refs)
+    me = Place()
+    r, f, z, y, c = me.r, me.f, me.z, me.y, me.c
+    shards = levels * 4
+    S, D = R.A32.shape
+    FF = R.G.shape[1]
+    ha = levels // 2
+    first, second = pl.ds(0, ha), pl.ds(ha, levels - ha)
+    source = ((0, D), (0, 2 * D), (0, 0), (1, 0), (2, 0), (3, 0))
+
+    half_loads = {}
+    for l in range(2):
+        for at, (master, stage) in enumerate(zip(R.masters, R.stages)):
+            rows = stage.shape[1]
+            cp = pltpu.make_async_copy(master.at[l, pl.ds(r * rows, rows)], stage.at[l], R.msem.at[l, at])
+            cp.start()
+            half_loads[(l, at)] = cp
+    vec_local = pltpu.make_async_copy(R.vecb, R.vecg.at[f], R.xsem.at[0])
+    vec_local.start()
+    meta_local = pltpu.make_async_copy(R.meta, R.metab.at[0], R.xsem.at[1])
+    meta_local.start()
+
+    barrier = pltpu.get_barrier_semaphore()
+    peers = [(r, lax.rem(f + s, shards)) for s in range(1, shards)] + [me.xn, me.dn]
+    for peer in peers:
+        pl.semaphore_signal(barrier, inc=1, device_id=peer, device_id_type=MESH)
+    pl.semaphore_wait(barrier, len(peers))
+
+    chunks = [(kind, l) for l in range(2) for kind in KINDS]
+    gs, gr = R.gs, R.gr
+    pending = []
+
+    def start(cp):
+        cp.start()
+        pending.append(cp)
+        return cp
+
+    loaded = set()
+    stage_copies = {}
+
+    def g_z(i):
+        kind, l = chunks[i]
+        w = R.w[kind]
+        at, offset = source[kind]
+        if (l, at) not in loaded:
+            half_loads[(l, at)].wait()
+            loaded.add((l, at))
+        w[l, z, y, c, r] = R.stages[at][l][:, offset : offset + w.shape[-1]].astype(BF)
+        cps = []
+        for s in range(1, levels):
+            _, dev = me.zn(s, levels)
+            spot = w.at[l, z, y, c, r]
+            cps.append(start(remote(spot, spot, gs.at[i, s - 1], gr.at[i, s - 1], dev)))
+        stage_copies[i] = cps
+
+    def g_1(i):
+        kind, l = chunks[i]
+        w = R.w[kind]
+        for cp in stage_copies[i]:
+            cp.wait_recv()
+        a, b = w.at[l, first, y, c, r], w.at[l, second, y, c, r]
+        stage_copies[i] = [
+            start(remote(a, a, gs.at[i, levels - 1], gr.at[i, levels - 1], me.xn)),
+            start(remote(b, b, gs.at[i, levels], gr.at[i, levels], me.yn)),
+        ]
+
+    def g_2(i):
+        kind, l = chunks[i]
+        w = R.w[kind]
+        for cp in stage_copies[i]:
+            cp.wait_recv()
+        a, b = w.at[l, first, y, c], w.at[l, second, :, c, r]
+        stage_copies[i] = [
+            start(remote(a, a, gs.at[i, levels + 1], gr.at[i, levels + 1], me.yn)),
+            start(remote(b, b, gs.at[i, levels + 2], gr.at[i, levels + 2], me.xn)),
+        ]
+
+    def g_core(i):
+        kind, l = chunks[i]
+        w = R.w[kind]
+        for cp in stage_copies[i]:
+            cp.wait_recv()
+        a = w.at[l, :, :, c]
+        stage_copies[i] = [start(remote(a, a, gs.at[i, levels + 3], gr.at[i, levels + 3], me.cn))]
+
+    def g_ready(i):
+        for cp in stage_copies.pop(i):
+            cp.wait_recv()
+
+    tick_at = [0]
+
+    def tick():
+        t = tick_at[0]
+        tick_at[0] += 1
+        for lag, step in ((4, g_ready), (3, g_core), (2, g_2), (1, g_1), (0, g_z)):
+            if 0 <= t - lag < len(chunks):
+                step(t - lag)
+
+    g_z(0)
+    meta_cp = start(remote(R.meta, R.metab.at[1], R.xs.at[0], R.xr.at[0], me.cn))
+    vec_cps = []
+    for s in range(1, shards):
+        spot = R.vecg.at[f]
+        vec_cps.append((s, remote(R.vecb, spot, R.vs.at[s - 1], R.vr.at[s - 1], (r, lax.rem(f + s, shards)))))
+    for _, cp in vec_cps:
+        start(cp)
+    tok_far = remote(R.tok.at[0], R.tokb, R.xs.at[1], R.xr.at[1], me.dn)
+    tok_near = pltpu.make_async_copy(R.tok.at[0], R.tokb, R.xsem.at[2])
+    stays = c == r
+
+    @pl.when(stays)
+    def _():
+        tok_near.start()
+
+    @pl.when(jnp.logical_not(stays))
+    def _():
+        tok_far.start()
+
+    tick_at[0] = 1
+    tick()
+    tick()
+
+    vec_local.wait()
+    meta_local.wait()
+    meta_cp.wait_recv()
+    for _, cp in vec_cps:
+        cp.wait_recv()
+    keep = stays.astype(F32)
+    msel = R.msel
+    msel[...] = (R.metab[0].astype(F32) * keep + R.metab[1].astype(F32) * (1.0 - keep)).astype(BF)
+    vec = R.vec
+    for zz in range(levels):
+        vec[:, 128 * zz : 128 * zz + 128] = jnp.sum(R.vecg[4 * zz : 4 * zz + 4].astype(F32), axis=0)
+    tag_row = msel[2 * S : 2 * S + 16].astype(F32)[:1]
+    tag_row = jnp.concatenate([tag_row] * (D // 128), axis=1)
+    low, high, spots = lane_masks()
+
+    out_copies = {}
+    out_at = [0]
+
+    def out(ref, dst, view=None):
+        cp = pltpu.make_async_copy(ref if view is None else view, dst, R.osem.at[out_at[0]])
+        out_at[0] += 1
+        cp.start()
+        out_copies[(id(ref), view is not None and out_at[0])] = cp
+
+    def settle(ref):
+        if (id(ref), False) in out_copies:
+            out_copies.pop((id(ref), False)).wait()
+
+    @pl.when(stays)
+    def _():
+        tok_near.wait()
+
+    @pl.when(jnp.logical_not(stays))
+    def _():
+        tok_far.wait()
+
+    T = 128
+    for l in range(2):
+        e = lambda row: vec[16 * l + row : 16 * l + row + 1, :]
+        direction = e(0) * (1.0 - tag_row) + e(1) * tag_row
+        A32, Ab, Q, K, V, CT = R.A32, R.Ab, R.Q, R.K, R.V, R.CT
+        x_in = R.tokb if l == 0 else R.X
+        summed = x_in[...].astype(F32) + direction
+        A32[...] = summed
+        Ab[...] = summed.astype(BF)
+        at = Ab[...].T
+        even, odd = parity_rows(at, shards)
+        settle(R.ATp)
+        R.ATp[: D // 2] = even
+        R.ATp[D // 2 :] = odd
+        out(R.ATp, R.at_o.at[l])
+
+        def weight(kind, lo=0, hi=None):
+            w = R.w[kind]
+            hi = w.shape[-1] if hi is None else hi
+            value = w[l, :, :, :, :, :, lo:hi]
+            return value.reshape(-1, hi - lo)
+
+        if l == 0:
+            tick()
+            tick()
+        K[l, c] = nn_dot(Ab[...], weight(KIND_K)).astype(BF)
+        k_cp = start(remote(K.at[l, c], K.at[l, c], R.ks.at[l, 0], R.kr.at[l, 0], me.cn))
+        if l == 0:
+            tick()
+        V[l, c] = (nn_dot(Ab[...], weight(KIND_V)) + e(3)).astype(BF)
+        v_cp = start(remote(V.at[l, c], V.at[l, c], R.ks.at[l, 1], R.kr.at[l, 1], me.cn))
+        if l == 0:
+            tick()
+        settle(R.Q)
+        q = (nn_dot(Ab[...], weight(KIND_Q)) + e(2)).astype(BF)
+        Q[...] = (q.astype(F32) * 0.125).astype(BF)
+        out(R.Q, R.q_o.at[l])
+        k_cp.wait_recv()
+        v_cp.wait_recv()
+        out(K, R.k_o.at[l], K.at[l])
+        out(V, R.v_o.at[l], V.at[l])
+        lse = R.lse
+        settle(R.lse)
+        settle(R.CT)
+        bias_rows = msel[: 2 * S]
+
+        def pair(j, carry):
+            sl = pl.ds(pl.multiple_of(j * 128, 128), 128)
+            k2 = K[l, :, :, sl].reshape(2 * S, 128)
+            v2t = V[l, :, :, sl].reshape(2 * S, 128).T
+            q2 = Q[:, sl]
+            for h in range(2):
+                mine, other = (low, high) if h == 0 else (high, low)
+                kh = k2 * mine + bias_rows * other
+                qh = q2 * mine + spots * other
+                for part in range(S // 256):
+                    cols = slice(part * 256, part * 256 + 256)
+                    st = nt_dot(kh, qh[cols])
+                    top = jnp.max(st, axis=0, keepdims=True)
+                    p = jnp.exp(st - top)
+                    total = jnp.sum(p, axis=0, keepdims=True)
+                    ctx = nn_dot(v2t, p.astype(BF))[64 * h : 64 * h + 64]
+                    rows = pl.ds(pl.multiple_of(j * 128 + 64 * h, 64), 64)
+                    CT[rows, cols] = (ctx / total).astype(BF)
+                    lse[j, h : h + 1, cols] = top + jnp.log(total)
+            return carry
+
+        pairs = D // 128
+        lax.fori_loop(0, pairs // 2, pair, 0)
+        if l == 0:
+            tick()
+        lax.fori_loop(pairs // 2, pairs, pair, 0)
+        out(R.lse, R.lse_o.at[l])
+        out(R.CT, R.ct_o.at[l])
+        even, odd = parity_rows(CT[...], shards)
+        settle(R.CTp)
+        R.CTp[: D // 2] = even
+        R.CTp[D // 2 :] = odd
+        out(R.CTp, R.ctp_o.at[l])
+        R.C[...] = CT[...].T
+        settle(R.N1)
+        settle(R.r1)
+
+        def norm_one(t, carry):
+            rows = pl.ds(pl.multiple_of(t * T, T), T)
+            pre = A32[rows] + nn_dot(R.C[rows], weight(KIND_O)) + e(4)
+            mean = jnp.mean(pre, axis=-1, keepdims=True)
+            centred = pre - mean
+            rstd = lax.rsqrt(jnp.mean(centred * centred, axis=-1, keepdims=True) + eps)
+            n1 = centred * rstd
+            hidden = n1 * e(5) + e(6)
+            R.N1[rows] = n1
+            R.r1[rows] = jnp.broadcast_to(rstd, (T, 128))
+            R.H32[rows] = hidden
+            R.Hb[rows] = hidden.astype(BF)
+            return carry
+
+        lax.fori_loop(0, S // T, norm_one, 0)
+        out(R.N1, R.n1_o.at[l])
+        out(R.r1, R.r1_o.at[l])
+        even, odd = parity_rows(R.Hb[...].T, shards)
+        settle(R.HTp)
+        R.HTp[: D // 2] = even
+        R.HTp[D // 2 :] = odd
+        out(R.HTp, R.ht_o.at[l])
+        if l == 0:
+            tick()
+        settle(R.G)
+        settle(R.Gp)
+
+        def inner(t, carry):
+            rows = pl.ds(pl.multiple_of(t * T, T), T)
+            hb = R.Hb[rows]
+            for b in range(FF // D):
+                u = nn_dot(hb, weight(KIND_I, b * D, b * D + D)) + e(10 + b)
+                u2 = u * u
+                th = jnp.tanh(u * (0.7978845608028654 + 0.035677408136300125 * u2))
+                half = 0.5 + 0.5 * th
+                slope = 0.7978845608028654 + 0.10703222440890038 * u2
+                R.G[rows, b * D : b * D + D] = (u * half).astype(BF)
+                R.Gp[rows, b * D : b * D + D] = (half + 0.5 * u * (1.0 - th * th) * slope).astype(BF)
+            return carry
+
+        lax.fori_loop(0, S // T, inner, 0)
+        out(R.G, R.g_o.at[l])
+        out(R.Gp, R.gp_o.at[l])
+        if l == 0:
+            tick()
+        settle(R.N2)
+        settle(R.r2)
+
+        def norm_two(t, carry):
+            rows = pl.ds(pl.multiple_of(t * T, T), T)
+            pre = R.H32[rows] + nn_dot(R.G[rows], weight(KIND_F)) + e(7)
+            mean = jnp.mean(pre, axis=-1, keepdims=True)
+            centred = pre - mean
+            rstd = lax.rsqrt(jnp.mean(centred * centred, axis=-1, keepdims=True) + eps)
+            n2 = centred * rstd
+            R.N2[rows] = n2
+            R.r2[rows] = jnp.broadcast_to(rstd, (T, 128))
+            R.X[rows] = n2 * e(8) + e(9)
+            return carry
+
+        lax.fori_loop(0, S // T, norm_two, 0)
+        out(R.N2, R.n2_o.at[l])
+        out(R.r2, R.r2_o.at[l])
+        if l == 0:
+            while tick_at[0] < len(chunks) + 4:
+                tick()
+            for kind in KINDS:
+                out(R.w[kind], R.w_o[kind])
+
+    R.Yb[...] = R.X[...].astype(BF)
+    out(R.Yb, R.y_o)
+    out(vec, R.vec_o)
+    out(msel, R.meta_o)
+    cot_far = remote(R.cot.at[0], R.cot_o, R.xs.at[2], R.xr.at[2], me.dn)
+    cot_near = pltpu.make_async_copy(R.cot.at[0], R.cot_o, R.xsem.at[3])
+
+    @pl.when(stays)
+    def _():
+        cot_near.start()
+
+    @pl.when(jnp.logical_not(stays))
+    def _():
+        cot_far.start()
+
+    for cp in out_copies.values():
+        cp.wait()
+    for cp in pending:
+        cp.wait_send()
+
+    @pl.when(stays)
+    def _():
+        cot_near.wait()
+
+    @pl.when(jnp.logical_not(stays))
+    def _():
+        cot_far.wait()
+
+
+def backward_kernel(parts, levels, *refs):
+    R = named(parts, refs)
+    me = Place()
+    r, f, z, y, c = me.r, me.f, me.z, me.y, me.c
+    shards = levels * 4
+    S, D = R.dy.shape
+    FF = R.G.shape[1]
+    ha = levels // 2
+    hb = levels - ha
+    first, second = pl.ds(0, ha), pl.ds(ha, hb)
+    saved = list(zip(R.w, R.w_o)) + [
+        (R.AT, R.at_o), (R.Q, R.q_o), (R.K, R.k_o), (R.V, R.v_o), (R.lse, R.lse_o), (R.CT, R.ct_o), (R.CTp, R.ctp_o),
+        (R.N1, R.n1_o), (R.r1, R.r1_o), (R.HT, R.ht_o), (R.G, R.g_o), (R.Gp, R.gp_o), (R.N2, R.n2_o), (R.r2, R.r2_o),
+    ]
+    order = {id(ref): at for at, (ref, _) in enumerate(saved)}
+    loads = {}
+
+    def load(ref, l):
+        at = order[id(ref)]
+        cp = pltpu.make_async_copy(saved[at][1].at[l], ref, R.lsem.at[l, at])
+        cp.start()
+        loads[id(ref)] = cp
+
+    def use(ref):
+        if id(ref) in loads:
+            loads.pop(id(ref)).wait()
+        return ref
+
+    small = []
+    for at, (dst, src) in enumerate(((R.vec, R.vec_o), (R.msel, R.meta_o), (R.cotb, R.cot_o))):
+        cp = pltpu.make_async_copy(src, dst, R.ssem.at[at])
+        cp.start()
+        small.append(cp)
+    wk, wv, wq, wo, wi, wf = R.w
+    for ref in (R.N2, R.r2, R.G, wf, R.Gp, R.HT, wi, R.N1, R.r1, R.CTp, wo, R.CT, R.K, R.V, R.Q, R.lse, R.AT, wq, wk, wv):
+        load(ref, 1)
+
+    barrier = pltpu.get_barrier_semaphore()
+    peers = [me.zn(s, levels)[1] for s in range(1, levels)] + [me.xn, me.yn, me.cn, me.dn]
+    for peer in peers:
+        pl.semaphore_signal(barrier, inc=1, device_id=peer, device_id_type=MESH)
+    pl.semaphore_wait(barrier, len(peers))
+
+    pending = []
+
+    def start(cp):
+        cp.start()
+        pending.append(cp)
+        return cp
+
+    stays = c == r
+    y_far = remote(R.y_o, R.yo, R.xs.at[0], R.xr.at[0], me.dn)
+    y_near = pltpu.make_async_copy(R.y_o, R.yo, R.ssem.at[3])
+
+    @pl.when(stays)
+    def _():
+        y_near.start()
+
+    @pl.when(jnp.logical_not(stays))
+    def _():
+        y_far.start()
+
+    gs, gr = R.gs, R.gr
+    chunks = [(kind, l) for l in (1, 0) for kind in (KIND_F, KIND_I, KIND_O, KIND_Q, KIND_K, KIND_V)]
+    index = {chunk: at for at, chunk in enumerate(chunks)}
+    flight = {}
+    stage = {}
+    fin_copies = []
+
+    def rs_core(i):
+        kind, l = chunks[i]
+        g = R.g[kind]
+        spot = g.at[0, 0] if l == 1 else R.landing[kind]
+        flight[i] = [start(remote(g.at[l, 1 - c], spot, gs.at[i, 0], gr.at[i, 0], me.cn))]
+
+    def rs_1(i):
+        kind, l = chunks[i]
+        g = R.g[kind]
+        g[l, c] = g[l, c] + (g[0, 0] if l == 1 else R.landing[kind][...])
+        flight[i] = [
+            start(remote(g.at[l, c, first, 1 - y], R.half_y[kind].at[l], gs.at[i, 1], gr.at[i, 1], me.yn)),
+            start(remote(g.at[l, c, second, :, 1 - r], R.half_x[kind].at[l], gs.at[i, 2], gr.at[i, 2], me.xn)),
+        ]
+
+    def rs_2(i):
+        kind, l = chunks[i]
+        g = R.g[kind]
+        g[l, c, first, y] = g[l, c, first, y] + R.half_y[kind][l]
+        g[l, c, second, :, r] = g[l, c, second, :, r] + R.half_x[kind][l]
+        flight[i] = [
+            start(remote(g.at[l, c, first, y, 1 - r], R.quarter_x[kind].at[l], gs.at[i, 3], gr.at[i, 3], me.xn)),
+            start(remote(g.at[l, c, second, 1 - y, r], R.quarter_y[kind].at[l], gs.at[i, 4], gr.at[i, 4], me.yn)),
+        ]
+
+    def rs_3(i):
+        kind, l = chunks[i]
+        g = R.g[kind]
+        g[l, c, first, y, r] = g[l, c, first, y, r] + R.quarter_x[kind][l]
+        g[l, c, second, y, r] = g[l, c, second, y, r] + R.quarter_y[kind][l]
+        flight[i] = []
+        for s in range(1, levels):
+            there, dev = me.zn(s, levels)
+            flight[i].append(
+                start(remote(g.at[l, c, there, y, r], R.level[kind].at[l, s - 1], gs.at[i, 4 + s], gr.at[i, 4 + s], dev))
+            )
+
+    def rs_4(i):
+        kind, l = chunks[i]
+        g, fin = R.g[kind], R.total[kind]
+        total = g[l, c, z, y, r].astype(F32)
+        for s in range(levels - 1):
+            total = total + R.level[kind][l, s].astype(F32)
+        fin[l, r] = total.astype(BF)
+        flight[i] = [start(remote(fin.at[l, r], fin.at[l, r], gs.at[i, 4 + levels], gr.at[i, 4 + levels], me.xn))]
+
+    def rs_5(i):
+        kind, l = chunks[i]
+        cp = pltpu.make_async_copy(R.total[kind].at[l], R.fin[kind].at[l], R.fsem.at[i])
+        cp.start()
+        fin_copies.append(cp)
+
+    steps = (rs_core, rs_1, rs_2, rs_3, rs_4, rs_5)
+
+    def advance(i):
+        at = stage.get(i, 0)
+        for cp in flight.pop(i, ()):
+            cp.wait_recv()
+        steps[at](i)
+        stage[i] = at + 1
+
+    started = []
+
+    def push():
+        for i in started:
+            if stage[i] < len(steps):
+                advance(i)
+
+    def begin(kind, l):
+        i = index[(kind, l)]
+        advance(i)
+        started.append(i)
+
+    for cp in small:
+        cp.wait()
+    vec, msel = R.vec, R.msel
+    tag_row = msel[2 * S : 2 * S + 16].astype(F32)[:1]
+    tag_row = jnp.concatenate([tag_row] * (D // 128), axis=1)
+    low, high, spots = lane_masks()
+    low32 = low.astype(F32)
+    vg = R.vg
+    vg[...] = jnp.zeros_like(vg)
+    R.dy[...] = R.cotb[...].astype(F32)
+    T = 128
+    dy, dpre, dF, dFT, dU, dZ = R.dy, R.dpre, R.dF, R.dFT, R.dU, R.dZ
+
+    def fold(value):
+        return jnp.sum(value.reshape(value.shape[0] // 8, 8, value.shape[1]), axis=0)
+
+    zero8 = jnp.zeros((8, D), F32)
+
+    for l in (1, 0):
+        base = 16 * l
+        e = lambda row: vec[base + row : base + row + 1, :]
+
+        def put(row, value):
+            vg[base + row : base + row + 1, :] = value
+
+        def weight(kind):
+            w = R.w[kind]
+            return w[...].reshape(-1, w.shape[-1])
+
+        N2, r2 = use(R.N2), use(R.r2)
+
+        def norm_two(t, carry):
+            s7, s8, s9 = carry
+            rows = pl.ds(pl.multiple_of(t * T, T), T)
+            g, n = dy[rows], N2[rows]
+            dn = g * e(8)
+            m1 = jnp.mean(dn, axis=-1, keepdims=True)
+            m2 = jnp.mean(dn * n, axis=-1, keepdims=True)
+            d = r2[rows][:, :1] * (dn - m1 - n * m2)
+            dpre[rows] = d
+            db = d.astype(BF)
+            dF[rows] = db
+            dFT[:, rows] = db.T
+            return s7 + fold(db.astype(F32)), s8 + fold(g * n), s9 + fold(g)
+
+        s7, s8, s9 = lax.fori_loop(0, S // T, norm_two, (zero8, zero8, zero8))
+        put(7, jnp.sum(s7, axis=0, keepdims=True))
+        put(8, jnp.sum(s8, axis=0, keepdims=True))
+        put(9, jnp.sum(s9, axis=0, keepdims=True))
+        push()
+        G = use(R.G)
+        gf = R.g[KIND_F]
+        piece = 2 * FF // shards
+
+        def grad_f(t, carry):
+            d = nn_dot(dFT[...], G[:, pl.ds(pl.multiple_of(t * piece, piece), piece)]).astype(BF)
+            zz, yy = lax.div(t, 2), lax.rem(t, 2)
+            half = piece // 2
+            gf[l, 0, zz, yy] = d[:, :half].reshape(2, D // 2, half)
+            gf[l, 1, zz, yy] = d[:, half:].reshape(2, D // 2, half)
+            return carry
+
+        lax.fori_loop(0, shards // 2, grad_f, 0)
+        begin(KIND_F, l)
+        if l == 1:
+            for ref in (R.N2, R.r2, R.G):
+                load(ref, 0)
+        use(R.w[KIND_F])
+        Gp = use(R.Gp)
+        zero_in = tuple(zero8 for _ in range(FF // D))
+
+        def grad_inner(t, carry):
+            rows = pl.ds(pl.multiple_of(t * T, T), T)
+            sums = []
+            wf = R.w[KIND_F]
+            for b in range(FF // D):
+                quarter = wf[b * (levels // (FF // D)) : (b + 1) * (levels // (FF // D))].reshape(D, D)
+                da = nt_dot(dF[rows], quarter)
+                du = (da * Gp[rows, b * D : b * D + D].astype(F32)).astype(BF)
+                dU[rows, b * D : b * D + D] = du
+                sums.append(carry[b] + fold(du.astype(F32)))
+            return tuple(sums)
+
+        sums = lax.fori_loop(0, S // T, grad_inner, zero_in)
+        for b in range(FF // D):
+            put(10 + b, jnp.sum(sums[b], axis=0, keepdims=True))
+        push()
+        if l == 1:
+            load(R.w[KIND_F], 0)
+            load(R.Gp, 0)
+        HT = use(R.HT)
+        gi = R.g[KIND_I]
+        rows_i = 2 * R.g[KIND_I].shape[-2]
+
+        def grad_in(t, carry):
+            rows = pl.ds(pl.multiple_of(t * T, T), T)
+            cc, zz = lax.div(t, D // 2 // T), lax.rem(t, D // 2 // T)
+            span = levels * T // (D // 2)
+            for b in range(FF // D):
+                d = nn_dot(HT[rows], dU[:, b * D : b * D + D]).astype(BF)
+                gi[l, cc, pl.ds(zz * span, span), :, :, :, b * D : b * D + D] = d.reshape(span, 2, 2, rows_i // 2, D)
+            return carry
+
+        lax.fori_loop(0, D // T, grad_in, 0)
+        begin(KIND_I, l)
+        if l == 1:
+            load(R.HT, 0)
+        use(R.w[KIND_I])
+        N1, r1 = use(R.N1), use(R.r1)
+
+        def norm_one(t, carry):
+            s4, s5, s6 = carry
+            rows = pl.ds(pl.multiple_of(t * T, T), T)
+            g = dpre[rows] + nt_dot(dU[rows], weight(KIND_I))
+            n = N1[rows]
+            dn = g * e(5)
+            m1 = jnp.mean(dn, axis=-1, keepdims=True)
+            m2 = jnp.mean(dn * n, axis=-1, keepdims=True)
+            d = r1[rows][:, :1] * (dn - m1 - n * m2)
+            dy[rows] = d
+            db = d.astype(BF)
+            dZ[rows] = db
+            return s4 + fold(db.astype(F32)), s5 + fold(g * n), s6 + fold(g)
+
+        s4, s5, s6 = lax.fori_loop(0, S // T, norm_one, (zero8, zero8, zero8))
+        put(4, jnp.sum(s4, axis=0, keepdims=True))
+        put(5, jnp.sum(s5, axis=0, keepdims=True))
+        put(6, jnp.sum(s6, axis=0, keepdims=True))
+        push()
+        if l == 1:
+            for ref in (R.w[KIND_I], R.N1, R.r1):
+                load(ref, 0)
+        CTp = use(R.CTp)
+        go = R.g[KIND_O]
+
+        def store(ref, value):
+            for cc in range(2):
+                ref[l, cc] = value[cc * (D // 2) : (cc + 1) * (D // 2)].reshape(ref.shape[2:])
+
+        store(R.g[KIND_O], nn_dot(CTp[...], dZ[...]).astype(BF))
+        begin(KIND_O, l)
+        use(R.w[KIND_O])
+        dF[...] = nt_dot(dZ[...], weight(KIND_O)).astype(BF)
+        CT = use(R.CT)
+        dct = dF[...].T
+        prod = dct.astype(F32) * CT[...].astype(F32)
+        prod = jnp.sum(prod.reshape(D // 64, 64, S), axis=1)
+        for j in range(D // 128):
+            R.delta[j, :2] = prod[2 * j : 2 * j + 2]
+        if l == 1:
+            for ref in (R.CTp, R.w[KIND_O], R.CT):
+                load(ref, 0)
+        K, V, Q, lse = use(R.K), use(R.V), use(R.Q), use(R.lse)
+        delta, dC, dQT = R.delta, dF, R.dQT
+        dkp, dvp, dkr, dvr = R.dkp, R.dvp, R.dkr, R.dvr
+        bias_rows = msel[: 2 * S]
+
+        def pair(j, carry):
+            sl = pl.ds(pl.multiple_of(j * 128, 128), 128)
+            k2 = K[:, :, sl].reshape(2 * S, 128)
+            v2 = V[:, :, sl].reshape(2 * S, 128)
+            k2t = k2.T
+            q2 = Q[:, sl]
+            dc2 = dC[:, sl]
+            dk_sum, dv_sum = None, None
+            for h in range(2):
+                mine, other = (low, high) if h == 0 else (high, low)
+                mine32 = low32 if h == 0 else 1.0 - low32
+                kh = k2 * mine + bias_rows * other
+                vh = v2 * mine
+                qh = q2 * mine + spots * other
+                dk_h, dv_h = None, None
+                for part in range(S // 256):
+                    cols = slice(part * 256, part * 256 + 256)
+                    st = nt_dot(kh, qh[cols])
+                    p = jnp.exp(st - lse[j, h : h + 1, cols])
+                    dp = nt_dot(vh, dc2[cols])
+                    ds = (p * (dp - delta[j, h : h + 1, cols])).astype(BF)
+                    pb = p.astype(BF)
+                    dv = nn_dot(pb, dc2[cols])
+                    dk = nn_dot(ds, q2[cols])
+                    dv_h = dv if dv_h is None else dv_h + dv
+                    dk_h = dk if dk_h is None else dk_h + dk
+                    dq = nn_dot(k2t, ds)[64 * h : 64 * h + 64]
+                    rows = pl.ds(pl.multiple_of(j * 128 + 64 * h, 64), 64)
+                    dQT[rows, cols] = (dq * 0.125).astype(BF)
+                dk_sum = dk_h * mine32 if dk_sum is None else dk_sum + dk_h * mine32
+                dv_sum = dv_h * mine32 if dv_sum is None else dv_sum + dv_h * mine32
+            dkp[l, :, j] = dk_sum.astype(BF).reshape(2, S, 128)
+            dvp[l, :, j] = dv_sum.astype(BF).reshape(2, S, 128)
+            return carry
+
+        pairs = D // 128
+        half_pairs = pairs // 2
+        kv_cps = []
+        for part in range(2):
+            lax.fori_loop(part * half_pairs, (part + 1) * half_pairs, pair, 0)
+            js = pl.ds(part * half_pairs, half_pairs)
+            kv_cps.append(start(remote(dkp.at[l, 1 - c, js], dkr.at[l, js], R.ks.at[l, part, 0], R.kr.at[l, part, 0], me.cn)))
+            kv_cps.append(start(remote(dvp.at[l, 1 - c, js], dvr.at[l, js], R.ks.at[l, part, 1], R.kr.at[l, part, 1], me.cn)))
+            push()
+        if l == 1:
+            for ref in (R.K, R.V, R.Q, R.lse):
+                load(ref, 0)
+        AT = use(R.AT)
+        dqb = dZ
+        dqb[...] = dQT[...].T
+        store(R.g[KIND_Q], nn_dot(AT[...], dqb[...]).astype(BF))
+        begin(KIND_Q, l)
+        for cp in kv_cps:
+            cp.wait_recv()
+        dkb, dvb = dFT, R.dvb
+        for j in range(pairs):
+            dkb[:, 128 * j : 128 * j + 128] = dkp[l, c, j] + dkr[l, j]
+            dvb[:, 128 * j : 128 * j + 128] = dvp[l, c, j] + dvr[l, j]
+        store(R.g[KIND_K], nn_dot(AT[...], dkb[...]).astype(BF))
+        begin(KIND_K, l)
+        store(R.g[KIND_V], nn_dot(AT[...], dvb[...]).astype(BF))
+        begin(KIND_V, l)
+        if l == 1:
+            load(R.AT, 0)
+        use(R.w[KIND_Q])
+        use(R.w[KIND_K])
+        use(R.w[KIND_V])
+
+        def last(t, carry):
+            s0, s2, s3 = carry
+            rows = pl.ds(pl.multiple_of(t * T, T), T)
+            d = dy[rows] + nt_dot(dqb[rows], weight(KIND_Q)) + nt_dot(dkb[rows], weight(KIND_K)) + nt_dot(dvb[rows], weight(KIND_V))
+            dy[rows] = d
+            return s0 + fold(d), s2 + fold(dqb[rows].astype(F32)), s3 + fold(dvb[rows].astype(F32))
+
+        s0, s2, s3 = lax.fori_loop(0, S // T, last, (zero8, zero8, zero8))
+        s0 = jnp.sum(s0, axis=0, keepdims=True)
+        put(0, s0 * (1.0 - tag_row))
+        put(1, s0 * tag_row)
+        put(2, jnp.sum(s2, axis=0, keepdims=True))
+        put(3, jnp.sum(s3, axis=0, keepdims=True))
+        push()
+        if l == 1:
+            for ref in (R.w[KIND_Q], R.w[KIND_K], R.w[KIND_V]):
+                load(ref, 0)
+
+    R.cotb[...] = dy[...].astype(BF)
+    dx_far = remote(R.cotb, R.dxo, R.xs.at[1], R.xr.at[1], me.dn)
+    dx_near = pltpu.make_async_copy(R.cotb, R.dxo, R.ssem.at[4])
+
+    @pl.when(stays)
+    def _():
+        dx_near.start()
+
+    @pl.when(jnp.logical_not(stays))
+    def _():
+        dx_far.start()
+
+    vb, vt = R.vb, R.vt
+    va, vrecv = R.va, R.vrecv
+    va[0] = vg[...]
+    for at, dev in enumerate((me.cn, me.xn, me.yn)):
+        cp = start(remote(va.at[at], vrecv.at[at], R.vs.at[at], R.vr.at[at], dev))
+        push()
+        cp.wait_recv()
+        va[at + 1] = va[at] + vrecv[at]
+    vz = []
+    for s in range(1, levels):
+        there, dev = me.zn(s, levels)
+        lanes = pl.ds(pl.multiple_of(there * 128, 128), 128)
+        vz.append(start(remote(va.at[3, :, lanes], vb.at[s - 1], R.vs.at[2 + s], R.vr.at[2 + s], dev)))
+    push()
+    for cp in vz:
+        cp.wait_recv()
+    total = va[3, :, pl.ds(pl.multiple_of(z * 128, 128), 128)]
+    for s in range(levels - 1):
+        total = total + vb[s]
+    vt[...] = total
+    vec_out = pltpu.make_async_copy(vt, R.vec_g, R.ssem.at[5])
+    vec_out.start()
+    while any(stage[i] < len(steps) for i in started):
+        push()
+    for cp in fin_copies:
+        cp.wait()
+    vec_out.wait()
+    for cp in pending:
+        cp.wait_send()
+
+    @pl.when(stays)
+    def _():
+        y_near.wait()
+        dx_near.wait()
+
+    @pl.when(jnp.logical_not(stays))
+    def _():
+        y_far.wait()
+        dx_far.wait()
+
+
+def update_kernel(parts, rates, decays, *refs):
+    R = named(parts, refs)
+    f = lax.axis_index("fsdp")
+
+    def step(at, where, grad):
+        new = adamw(R.masters[at][where], R.firsts[at][where], R.seconds[at][where], grad, rates[at], decays[at])
+        for refs, value in zip((R.new_masters, R.new_firsts, R.new_seconds), new):
+            refs[at][where] = value
+
+    D = R.dx.shape[1]
+    for l in range(2):
+        for at, kind in enumerate((KIND_Q, KIND_K, KIND_V)):
+            grad = R.fin[kind][l].astype(F32).reshape(-1, D)
+            step(0, (l, slice(None), slice(at * D, at * D + D)), grad)
+        for at, kind in ((1, KIND_O), (2, KIND_I)):
+            ref = R.fin[kind]
+            step(at, (l,), ref[l].astype(F32).reshape(-1, ref.shape[-1]))
+        ref = R.fin[KIND_F]
+        step(3, (l,), ref[l].astype(F32).reshape(-1, ref.shape[-1]).T)
+        wide = R.masters[4].shape[2]
+        span = 128 // wide
+        rows = R.masters[4].shape[1]
+        block = R.fvec[16 * l : 16 * l + 16]
+        grad = block[:, :wide]
+        slot = lax.rem(f, span)
+        for s in range(1, span):
+            grad = jnp.where(slot == s, block[:, s * wide : s * wide + wide], grad)
+        step(4, (l,), grad[:rows])
+    R.out[0] = R.y[...]
+    R.grad[0] = R.dx[...].astype(F32)
+
+
+def fast_body(
+    tokens, cotangent, tags, lengths, key_mask,
+    master_qkv, master_out, master_in, master_feed_output, master_vec,
+    first_qkv, first_out, first_in, first_ffo, first_vec,
+    second_qkv, second_out, second_in, second_ffo, second_moment_vector,
+    shards,
+):
+    S, D = tokens.shape[1:]
+    FF = master_in.shape[2]
+    levels = shards // 4
+    rows, cols = sizes_of(shards, D, FF)
+    f = lax.axis_index("fsdp")
+    key_count = key_mask.shape[1]
+    key_pos = jnp.arange(key_count, dtype=jnp.int32)
+    valid = key_pos < lengths[0]
+    key_valid = valid & ((key_mask[0] == 1) | (key_pos == 0))
+    lane = jnp.arange(128, dtype=jnp.int32)
+    bias = jnp.where(key_valid, 0.0, masked_score).astype(F32)
+    meta = jnp.where((lane % 64 == 0)[None, :], bias[:, None], 0.0)
+    tag_rows = jnp.full((16, 128), tags[0], F32)
+    meta = jnp.concatenate([meta, tag_rows], axis=0).astype(BF)
+    start_row = lax.axis_index("rep") * S
+    query_valid = (start_row + jnp.arange(S, dtype=jnp.int32)) < lengths[0]
+    cot = jnp.where(query_valid[None, :, None], cotangent, jnp.zeros_like(cotangent))
+    wide = master_vec.shape[2]
+    vec_rows = jnp.pad(master_vec, ((0, 0), (0, 16 - master_vec.shape[1]), (0, 0))).reshape(32, wide)
+    slot = (lane // wide) == lax.rem(f, 128 // wide)
+    vecb = jnp.where(slot[None, :], jnp.tile(vec_rows, (1, 128 // wide)), 0.0).astype(BF)
+
+    hbm = pl.BlockSpec(memory_space=pl.ANY)
+    shape = jax.ShapeDtypeStruct
+    V = pltpu.VMEM
+    dma = pltpu.SemaphoreType.DMA
+    w_tail = [(levels, 2, 2, 2, rows[k], cols[k]) for k in KINDS]
+    masters = (master_qkv, master_out, master_in, master_feed_output, master_vec)
+    firsts = (first_qkv, first_out, first_in, first_ffo, first_vec)
+    seconds = (second_qkv, second_out, second_in, second_ffo, second_moment_vector)
+
+    saved = call_kernel(
+        lambda parts, *refs: forward_kernel(parts, levels, norm_epsilon, *refs),
+        ForwardIn(tok=tokens, cot=cot, meta=meta, vecb=vecb, masters=masters[:4]),
+        Saved(
+            w_o=tuple(shape((2,) + tail, BF) for tail in w_tail),
+            vec_o=shape((32, D), F32),
+            meta_o=shape(meta.shape, BF),
+            cot_o=shape((S, D), BF),
+            y_o=shape((S, D), BF),
+            at_o=shape((2, D, S), BF),
+            q_o=shape((2, S, D), BF),
+            k_o=shape((2, 2, S, D), BF),
+            v_o=shape((2, 2, S, D), BF),
+            lse_o=shape((2, D // 128, 8, S), F32),
+            ct_o=shape((2, D, S), BF),
+            ctp_o=shape((2, D, S), BF),
+            n1_o=shape((2, S, D), F32),
+            r1_o=shape((2, S, 128), F32),
+            ht_o=shape((2, D, S), BF),
+            g_o=shape((2, S, FF), BF),
+            gp_o=shape((2, S, FF), BF),
+            n2_o=shape((2, S, D), F32),
+            r2_o=shape((2, S, 128), F32),
+        ),
+        ForwardScratch(
+            w=tuple(V((2,) + tail, BF) for tail in w_tail),
+            stages=tuple(V((2, m.shape[1] // 2, m.shape[2]), F32) for m in masters[:4]),
+            vecg=V((shards, 32, 128), BF),
+            vec=V((32, D), F32),
+            metab=V((2,) + meta.shape, BF),
+            msel=V(meta.shape, BF),
+            tokb=V((S, D), BF),
+            A32=V((S, D), F32),
+            Ab=V((S, D), BF),
+            ATp=V((D, S), BF),
+            Q=V((S, D), BF),
+            K=V((2, 2, S, D), BF),
+            V=V((2, 2, S, D), BF),
+            lse=V((D // 128, 8, S), F32),
+            CT=V((D, S), BF),
+            CTp=V((D, S), BF),
+            C=V((S, D), BF),
+            N1=V((S, D), F32),
+            r1=V((S, 128), F32),
+            H32=V((S, D), F32),
+            Hb=V((S, D), BF),
+            HTp=V((D, S), BF),
+            G=V((S, FF), BF),
+            Gp=V((S, FF), BF),
+            N2=V((S, D), F32),
+            r2=V((S, 128), F32),
+            X=V((S, D), F32),
+            Yb=V((S, D), BF),
+            msem=dma((2, 4)),
+            xsem=dma((4,)),
+            osem=dma((48,)),
+            gs=dma((12, levels + 4)),
+            gr=dma((12, levels + 4)),
+            vs=dma((shards - 1,)),
+            vr=dma((shards - 1,)),
+            xs=dma((3,)),
+            xr=dma((3,)),
+            ks=dma((2, 2)),
+            kr=dma((2, 2)),
+        ),
+        hbm,
+        collective_id=0,
+        has_side_effects=True,
+        vmem_limit_bytes=VMEM_BYTES,
+    )
+
+    tails = [(rows[k], cols[k]) for k in KINDS]
+    tails[KIND_F] = (D // 2, FF // shards)
+    ha, hb = levels // 2, levels - levels // 2
+    each = lambda *lead: tuple(V(lead + tail, BF) for tail in tails)
+    grads = call_kernel(
+        lambda parts, *refs: backward_kernel(parts, levels, *refs),
+        saved,
+        BackwardOut(
+            fin=tuple(shape((2, 2) + tail, BF) for tail in tails),
+            vec_g=shape((32, 128), F32),
+            yo=shape((S, D), BF),
+            dxo=shape((S, D), BF),
+        ),
+        BackwardScratch(
+            g=each(2, 2, levels, 2, 2),
+            landing=each(levels, 2, 2),
+            half_y=each(2, ha, 2),
+            half_x=each(2, hb, 2),
+            quarter_x=each(2, ha),
+            quarter_y=each(2, hb),
+            level=each(2, levels - 1),
+            total=each(2, 2),
+            w=tuple(V(tail, BF) for tail in w_tail),
+            AT=V((D, S), BF),
+            Q=V((S, D), BF),
+            K=V((2, S, D), BF),
+            V=V((2, S, D), BF),
+            lse=V((D // 128, 8, S), F32),
+            CT=V((D, S), BF),
+            CTp=V((D, S), BF),
+            N1=V((S, D), F32),
+            r1=V((S, 128), F32),
+            HT=V((D, S), BF),
+            G=V((S, FF), BF),
+            Gp=V((S, FF), BF),
+            N2=V((S, D), F32),
+            r2=V((S, 128), F32),
+            vec=V((32, D), F32),
+            msel=V(meta.shape, BF),
+            cotb=V((S, D), BF),
+            dy=V((S, D), F32),
+            dpre=V((S, D), F32),
+            dF=V((S, D), BF),
+            dFT=V((D, S), BF),
+            dU=V((S, FF), BF),
+            dZ=V((S, D), BF),
+            delta=V((D // 128, 8, S), F32),
+            dQT=V((D, S), BF),
+            dvb=V((S, D), BF),
+            dkp=V((2, 2, D // 128, S, 128), BF),
+            dvp=V((2, 2, D // 128, S, 128), BF),
+            dkr=V((2, D // 128, S, 128), BF),
+            dvr=V((2, D // 128, S, 128), BF),
+            vg=V((32, D), F32),
+            va=V((4, 32, D), F32),
+            vrecv=V((3, 32, D), F32),
+            vb=V((levels - 1, 32, 128), F32),
+            vt=V((32, 128), F32),
+            lsem=dma((2, 20)),
+            ssem=dma((6,)),
+            fsem=dma((12,)),
+            gs=dma((12, levels + 5)),
+            gr=dma((12, levels + 5)),
+            xs=dma((2,)),
+            xr=dma((2,)),
+            ks=dma((2, 2, 2)),
+            kr=dma((2, 2, 2)),
+            vs=dma((levels + 2,)),
+            vr=dma((levels + 2,)),
+        ),
+        hbm,
+        collective_id=1,
+        has_side_effects=True,
+        vmem_limit_bytes=VMEM_BYTES,
+    )
+
+    rates = (
+        matrix_rate * D ** (-0.5),
+        matrix_rate * (D // 16) ** (-0.5),
+        matrix_rate * D ** (-0.5),
+        matrix_rate * (FF // 2) ** (-0.5),
+        vector_rate,
+    )
+    decays = (weight_decay, weight_decay, weight_decay, weight_decay, 0.0)
+    like = tuple(shape(p.shape, F32) for p in masters)
+    new = call_kernel(
+        lambda parts, *refs: update_kernel(parts, rates, decays, *refs),
+        UpdateIn(fin=grads.fin, fvec=grads.vec_g, y=grads.yo, dx=grads.dxo, masters=masters, firsts=firsts, seconds=seconds),
+        UpdateOut(
+            out=shape(tokens.shape, BF),
+            grad=shape(tokens.shape, F32),
+            new_masters=like,
+            new_firsts=like,
+            new_seconds=like,
+        ),
+        None,
+        pl.BlockSpec(memory_space=pltpu.VMEM),
+        vmem_limit_bytes=40 << 20,
+    )
+    return (new.out, new.grad, *new.new_masters, *new.new_firsts, *new.new_seconds)
+
+
 def solution(mesh):
     placed = (
         P("fsdp", "rep", None),
@@ -367,8 +1639,18 @@
         P(None, "fsdp", None),
         P(None, None, "fsdp"),
     )
+    shards = mesh.shape["fsdp"]
+
+    def chosen(*args):
+        tokens, master_in = args[0], args[7]
+        width = tokens.shape[2]
+        whole_tiles = width % (32 * shards) == 0 and shards * 32 == width
+        if mesh.shape["rep"] == 2 and shards % 4 == 0 and whole_tiles and master_in.shape[2] == 4 * width:
+            return fast_body(*args, shards)
+        return body(*args)
+
     return jax.shard_map(
-        body,
+        chosen,
         mesh=mesh,
         in_specs=placed,
         out_specs=(

time: 1300 us -> 272 us (0.21)
  waiting for transfers between devices: 814 us -> 0 us
  matrix products: 255 us -> 0 us
  Pallas kernels: 0 us -> 248 us
  blocking collectives: 86.2 us -> 0 us
  other arithmetic: 74 us -> 3.52 us
  local copies, waits for them, and re-layouts: 46.7 us -> 14.3 us
  between operations: 16.8 us -> 2.5 us
    reduce_scatter x12 -> x0, waiting for transfers between devices: 493 us -> none  [the longest x2 148 us: reduce_layer(): lax.psum_scatter(grads[2], 'fsdp', scatter_dimension=0, tiled=True)]
    dot_general x36 -> x0, matrix products: 255 us -> none  [the longest x2 67.6 us: attention_grads(): jnp.einsum('hqk,khd->qhd', grad_scores, key_heads, preferred_element_type...]
    pallas_call x0 -> x3, Pallas kernels: none -> 248 us  [call_kernel(): pl.pallas_call(functools.partial(kernel, empty), out_shape=out_leaves, in...]
    all_gather x10 -> x0, waiting for transfers between devices: 152 us -> none  [the longest x1 37.8 us: body(): lax.all_gather(master_feed_output[1].astype(jnp.bfloat16), 'fsdp', axis=0...]
    unnamed x28 -> x0, waiting for transfers between devices: 116 us -> none
    all_gather x4 -> x0, blocking collectives: 86.2 us -> none  [the longest x1 23.9 us: body(): lax.all_gather(master_vec[0].astype(jnp.bfloat16), 'fsdp', axis=1, tiled=...]
    psum x2 -> x0, waiting for transfers between devices: 52.9 us -> none  [the longest x1 33.2 us: reduce_layer(): lax.psum(shards[0].astype(jnp.bfloat16), 'rep').astype(jnp.float32)]
    slice x2 -> x0, other arithmetic: 30.6 us -> none  [forward_layer(): vectors[8]]
  transfers between devices with their start and end apart: 26 -> 0, of which waited for: 19 -> 0; matrix products, arithmetic and copies ran while one was open for 24% -> 0% of each run, Pallas kernels for 0% -> 0%
where the time goes in v1:
time: 272 us; the launch traced here: 269 us
  Pallas kernels  248 us (91%)
  local copies, waits for them, and re-layouts  14.3 us (5%)
  other arithmetic  3.52 us (1%)
    pallas_call x3, Pallas kernels, call_kernel(): pl.pallas_call(functools.partial(kernel, empty), out_shape=out_leaves, in...  248 us
    unnamed x49, local copies, waits for them, and re-layouts  11.6 us

profile of v1, /device:TPU:0, one launch (start us, length us, event | category | flops | bytes accessed | tf_op | source)
XLA Modules:
  0.0 268.8 jit_solution(17378796799404120276)
XLA Ops:
  0.7 0.7 copy.43.refs_13_
  1.4 0.1 tile.12
  1.5 0.6 select_convert_fusion.1.refs_3_
  2.8 2.0 broadcast_select_fusion.refs_1_
  4.8 0.7 compare_reduce_fusion
  5.5 0.2 select_convert_fusion
  6.4 0.7 concatenate.3.refs_2_
  7.1 131.5 %shard_map.323 = (bf16[2,4,2,2,2,16,512]{6,5,4,3,2,1,0:T(8,128)(2,1)}, bf16[2,4,2,2,2,16,512]{6,5,4,3,2,1,0:T(8,128)(2,1)}, bf16[2,4,2,2,2,16,512]{6,5,4,3,2,1,0...) custom-call(bf16[1,512,512]{2,1,0:T(8,128)(2,1)} %refs_0_.1, ...), custom_call_target="tpu_custom_call" | custom-call | tf_op jit(solution)/shard_map/pallas_call | solution.py:548
  138.6 0.0 copy-start.21
  138.6 0.0 copy-start.22
  138.6 0.0 copy-start
  138.7 0.0 copy-start.1
  138.7 0.0 copy-start.2
  138.7 0.0 copy-start.3
  138.7 0.0 copy-start.4
  138.7 0.0 copy-start.5
  138.7 0.0 copy-start.6
  138.7 0.0 copy-start.9
  138.7 0.0 copy-start.10
  138.8 113.6 %shard_map.324 = (bf16[2,2,16,512]{3,2,1,0:T(8,128)(2,1)}, bf16[2,2,16,512]{3,2,1,0:T(8,128)(2,1)}, bf16[2,2,16,512]{3,2,1,0:T(8,128)(2,1)}, bf16[2,2,16,512]{3,...) custom-call(bf16[2,4,2,2,2,16,512]{6,5,4,3,2,1,0:T(8,128)(2,1)} %get, ...), custom_call_target="tpu_custom_call" | custom-call | tf_op jit(solution)/shard_map/pallas_call | solution.py:548
  252.4 0.0 copy-done.21
  252.4 0.0 copy-done.22
  252.4 0.0 copy-done
  252.4 0.0 copy-done.1
  252.4 0.0 copy-done.2
  252.4 0.0 copy-done.3
  252.4 0.0 copy-done.4
  252.5 0.0 copy-done.5
  252.5 0.0 copy-done.6
  252.5 0.0 copy-done.9
  252.5 0.0 copy-done.10
  252.5 0.0 copy-start.7
  252.5 1.0 copy-done.7
  253.5 0.0 copy-start.8
  253.5 1.0 copy-done.8
  254.6 0.0 copy-start.11
  254.6 1.0 copy-done.11
  255.6 0.0 copy-start.12
  255.6 0.9 copy-done.12
  256.5 0.0 copy-start.13
  256.5 0.9 copy-done.13
  257.5 0.0 copy-start.14
  257.5 0.9 copy-done.14
  258.4 0.0 copy-start.15
  258.4 0.9 copy-done.15
  259.3 0.0 copy-start.16
  259.3 0.8 copy-done.16
  260.1 0.0 copy-start.17
  260.1 0.8 copy-done.17
  261.0 0.0 copy-start.18
  261.0 0.8 copy-done.18
  261.8 0.0 copy-start.19
  261.8 0.8 copy-done.19
  262.7 0.0 copy-start.20
  262.7 0.7 copy-done.20
  263.4 3.3 %shard_map.325 = (bf16[1,512,512]{2,1,0:T(8,128)(2,1)}, f32[1,512,512]{2,1,0:T(8,128)}, f32[2,32,1536]{2,1,0:T(8,128)}, f32[2,32,512]{2,1,0:T(8,128)}, f32[2,32,...) custom-call(bf16[2,2,16,512]{3,2,1,0:T(8,128)(2,1)S(1)} %copy-done.1, ...), custom_call_target="tpu_custom_call" | custom-call | tf_op jit(solution)/shard_map/pallas_call | solution.py:548
  266.7 0.6 copy.47
  267.3 0.6 copy.48
  267.9 0.6 copy.49
  (8 shorter events, 0.1 us)
Async XLA Ops:
  138.6 113.7 %copy-start.21 = (f32[2,14,32]{2,0,1:T(2,128)S(1)}, f32[2,14,32]{2,0,1:T(2,128)}, u32[]{:S(2)}) copy-start(f32[2,14,32]{2,0,1:T(2,128)} %param.34) | copy-start | bytes 10756
  138.6 113.8 %copy-start.22 = (f32[2,14,32]{2,0,1:T(2,128)S(1)}, f32[2,14,32]{2,0,1:T(2,128)}, u32[]{:S(2)}) copy-start(f32[2,14,32]{2,0,1:T(2,128)} %param.39) | copy-start | bytes 10756
  138.6 113.8 %copy-start = (f32[2,32,2048]{2,1,0:T(8,128)S(1)}, f32[2,32,2048]{2,1,0:T(8,128)}, u32[]{:S(2)}) copy-start(f32[2,32,2048]{2,1,0:T(8,128)} %refs_11_.1) | copy-start | bytes 1572868
  138.7 113.8 %copy-start.1 = (f32[2,128,512]{2,1,0:T(8,128)S(1)}, f32[2,128,512]{2,1,0:T(8,128)}, u32[]{:S(2)}) copy-start(f32[2,128,512]{2,1,0:T(8,128)} %refs_12_.1) | copy-start | bytes 1572868
  138.7 113.8 %copy-start.2 = (f32[2,32,1536]{2,1,0:T(8,128)S(1)}, f32[2,32,1536]{2,1,0:T(8,128)}, u32[]{:S(2)}) copy-start(f32[2,32,1536]{2,1,0:T(8,128)} %refs_9_.1) | copy-start | bytes 1179652
  138.7 113.8 %copy-start.3 = (f32[2,32,2048]{2,1,0:T(8,128)S(1)}, f32[2,32,2048]{2,1,0:T(8,128)}, u32[]{:S(2)}) copy-start(f32[2,32,2048]{2,1,0:T(8,128)} %refs_16_.1) | copy-start | bytes 1572868
  138.7 113.8 %copy-start.4 = (f32[2,128,512]{2,1,0:T(8,128)S(1)}, f32[2,128,512]{2,1,0:T(8,128)}, u32[]{:S(2)}) copy-start(f32[2,128,512]{2,1,0:T(8,128)} %refs_17_.1) | copy-start | bytes 1572868
  138.7 113.8 %copy-start.5 = (f32[2,32,2048]{2,1,0:T(8,128)S(1)}, f32[2,32,2048]{2,1,0:T(8,128)}, u32[]{:S(2)}) copy-start(f32[2,32,2048]{2,1,0:T(8,128)} %refs_21_.1) | copy-start | bytes 1572868
  138.7 113.8 %copy-start.6 = (f32[2,128,512]{2,1,0:T(8,128)S(1)}, f32[2,128,512]{2,1,0:T(8,128)}, u32[]{:S(2)}) copy-start(f32[2,128,512]{2,1,0:T(8,128)} %refs_22_.1) | copy-start | bytes 1572868
  138.7 113.7 %copy-start.9 = (f32[2,32,512]{2,1,0:T(8,128)S(1)}, f32[2,32,512]{2,1,0:T(8,128)}, u32[]{:S(2)}) copy-start(f32[2,32,512]{2,1,0:T(8,128)} %refs_10_.1) | copy-start | bytes 393220
  138.7 113.7 %copy-start.10 = (f32[2,32,1536]{2,1,0:T(8,128)S(1)}, f32[2,32,1536]{2,1,0:T(8,128)}, u32[]{:S(2)}) copy-start(f32[2,32,1536]{2,1,0:T(8,128)} %refs_14_.1) | copy-start | bytes 1179652
  252.5 1.0 copy-start.7
  253.5 1.0 copy-start.8
  254.6 1.0 copy-start.11
  255.6 0.9 copy-start.12
  256.5 0.9 copy-start.13
  257.5 0.9 copy-start.14
  258.4 0.9 copy-start.15
  259.3 0.8 copy-start.16
  260.1 0.8 copy-start.17
  261.0 0.8 copy-start.18
  261.8 0.8 copy-start.19
  262.7 0.7 copy-start.20

commit v2 on v1

--- a/solution.py
+++ b/solution.py
@@ -355,6 +355,72 @@
 MESH = pl.DeviceIdType.MESH
 KIND_K, KIND_V, KIND_Q, KIND_O, KIND_I, KIND_F = KINDS = tuple(range(6))
 VMEM_BYTES = 60 << 20
+FORWARD_TURNS = (
+    (1, 2, 0, 3, 1, 4, 2),
+    (0, 3, 5, 1, 2, 4, 6, 0, 3, 5, 0, 1, 7),
+    (2, 1),
+    (6, 4, 8, 2),
+    (),
+    (3, 9),
+    (5, 7, 10, 3, 8, 6),
+    (9, 11),
+    (4, 10, 12),
+    (),
+    (5, 11),
+    (4, 13),
+    (5, 7, 8, 12),
+    (14, 6, 9, 10, 13, 11, 6, 15, 14, 7, 8, 12, 7, 15),
+    (8, 9),
+    (10,),
+    (13, 9),
+    (10,),
+    (),
+    (11,),
+    (14,),
+    (11,),
+    (12,),
+    (15,),
+    (),
+    (12, 13),
+    (13, 14),
+    (14, 15, 15),
+    (),
+)
+BACKWARD_TURNS = (
+    (),
+    (),
+    (0,),
+    (),
+    (),
+    (1,),
+    (),
+    (0,),
+    (2,),
+    (1, 2),
+    (),
+    (0,),
+    (),
+    (3, 1),
+    (4, 5),
+    (2,),
+    (3, 12),
+    (4, 5, 0, 12),
+    (1, 6),
+    (2,),
+    (),
+    (3, 7),
+    (4,),
+    (5, 0, 6, 12, 3),
+    (4, 7, 8, 5),
+    (0, 1, 8),
+    (2, 3, 12),
+    (4, 5, 6, 12),
+    (7,),
+    (9,),
+    (1, 10, 11),
+    (),
+    (8, 2, 9, 3, 13, 4, 10, 5, 11, 13, 6, 7, 6, 8, 9, 10, 11, 7, 13, 8, 6, 9, 10, 13, 11, 7, 8, 9, 10, 13, 9, 11, 10, 11),
+)
 
 
 def nt_dot(left, right):
@@ -414,6 +480,7 @@
     metab: object
     msel: object
     tokb: object
+    cotb: object
     A32: object
     Ab: object
     ATp: object
@@ -531,6 +598,13 @@
     new_seconds: object
 
 
+class UpdateScratch(NamedTuple):
+    inside: object
+    wide: object
+    isem: object
+    osem: object
+
+
 def named(parts, refs):
     fields, at = {}, 0
     for part in parts:
@@ -579,6 +653,16 @@
     return blocks[:, 0].reshape(half, rows.shape[1]), blocks[:, 1].reshape(half, rows.shape[1])
 
 
+def go_or_stay(stays, stay, go):
+    @pl.when(stays)
+    def _():
+        stay()
+
+    @pl.when(jnp.logical_not(stays))
+    def _():
+        go()
+
+
 def lane_masks():
     lane = lax.broadcasted_iota(jnp.int32, (16, 128), 1)
     low = (lane < 64).astype(F32)
@@ -624,7 +708,12 @@
         pl.semaphore_signal(barrier, inc=1, device_id=peer, device_id_type=MESH)
     pl.semaphore_wait(barrier, len(peers))
 
-    chunks = [(kind, l) for l in range(2) for kind in KINDS]
+    chunks = []
+    for l in range(2):
+        for kind in KINDS:
+            parts = 2 if kind in (KIND_I, KIND_F) else 1
+            span = R.w[kind].shape[-1] // parts
+            chunks += [(kind, l, slice(part * span, part * span + span)) for part in range(parts)]
     gs, gr = R.gs, R.gr
     pending = []
 
@@ -633,68 +722,85 @@
         pending.append(cp)
         return cp
 
+    out_copies = {}
+    out_at = [0]
+
+    def out(ref, dst, view=None):
+        cp = pltpu.make_async_copy(ref if view is None else view, dst, R.osem.at[out_at[0]])
+        out_at[0] += 1
+        cp.start()
+        out_copies[(id(ref), view is not None and out_at[0])] = cp
+
+    def settle(ref):
+        if (id(ref), False) in out_copies:
+            out_copies.pop((id(ref), False)).wait()
+
     loaded = set()
     stage_copies = {}
 
     def g_z(i):
-        kind, l = chunks[i]
+        kind, l, cols = chunks[i]
         w = R.w[kind]
         at, offset = source[kind]
         if (l, at) not in loaded:
             half_loads[(l, at)].wait()
             loaded.add((l, at))
-        w[l, z, y, c, r] = R.stages[at][l][:, offset : offset + w.shape[-1]].astype(BF)
+        w[l, z, y, c, r, :, cols] = R.stages[at][l][:, offset + cols.start : offset + cols.stop].astype(BF)
         cps = []
         for s in range(1, levels):
             _, dev = me.zn(s, levels)
-            spot = w.at[l, z, y, c, r]
+            spot = w.at[l, z, y, c, r, :, cols]
             cps.append(start(remote(spot, spot, gs.at[i, s - 1], gr.at[i, s - 1], dev)))
         stage_copies[i] = cps
 
     def g_1(i):
-        kind, l = chunks[i]
+        kind, l, cols = chunks[i]
         w = R.w[kind]
         for cp in stage_copies[i]:
             cp.wait_recv()
-        a, b = w.at[l, first, y, c, r], w.at[l, second, y, c, r]
+        a, b = w.at[l, first, y, c, r, :, cols], w.at[l, second, y, c, r, :, cols]
         stage_copies[i] = [
             start(remote(a, a, gs.at[i, levels - 1], gr.at[i, levels - 1], me.xn)),
             start(remote(b, b, gs.at[i, levels], gr.at[i, levels], me.yn)),
         ]
 
     def g_2(i):
-        kind, l = chunks[i]
+        kind, l, cols = chunks[i]
         w = R.w[kind]
         for cp in stage_copies[i]:
             cp.wait_recv()
-        a, b = w.at[l, first, y, c], w.at[l, second, :, c, r]
+        a, b = w.at[l, first, y, c, :, :, cols], w.at[l, second, :, c, r, :, cols]
         stage_copies[i] = [
             start(remote(a, a, gs.at[i, levels + 1], gr.at[i, levels + 1], me.yn)),
             start(remote(b, b, gs.at[i, levels + 2], gr.at[i, levels + 2], me.xn)),
         ]
 
     def g_core(i):
-        kind, l = chunks[i]
+        kind, l, cols = chunks[i]
         w = R.w[kind]
         for cp in stage_copies[i]:
             cp.wait_recv()
-        a = w.at[l, :, :, c]
+        a = w.at[l, :, :, c, :, :, cols]
         stage_copies[i] = [start(remote(a, a, gs.at[i, levels + 3], gr.at[i, levels + 3], me.cn))]
 
     def g_ready(i):
+        kind, l, cols = chunks[i]
         for cp in stage_copies.pop(i):
             cp.wait_recv()
-
-    tick_at = [0]
-
-    def tick():
-        t = tick_at[0]
-        tick_at[0] += 1
-        for lag, step in ((4, g_ready), (3, g_core), (2, g_2), (1, g_1), (0, g_z)):
-            if 0 <= t - lag < len(chunks):
-                step(t - lag)
-
-    g_z(0)
+        if cols.stop == R.w[kind].shape[-1]:
+            out(R.w[kind], R.w_o[kind].at[l], R.w[kind].at[l])
+
+    steps = (g_z, g_1, g_2, g_core, g_ready)
+    reached = [0] * len(chunks)
+    turns = iter(FORWARD_TURNS)
+
+    def turn():
+        for i in next(turns):
+            steps[reached[i]](i)
+            reached[i] += 1
+
+    steps[0](0)
+    reached[0] = 1
     meta_cp = start(remote(R.meta, R.metab.at[1], R.xs.at[0], R.xr.at[0], me.cn))
     vec_cps = []
     for s in range(1, shards):
@@ -706,18 +812,9 @@
     tok_near = pltpu.make_async_copy(R.tok.at[0], R.tokb, R.xsem.at[2])
     stays = c == r
 
-    @pl.when(stays)
-    def _():
-        tok_near.start()
-
-    @pl.when(jnp.logical_not(stays))
-    def _():
-        tok_far.start()
-
-    tick_at[0] = 1
-    tick()
-    tick()
-
+    go_or_stay(stays, tok_near.start, tok_far.start)
+
+    turn()
     vec_local.wait()
     meta_local.wait()
     meta_cp.wait_recv()
@@ -733,31 +830,17 @@
     tag_row = jnp.concatenate([tag_row] * (D // 128), axis=1)
     low, high, spots = lane_masks()
 
-    out_copies = {}
-    out_at = [0]
-
-    def out(ref, dst, view=None):
-        cp = pltpu.make_async_copy(ref if view is None else view, dst, R.osem.at[out_at[0]])
-        out_at[0] += 1
-        cp.start()
-        out_copies[(id(ref), view is not None and out_at[0])] = cp
-
-    def settle(ref):
-        if (id(ref), False) in out_copies:
-            out_copies.pop((id(ref), False)).wait()
-
-    @pl.when(stays)
-    def _():
-        tok_near.wait()
-
-    @pl.when(jnp.logical_not(stays))
-    def _():
-        tok_far.wait()
-
-    T = 128
+    go_or_stay(stays, tok_near.wait, tok_far.wait)
+    cot_far = remote(R.cot.at[0], R.cotb, R.xs.at[2], R.xr.at[2], me.dn)
+    cot_near = pltpu.make_async_copy(R.cot.at[0], R.cotb, R.xsem.at[3])
+
+    T = 256
     for l in range(2):
         e = lambda row: vec[16 * l + row : 16 * l + row + 1, :]
         direction = e(0) * (1.0 - tag_row) + e(1) * tag_row
+        if l == 1:
+            turn()
+            go_or_stay(stays, cot_near.start, cot_far.start)
         A32, Ab, Q, K, V, CT = R.A32, R.Ab, R.Q, R.K, R.V, R.CT
         x_in = R.tokb if l == 0 else R.X
         summed = x_in[...].astype(F32) + direction
@@ -776,21 +859,18 @@
             value = w[l, :, :, :, :, :, lo:hi]
             return value.reshape(-1, hi - lo)
 
-        if l == 0:
-            tick()
-            tick()
+        turn()
         K[l, c] = nn_dot(Ab[...], weight(KIND_K)).astype(BF)
         k_cp = start(remote(K.at[l, c], K.at[l, c], R.ks.at[l, 0], R.kr.at[l, 0], me.cn))
-        if l == 0:
-            tick()
+        turn()
         V[l, c] = (nn_dot(Ab[...], weight(KIND_V)) + e(3)).astype(BF)
         v_cp = start(remote(V.at[l, c], V.at[l, c], R.ks.at[l, 1], R.kr.at[l, 1], me.cn))
-        if l == 0:
-            tick()
+        turn()
         settle(R.Q)
         q = (nn_dot(Ab[...], weight(KIND_Q)) + e(2)).astype(BF)
         Q[...] = (q.astype(F32) * 0.125).astype(BF)
         out(R.Q, R.q_o.at[l])
+        turn()
         k_cp.wait_recv()
         v_cp.wait_recv()
         out(K, R.k_o.at[l], K.at[l])
@@ -800,32 +880,27 @@
         settle(R.CT)
         bias_rows = msel[: 2 * S]
 
-        def pair(j, carry):
-            sl = pl.ds(pl.multiple_of(j * 128, 128), 128)
+        def pair(j):
+            sl = slice(j * 128, j * 128 + 128)
             k2 = K[l, :, :, sl].reshape(2 * S, 128)
             v2t = V[l, :, :, sl].reshape(2 * S, 128).T
             q2 = Q[:, sl]
-            for h in range(2):
-                mine, other = (low, high) if h == 0 else (high, low)
-                kh = k2 * mine + bias_rows * other
-                qh = q2 * mine + spots * other
-                for part in range(S // 256):
-                    cols = slice(part * 256, part * 256 + 256)
-                    st = nt_dot(kh, qh[cols])
-                    top = jnp.max(st, axis=0, keepdims=True)
-                    p = jnp.exp(st - top)
-                    total = jnp.sum(p, axis=0, keepdims=True)
-                    ctx = nn_dot(v2t, p.astype(BF))[64 * h : 64 * h + 64]
-                    rows = pl.ds(pl.multiple_of(j * 128 + 64 * h, 64), 64)
-                    CT[rows, cols] = (ctx / total).astype(BF)
-                    lse[j, h : h + 1, cols] = top + jnp.log(total)
-            return carry
-
-        pairs = D // 128
-        lax.fori_loop(0, pairs // 2, pair, 0)
-        if l == 0:
-            tick()
-        lax.fori_loop(pairs // 2, pairs, pair, 0)
+            scores = []
+            for mine, other in ((low, high), (high, low)):
+                scores.append(nt_dot(k2 * mine + bias_rows * other, q2 * mine + spots * other))
+            for h, st in enumerate(scores):
+                top = jnp.max(st, axis=0, keepdims=True)
+                p = jnp.exp(st - top)
+                total = jnp.sum(p, axis=0, keepdims=True)
+                ctx = nn_dot(v2t, p.astype(BF))[64 * h : 64 * h + 64]
+                rows = slice(j * 128 + 64 * h, j * 128 + 64 * h + 64)
+                CT[rows] = (ctx * (1.0 / total)).astype(BF)
+                lse[j, h : h + 1] = top + jnp.log(total)
+
+        for j in range(D // 128):
+            turn()
+            pair(j)
+        turn()
         out(R.lse, R.lse_o.at[l])
         out(R.CT, R.ct_o.at[l])
         even, odd = parity_rows(CT[...], shards)
@@ -851,6 +926,10 @@
             R.Hb[rows] = hidden.astype(BF)
             return carry
 
+        turn()
+        if l == 1:
+            go_or_stay(stays, cot_near.wait, cot_far.wait_recv)
+            out(R.cotb, R.cot_o)
         lax.fori_loop(0, S // T, norm_one, 0)
         out(R.N1, R.n1_o.at[l])
         out(R.r1, R.r1_o.at[l])
@@ -859,29 +938,25 @@
         R.HTp[: D // 2] = even
         R.HTp[D // 2 :] = odd
         out(R.HTp, R.ht_o.at[l])
-        if l == 0:
-            tick()
         settle(R.G)
         settle(R.Gp)
 
-        def inner(t, carry):
-            rows = pl.ds(pl.multiple_of(t * T, T), T)
-            hb = R.Hb[rows]
-            for b in range(FF // D):
-                u = nn_dot(hb, weight(KIND_I, b * D, b * D + D)) + e(10 + b)
-                u2 = u * u
-                th = jnp.tanh(u * (0.7978845608028654 + 0.035677408136300125 * u2))
-                half = 0.5 + 0.5 * th
-                slope = 0.7978845608028654 + 0.10703222440890038 * u2
-                R.G[rows, b * D : b * D + D] = (u * half).astype(BF)
-                R.Gp[rows, b * D : b * D + D] = (half + 0.5 * u * (1.0 - th * th) * slope).astype(BF)
-            return carry
-
-        lax.fori_loop(0, S // T, inner, 0)
+        def inner(b):
+            u = nn_dot(R.Hb[...], weight(KIND_I, b * D, b * D + D)) + e(10 + b)
+            u2 = u * u
+            th = jnp.tanh(u * (0.7978845608028654 + 0.035677408136300125 * u2))
+            half = 0.5 + 0.5 * th
+            slope = 0.7978845608028654 + 0.10703222440890038 * u2
+            R.G[:, b * D : b * D + D] = (u * half).astype(BF)
+            R.Gp[:, b * D : b * D + D] = (half + 0.5 * u * (1.0 - th * th) * slope).astype(BF)
+
+        for b in range(FF // D):
+            if b % 2 == 0:
+                turn()
+            inner(b)
         out(R.G, R.g_o.at[l])
         out(R.Gp, R.gp_o.at[l])
-        if l == 0:
-            tick()
+        turn()
         settle(R.N2)
         settle(R.r2)
 
@@ -900,39 +975,17 @@
         lax.fori_loop(0, S // T, norm_two, 0)
         out(R.N2, R.n2_o.at[l])
         out(R.r2, R.r2_o.at[l])
-        if l == 0:
-            while tick_at[0] < len(chunks) + 4:
-                tick()
-            for kind in KINDS:
-                out(R.w[kind], R.w_o[kind])
-
+
+    turn()
     R.Yb[...] = R.X[...].astype(BF)
     out(R.Yb, R.y_o)
     out(vec, R.vec_o)
     out(msel, R.meta_o)
-    cot_far = remote(R.cot.at[0], R.cot_o, R.xs.at[2], R.xr.at[2], me.dn)
-    cot_near = pltpu.make_async_copy(R.cot.at[0], R.cot_o, R.xsem.at[3])
-
-    @pl.when(stays)
-    def _():
-        cot_near.start()
-
-    @pl.when(jnp.logical_not(stays))
-    def _():
-        cot_far.start()
-
     for cp in out_copies.values():
         cp.wait()
     for cp in pending:
         cp.wait_send()
-
-    @pl.when(stays)
-    def _():
-        cot_near.wait()
-
-    @pl.when(jnp.logical_not(stays))
-    def _():
-        cot_far.wait()
+    go_or_stay(stays, lambda: None, cot_far.wait_send)
 
 
 def backward_kernel(parts, levels, *refs):
@@ -988,18 +1041,13 @@
     stays = c == r
     y_far = remote(R.y_o, R.yo, R.xs.at[0], R.xr.at[0], me.dn)
     y_near = pltpu.make_async_copy(R.y_o, R.yo, R.ssem.at[3])
-
-    @pl.when(stays)
-    def _():
-        y_near.start()
-
-    @pl.when(jnp.logical_not(stays))
-    def _():
-        y_far.start()
+    dx_cps = []
+
+    go_or_stay(stays, y_near.start, y_far.start)
 
     gs, gr = R.gs, R.gr
     chunks = [(kind, l) for l in (1, 0) for kind in (KIND_F, KIND_I, KIND_O, KIND_Q, KIND_K, KIND_V)]
-    index = {chunk: at for at, chunk in enumerate(chunks)}
+    chunks += [(None, 1), (None, 0)]
     flight = {}
     stage = {}
     fin_copies = []
@@ -1056,26 +1104,46 @@
         cp.start()
         fin_copies.append(cp)
 
-    steps = (rs_core, rs_1, rs_2, rs_3, rs_4, rs_5)
-
-    def advance(i):
-        at = stage.get(i, 0)
-        for cp in flight.pop(i, ()):
-            cp.wait_recv()
-        steps[at](i)
-        stage[i] = at + 1
-
-    started = []
-
-    def push():
-        for i in started:
-            if stage[i] < len(steps):
-                advance(i)
-
-    def begin(kind, l):
-        i = index[(kind, l)]
-        advance(i)
-        started.append(i)
+    vg, va, vb, vt = R.vg, R.va, R.vb, R.vt
+
+    def vec_hop(at, device):
+        def step(i):
+            l = chunks[i][1]
+            if at == 0:
+                va[l, 0] = vg[16 * l : 16 * l + 16]
+            else:
+                va[l, at] = va[l, at - 1] + R.vrecv[l, at - 1]
+            flight[i] = [start(remote(va.at[l, at], R.vrecv.at[l, at], R.vs.at[l, at], R.vr.at[l, at], device))]
+
+        return step
+
+    def vec_level(i):
+        l = chunks[i][1]
+        va[l, 3] = va[l, 2] + R.vrecv[l, 2]
+        flight[i] = []
+        for s in range(1, levels):
+            there, dev = me.zn(s, levels)
+            lanes = pl.ds(pl.multiple_of(there * 128, 128), 128)
+            flight[i].append(start(remote(va.at[l, 3, :, lanes], vb.at[l, s - 1], R.vs.at[l, 2 + s], R.vr.at[l, 2 + s], dev)))
+
+    def vec_end(i):
+        l = chunks[i][1]
+        total = va[l, 3, :, pl.ds(pl.multiple_of(z * 128, 128), 128)]
+        for s in range(levels - 1):
+            total = total + vb[l, s]
+        vt[16 * l : 16 * l + 16] = total
+
+    matrix_steps = (rs_core, rs_1, rs_2, rs_3, rs_4, rs_5)
+    vec_steps = (vec_hop(0, me.cn), vec_hop(1, me.xn), vec_hop(2, me.yn), vec_level, vec_end)
+    turns = iter(BACKWARD_TURNS)
+
+    def turn():
+        for i in next(turns):
+            at = stage.get(i, 0)
+            for cp in flight.pop(i, ()):
+                cp.wait_recv()
+            (matrix_steps if chunks[i][0] is not None else vec_steps)[at](i)
+            stage[i] = at + 1
 
     for cp in small:
         cp.wait()
@@ -1084,10 +1152,9 @@
     tag_row = jnp.concatenate([tag_row] * (D // 128), axis=1)
     low, high, spots = lane_masks()
     low32 = low.astype(F32)
-    vg = R.vg
     vg[...] = jnp.zeros_like(vg)
     R.dy[...] = R.cotb[...].astype(F32)
-    T = 128
+    T = 256
     dy, dpre, dF, dFT, dU, dZ = R.dy, R.dpre, R.dF, R.dFT, R.dU, R.dZ
 
     def fold(value):
@@ -1106,6 +1173,7 @@
             w = R.w[kind]
             return w[...].reshape(-1, w.shape[-1])
 
+        turn()
         N2, r2 = use(R.N2), use(R.r2)
 
         def norm_two(t, carry):
@@ -1126,7 +1194,7 @@
         put(7, jnp.sum(s7, axis=0, keepdims=True))
         put(8, jnp.sum(s8, axis=0, keepdims=True))
         put(9, jnp.sum(s9, axis=0, keepdims=True))
-        push()
+        turn()
         G = use(R.G)
         gf = R.g[KIND_F]
         piece = 2 * FF // shards
@@ -1140,30 +1208,25 @@
             return carry
 
         lax.fori_loop(0, shards // 2, grad_f, 0)
-        begin(KIND_F, l)
         if l == 1:
             for ref in (R.N2, R.r2, R.G):
                 load(ref, 0)
         use(R.w[KIND_F])
         Gp = use(R.Gp)
-        zero_in = tuple(zero8 for _ in range(FF // D))
-
-        def grad_inner(t, carry):
-            rows = pl.ds(pl.multiple_of(t * T, T), T)
-            sums = []
+
+        def grad_inner(b):
             wf = R.w[KIND_F]
-            for b in range(FF // D):
-                quarter = wf[b * (levels // (FF // D)) : (b + 1) * (levels // (FF // D))].reshape(D, D)
-                da = nt_dot(dF[rows], quarter)
-                du = (da * Gp[rows, b * D : b * D + D].astype(F32)).astype(BF)
-                dU[rows, b * D : b * D + D] = du
-                sums.append(carry[b] + fold(du.astype(F32)))
-            return tuple(sums)
-
-        sums = lax.fori_loop(0, S // T, grad_inner, zero_in)
+            quarter = wf[b * (levels // (FF // D)) : (b + 1) * (levels // (FF // D))].reshape(D, D)
+            cols = slice(b * D, b * D + D)
+            du = (nt_dot(dF[...], quarter) * Gp[:, cols].astype(F32)).astype(BF)
+            dU[:, cols] = du
+            put(10 + b, jnp.sum(fold(du.astype(F32)), axis=0, keepdims=True))
+
         for b in range(FF // D):
-            put(10 + b, jnp.sum(sums[b], axis=0, keepdims=True))
-        push()
+            if b % 2 == 0:
+                turn()
+            grad_inner(b)
+        turn()
         if l == 1:
             load(R.w[KIND_F], 0)
             load(R.Gp, 0)
@@ -1171,17 +1234,11 @@
         gi = R.g[KIND_I]
         rows_i = 2 * R.g[KIND_I].shape[-2]
 
-        def grad_in(t, carry):
-            rows = pl.ds(pl.multiple_of(t * T, T), T)
-            cc, zz = lax.div(t, D // 2 // T), lax.rem(t, D // 2 // T)
-            span = levels * T // (D // 2)
-            for b in range(FF // D):
-                d = nn_dot(HT[rows], dU[:, b * D : b * D + D]).astype(BF)
-                gi[l, cc, pl.ds(zz * span, span), :, :, :, b * D : b * D + D] = d.reshape(span, 2, 2, rows_i // 2, D)
-            return carry
-
-        lax.fori_loop(0, D // T, grad_in, 0)
-        begin(KIND_I, l)
+        for b in range(FF // D):
+            d = nn_dot(HT[...], dU[:, b * D : b * D + D]).astype(BF)
+            for cc in range(2):
+                part = d[cc * (D // 2) : (cc + 1) * (D // 2)]
+                gi[l, cc, :, :, :, :, b * D : b * D + D] = part.reshape(levels, 2, 2, rows_i // 2, D)
         if l == 1:
             load(R.HT, 0)
         use(R.w[KIND_I])
@@ -1201,11 +1258,14 @@
             dZ[rows] = db
             return s4 + fold(db.astype(F32)), s5 + fold(g * n), s6 + fold(g)
 
-        s4, s5, s6 = lax.fori_loop(0, S // T, norm_one, (zero8, zero8, zero8))
+        turn()
+        sums = lax.fori_loop(0, S // T // 2, norm_one, (zero8, zero8, zero8))
+        turn()
+        s4, s5, s6 = lax.fori_loop(S // T // 2, S // T, norm_one, sums)
         put(4, jnp.sum(s4, axis=0, keepdims=True))
         put(5, jnp.sum(s5, axis=0, keepdims=True))
         put(6, jnp.sum(s6, axis=0, keepdims=True))
-        push()
+        turn()
         if l == 1:
             for ref in (R.w[KIND_I], R.N1, R.r1):
                 load(ref, 0)
@@ -1217,7 +1277,6 @@
                 ref[l, cc] = value[cc * (D // 2) : (cc + 1) * (D // 2)].reshape(ref.shape[2:])
 
         store(R.g[KIND_O], nn_dot(CTp[...], dZ[...]).astype(BF))
-        begin(KIND_O, l)
         use(R.w[KIND_O])
         dF[...] = nt_dot(dZ[...], weight(KIND_O)).astype(BF)
         CT = use(R.CT)
@@ -1234,8 +1293,8 @@
         dkp, dvp, dkr, dvr = R.dkp, R.dvp, R.dkr, R.dvr
         bias_rows = msel[: 2 * S]
 
-        def pair(j, carry):
-            sl = pl.ds(pl.multiple_of(j * 128, 128), 128)
+        def pair(j):
+            sl = slice(j * 128, j * 128 + 128)
             k2 = K[:, :, sl].reshape(2 * S, 128)
             v2 = V[:, :, sl].reshape(2 * S, 128)
             k2t = k2.T
@@ -1261,31 +1320,34 @@
                     dv_h = dv if dv_h is None else dv_h + dv
                     dk_h = dk if dk_h is None else dk_h + dk
                     dq = nn_dot(k2t, ds)[64 * h : 64 * h + 64]
-                    rows = pl.ds(pl.multiple_of(j * 128 + 64 * h, 64), 64)
+                    rows = slice(j * 128 + 64 * h, j * 128 + 64 * h + 64)
                     dQT[rows, cols] = (dq * 0.125).astype(BF)
                 dk_sum = dk_h * mine32 if dk_sum is None else dk_sum + dk_h * mine32
                 dv_sum = dv_h * mine32 if dv_sum is None else dv_sum + dv_h * mine32
             dkp[l, :, j] = dk_sum.astype(BF).reshape(2, S, 128)
             dvp[l, :, j] = dv_sum.astype(BF).reshape(2, S, 128)
-            return carry
 
         pairs = D // 128
         half_pairs = pairs // 2
         kv_cps = []
-        for part in range(2):
-            lax.fori_loop(part * half_pairs, (part + 1) * half_pairs, pair, 0)
-            js = pl.ds(part * half_pairs, half_pairs)
-            kv_cps.append(start(remote(dkp.at[l, 1 - c, js], dkr.at[l, js], R.ks.at[l, part, 0], R.kr.at[l, part, 0], me.cn)))
-            kv_cps.append(start(remote(dvp.at[l, 1 - c, js], dvr.at[l, js], R.ks.at[l, part, 1], R.kr.at[l, part, 1], me.cn)))
-            push()
+        for j in range(pairs):
+            turn()
+            pair(j)
+            if (j + 1) % half_pairs == 0:
+                part = j // half_pairs
+                js = pl.ds(part * half_pairs, half_pairs)
+                for at, (mine, theirs) in enumerate(((dkp, dkr), (dvp, dvr))):
+                    sems = R.ks.at[l, part, at], R.kr.at[l, part, at]
+                    kv_cps.append(start(remote(mine.at[l, 1 - c, js], theirs.at[l, js], *sems, me.cn)))
         if l == 1:
             for ref in (R.K, R.V, R.Q, R.lse):
                 load(ref, 0)
+        turn()
         AT = use(R.AT)
         dqb = dZ
         dqb[...] = dQT[...].T
         store(R.g[KIND_Q], nn_dot(AT[...], dqb[...]).astype(BF))
-        begin(KIND_Q, l)
+        turn()
         for cp in kv_cps:
             cp.wait_recv()
         dkb, dvb = dFT, R.dvb
@@ -1293,9 +1355,7 @@
             dkb[:, 128 * j : 128 * j + 128] = dkp[l, c, j] + dkr[l, j]
             dvb[:, 128 * j : 128 * j + 128] = dvp[l, c, j] + dvr[l, j]
         store(R.g[KIND_K], nn_dot(AT[...], dkb[...]).astype(BF))
-        begin(KIND_K, l)
         store(R.g[KIND_V], nn_dot(AT[...], dvb[...]).astype(BF))
-        begin(KIND_V, l)
         if l == 1:
             load(R.AT, 0)
         use(R.w[KIND_Q])
@@ -1309,100 +1369,106 @@
             dy[rows] = d
             return s0 + fold(d), s2 + fold(dqb[rows].astype(F32)), s3 + fold(dvb[rows].astype(F32))
 
-        s0, s2, s3 = lax.fori_loop(0, S // T, last, (zero8, zero8, zero8))
+        sums = (zero8, zero8, zero8)
+        for part in range(2):
+            turn()
+            sums = lax.fori_loop(part * (S // T // 2), (part + 1) * (S // T // 2), last, sums)
+            if l == 0:
+                half = pl.ds(part * (S // 2), S // 2)
+                R.cotb[half] = dy[half].astype(BF)
+                far = remote(R.cotb.at[half], R.dxo.at[half], R.xs.at[1 + part], R.xr.at[1 + part], me.dn)
+                near = pltpu.make_async_copy(R.cotb.at[half], R.dxo.at[half], R.ssem.at[4 + part])
+                dx_cps.append((far, near))
+                go_or_stay(stays, near.start, far.start)
+        s0, s2, s3 = sums
         s0 = jnp.sum(s0, axis=0, keepdims=True)
         put(0, s0 * (1.0 - tag_row))
         put(1, s0 * tag_row)
         put(2, jnp.sum(s2, axis=0, keepdims=True))
         put(3, jnp.sum(s3, axis=0, keepdims=True))
-        push()
         if l == 1:
             for ref in (R.w[KIND_Q], R.w[KIND_K], R.w[KIND_V]):
                 load(ref, 0)
 
-    R.cotb[...] = dy[...].astype(BF)
-    dx_far = remote(R.cotb, R.dxo, R.xs.at[1], R.xr.at[1], me.dn)
-    dx_near = pltpu.make_async_copy(R.cotb, R.dxo, R.ssem.at[4])
-
-    @pl.when(stays)
-    def _():
-        dx_near.start()
-
-    @pl.when(jnp.logical_not(stays))
-    def _():
-        dx_far.start()
-
-    vb, vt = R.vb, R.vt
-    va, vrecv = R.va, R.vrecv
-    va[0] = vg[...]
-    for at, dev in enumerate((me.cn, me.xn, me.yn)):
-        cp = start(remote(va.at[at], vrecv.at[at], R.vs.at[at], R.vr.at[at], dev))
-        push()
-        cp.wait_recv()
-        va[at + 1] = va[at] + vrecv[at]
-    vz = []
-    for s in range(1, levels):
-        there, dev = me.zn(s, levels)
-        lanes = pl.ds(pl.multiple_of(there * 128, 128), 128)
-        vz.append(start(remote(va.at[3, :, lanes], vb.at[s - 1], R.vs.at[2 + s], R.vr.at[2 + s], dev)))
-    push()
-    for cp in vz:
-        cp.wait_recv()
-    total = va[3, :, pl.ds(pl.multiple_of(z * 128, 128), 128)]
-    for s in range(levels - 1):
-        total = total + vb[s]
-    vt[...] = total
-    vec_out = pltpu.make_async_copy(vt, R.vec_g, R.ssem.at[5])
+    turn()
+    vec_out = pltpu.make_async_copy(vt, R.vec_g, R.ssem.at[6])
     vec_out.start()
-    while any(stage[i] < len(steps) for i in started):
-        push()
     for cp in fin_copies:
         cp.wait()
     vec_out.wait()
     for cp in pending:
         cp.wait_send()
 
-    @pl.when(stays)
-    def _():
-        y_near.wait()
-        dx_near.wait()
-
-    @pl.when(jnp.logical_not(stays))
-    def _():
-        y_far.wait()
-        dx_far.wait()
+    for far, near in dx_cps:
+        go_or_stay(stays, near.wait, far.wait)
+    go_or_stay(stays, y_near.wait, y_far.wait)
 
 
 def update_kernel(parts, rates, decays, *refs):
     R = named(parts, refs)
     f = lax.axis_index("fsdp")
+    sources, _ = jax.tree.flatten((R.fin, R.fvec, R.y, R.dx, R.masters, R.firsts, R.seconds))
+    places, tree = jax.tree.flatten(R.inside)
+    copies = [pltpu.make_async_copy(s, p, R.isem.at[at]) for at, (s, p) in enumerate(zip(sources, places))]
+    for cp in copies:
+        cp.start()
+    fin, fvec, y, dx, masters, firsts, seconds = R.inside
+    waits = tree.unflatten(copies)
+    finals = (R.new_masters, R.new_firsts, R.new_seconds)
+    leaving = []
+
+    def leave(src, dst):
+        cp = pltpu.make_async_copy(src, dst, R.osem.at[len(leaving)])
+        cp.start()
+        leaving.append(cp)
+
+    def arrive(at, kinds):
+        for cp in [waits[0][k] for k in kinds] + [w[at] for w in waits[4:]]:
+            cp.wait()
 
     def step(at, where, grad):
-        new = adamw(R.masters[at][where], R.firsts[at][where], R.seconds[at][where], grad, rates[at], decays[at])
-        for refs, value in zip((R.new_masters, R.new_firsts, R.new_seconds), new):
+        new = adamw(masters[at][where], firsts[at][where], seconds[at][where], grad, rates[at], decays[at])
+        for refs, value in zip((masters, firsts, seconds), new):
             refs[at][where] = value
 
-    D = R.dx.shape[1]
+    def done(at):
+        for kept, final in zip((masters, firsts, seconds), finals):
+            leave(kept[at], final[at])
+
+    D = dx.shape[1]
+    for at, kind in ((2, KIND_I), (3, KIND_F), (1, KIND_O)):
+        arrive(at, (kind,))
+        for l in range(2):
+            ref = fin[kind]
+            grad = ref[l].astype(F32).reshape(-1, ref.shape[-1])
+            step(at, (l,), grad.T if kind == KIND_F else grad)
+        done(at)
+    arrive(0, (KIND_Q, KIND_K, KIND_V))
     for l in range(2):
         for at, kind in enumerate((KIND_Q, KIND_K, KIND_V)):
-            grad = R.fin[kind][l].astype(F32).reshape(-1, D)
+            grad = fin[kind][l].astype(F32).reshape(-1, D)
             step(0, (l, slice(None), slice(at * D, at * D + D)), grad)
-        for at, kind in ((1, KIND_O), (2, KIND_I)):
-            ref = R.fin[kind]
-            step(at, (l,), ref[l].astype(F32).reshape(-1, ref.shape[-1]))
-        ref = R.fin[KIND_F]
-        step(3, (l,), ref[l].astype(F32).reshape(-1, ref.shape[-1]).T)
-        wide = R.masters[4].shape[2]
-        span = 128 // wide
-        rows = R.masters[4].shape[1]
-        block = R.fvec[16 * l : 16 * l + 16]
+    done(0)
+    arrive(4, ())
+    waits[1].wait()
+    wide = masters[4].shape[2]
+    rows = masters[4].shape[1]
+    span = 128 // wide
+    slot = lax.rem(f, span)
+    for l in range(2):
+        block = fvec[16 * l : 16 * l + 16]
         grad = block[:, :wide]
-        slot = lax.rem(f, span)
         for s in range(1, span):
             grad = jnp.where(slot == s, block[:, s * wide : s * wide + wide], grad)
         step(4, (l,), grad[:rows])
-    R.out[0] = R.y[...]
-    R.grad[0] = R.dx[...].astype(F32)
+    done(4)
+    waits[2].wait()
+    leave(y, R.out.at[0])
+    waits[3].wait()
+    R.wide[...] = dx[...].astype(F32)
+    leave(R.wide, R.grad.at[0])
+    for cp in leaving:
+        cp.wait()
 
 
 def fast_body(
@@ -1475,6 +1541,7 @@
             metab=V((2,) + meta.shape, BF),
             msel=V(meta.shape, BF),
             tokb=V((S, D), BF),
+            cotb=V((S, D), BF),
             A32=V((S, D), F32),
             Ab=V((S, D), BF),
             ATp=V((D, S), BF),
@@ -1499,8 +1566,8 @@
             msem=dma((2, 4)),
             xsem=dma((4,)),
             osem=dma((48,)),
-            gs=dma((12, levels + 4)),
-            gr=dma((12, levels + 4)),
+            gs=dma((16, levels + 4)),
+            gr=dma((16, levels + 4)),
             vs=dma((shards - 1,)),
             vr=dma((shards - 1,)),
             xs=dma((3,)),
@@ -1568,21 +1635,21 @@
             dkr=V((2, D // 128, S, 128), BF),
             dvr=V((2, D // 128, S, 128), BF),
             vg=V((32, D), F32),
-            va=V((4, 32, D), F32),
-            vrecv=V((3, 32, D), F32),
-            vb=V((levels - 1, 32, 128), F32),
+            va=V((2, 4, 16, D), F32),
+            vrecv=V((2, 3, 16, D), F32),
+            vb=V((2, levels - 1, 16, 128), F32),
             vt=V((32, 128), F32),
             lsem=dma((2, 20)),
-            ssem=dma((6,)),
+            ssem=dma((7,)),
             fsem=dma((12,)),
             gs=dma((12, levels + 5)),
             gr=dma((12, levels + 5)),
-            xs=dma((2,)),
-            xr=dma((2,)),
+            xs=dma((3,)),
+            xr=dma((3,)),
             ks=dma((2, 2, 2)),
             kr=dma((2, 2, 2)),
-            vs=dma((levels + 2,)),
-            vr=dma((levels + 2,)),
+            vs=dma((2, levels + 2)),
+            vr=dma((2, levels + 2)),
         ),
         hbm,
         collective_id=1,
@@ -1609,9 +1676,20 @@
             new_firsts=like,
             new_seconds=like,
         ),
-        None,
-        pl.BlockSpec(memory_space=pltpu.VMEM),
-        vmem_limit_bytes=40 << 20,
+        UpdateScratch(
+            inside=(
+                tuple(V(g.shape, BF) for g in grads.fin),
+                V((32, 128), F32),
+                V((S, D), BF),
+                V((S, D), BF),
+                *(tuple(V(p.shape, F32) for p in masters) for _ in range(3)),
+            ),
+            wide=V((S, D), F32),
+            isem=dma((24,)),
+            osem=dma((17,)),
+        ),
+        hbm,
+        vmem_limit_bytes=VMEM_BYTES,
     )
     return (new.out, new.grad, *new.new_masters, *new.new_firsts, *new.new_seconds)
 
@@ -1644,8 +1722,8 @@
     def chosen(*args):
         tokens, master_in = args[0], args[7]
         width = tokens.shape[2]
-        whole_tiles = width % (32 * shards) == 0 and shards * 32 == width
-        if mesh.shape["rep"] == 2 and shards % 4 == 0 and whole_tiles and master_in.shape[2] == 4 * width:
+        whole_tiles = shards * 32 == width and master_in.shape[2] == 4 * width
+        if mesh.shape["rep"] == 2 and shards % 4 == 0 and whole_tiles:
             return fast_body(*args, shards)
         return body(*args)
 

time: 272 us -> 206 us (0.76)
  Pallas kernels: 248 us -> 192 us
  local copies, waits for them, and re-layouts: 14.3 us -> 6.74 us
    pallas_call x3, Pallas kernels: 248 us -> 192 us  [call_kernel(): pl.pallas_call(functools.partial(kernel, empty), out_shape=out_leaves, in...]
    unnamed x49 -> x9, local copies, waits for them, and re-layouts: 11.6 us -> 1.93 us
where the time goes in v2:
time: 206 us; the launch traced here: 205 us
  Pallas kernels  192 us (93%)
  local copies, waits for them, and re-layouts  6.74 us (3%)
  other arithmetic  3.52 us (2%)
  between operations  2.29 us (1%)
    pallas_call x3, Pallas kernels, call_kernel(): pl.pallas_call(functools.partial(kernel, empty), out_shape=out_leaves, in...  192 us

profile of v2, /device:TPU:0, one launch (start us, length us, event | category | flops | bytes accessed | tf_op | source)
XLA Modules:
  0.0 205.0 jit_solution(643839402082979240)
XLA Ops:
  0.7 0.7 copy.43.refs_13_
  1.4 0.0 copy-start
  1.4 0.1 tile.12
  1.5 0.6 select_convert_fusion.1.refs_3_
  2.8 2.0 broadcast_select_fusion.refs_1_
  4.8 0.7 compare_reduce_fusion
  5.5 0.2 select_convert_fusion
  6.4 0.7 concatenate.3.refs_2_
  7.1 92.8 %shard_map.323 = (bf16[2,4,2,2,2,16,512]{6,5,4,3,2,1,0:T(8,128)(2,1)}, bf16[2,4,2,2,2,16,512]{6,5,4,3,2,1,0:T(8,128)(2,1)}, bf16[2,4,2,2,2,16,512]{6,5,4,3,2,1,0...) custom-call(bf16[1,512,512]{2,1,0:T(8,128)(2,1)} %refs_0_.1, ...), custom_call_target="tpu_custom_call" | custom-call | tf_op jit(solution)/shard_map/pallas_call | solution.py:622
  99.9 0.0 copy-start.1
  99.9 0.0 copy-start.2
  100.0 93.3 %shard_map.324 = (bf16[2,2,16,512]{3,2,1,0:T(8,128)(2,1)}, bf16[2,2,16,512]{3,2,1,0:T(8,128)(2,1)}, bf16[2,2,16,512]{3,2,1,0:T(8,128)(2,1)}, bf16[2,2,16,512]{3,...) custom-call(bf16[2,4,2,2,2,16,512]{6,5,4,3,2,1,0:T(8,128)(2,1)} %get, ...), custom_call_target="tpu_custom_call" | custom-call | tf_op jit(solution)/shard_map/pallas_call | solution.py:622
  193.3 0.0 copy-done
  193.3 0.0 copy-done.1
  193.3 0.6 copy.45.refs_18_
  193.9 0.0 copy-done.2
  193.9 0.6 copy.46.refs_23_
  194.5 6.2 %shard_map.325 = (bf16[1,512,512]{2,1,0:T(8,128)(2,1)}, f32[1,512,512]{2,1,0:T(8,128)}, f32[2,32,1536]{2,1,0:T(8,128)}, f32[2,32,512]{2,1,0:T(8,128)}, f32[2,32,...) custom-call(bf16[2,2,16,512]{3,2,1,0:T(8,128)(2,1)} %get-tuple-eleme, ...), custom_call_target="tpu_custom_call" | custom-call | tf_op jit(solution)/shard_map/pallas_call | solution.py:622
  200.8 1.3 copy.47
  202.1 1.3 copy.48
  203.4 1.3 copy.49
  (6 shorter events, 0.1 us)
Async XLA Ops:
  1.4 191.9 %copy-start = (f32[2,14,32]{2,1,0:T(8,128)}, f32[2,14,32]{2,1,0:T(8,128)S(1)}, u32[]{:S(2)}) copy-start(f32[2,14,32]{2,1,0:T(8,128)S(1)} %copy.43.refs_13_) | copy-start | bytes 10756
  99.9 93.4 %copy-start.1 = (f32[2,14,32]{2,0,1:T(2,128)S(1)}, f32[2,14,32]{2,0,1:T(2,128)}, u32[]{:S(2)}) copy-start(f32[2,14,32]{2,0,1:T(2,128)} %param.34) | copy-start | bytes 10756
  99.9 94.0 %copy-start.2 = (f32[2,14,32]{2,0,1:T(2,128)S(1)}, f32[2,14,32]{2,0,1:T(2,128)}, u32[]{:S(2)}) copy-start(f32[2,14,32]{2,0,1:T(2,128)} %param.39) | copy-start | bytes 10756

commit v3 on v2

--- a/solution.py
+++ b/solution.py
@@ -355,37 +355,41 @@
 MESH = pl.DeviceIdType.MESH
 KIND_K, KIND_V, KIND_Q, KIND_O, KIND_I, KIND_F = KINDS = tuple(range(6))
 VMEM_BYTES = 60 << 20
+FORWARD_SPLIT = (2, 2, 1, 2, 2, 1, 3, 2, 0, 2, 1, 2, 3, 0, 2, 3)
+BACKWARD_SPLIT = (2, 2, 0, 1, 0, 3, 2, 2, 0, 3, 0, 2)
+WHOLE_LEVEL_KINDS = (KIND_O, KIND_K)
 FORWARD_TURNS = (
     (1, 2, 0, 3, 1, 4, 2),
     (0, 3, 5, 1, 2, 4, 6, 0, 3, 5, 0, 1, 7),
     (2, 1),
-    (6, 4, 8, 2),
+    (6, 8, 4, 9, 2),
     (),
-    (3, 9),
-    (5, 7, 10, 3, 8, 6),
-    (9, 11),
-    (4, 10, 12),
+    (3, 10, 5, 7),
+    (8, 3, 9, 6),
+    (10,),
+    (4,),
     (),
-    (5, 11),
-    (4, 13),
-    (5, 7, 8, 12),
-    (14, 6, 9, 10, 13, 11, 6, 15, 14, 7, 8, 12, 7, 15),
-    (8, 9),
-    (10,),
-    (13, 9),
-    (10,),
+    (11,),
+    (4,),
+    (5, 8, 12, 7, 11, 9, 5, 13, 6, 14, 10, 8),
+    (12, 6, 15, 7, 11, 9, 14, 7),
+    (9, 10, 13),
+    (15,),
+    (),
+    (12, 10),
     (),
     (11,),
     (14,),
     (11,),
+    (15,),
     (12,),
+    (),
+    (14, 12),
+    (13, 14, 15, 13),
     (15,),
     (),
-    (12, 13),
-    (13, 14),
-    (14, 15, 15),
-    (),
 )
+COTANGENT_AT = 0
 BACKWARD_TURNS = (
     (),
     (),
@@ -399,27 +403,27 @@
     (1, 2),
     (),
     (0,),
+    (2,),
+    (1, 3),
+    (4, 5),
     (),
-    (3, 1),
-    (4, 5),
+    (12, 3),
+    (0, 2, 4, 5, 12),
+    (1, 3, 6),
     (2,),
-    (3, 12),
-    (4, 5, 0, 12),
-    (1, 6),
-    (2,),
+    (5, 12),
+    (7,),
+    (2, 0, 3, 6, 5, 12),
     (),
-    (3, 7),
-    (4,),
-    (5, 0, 6, 12, 3),
-    (4, 7, 8, 5),
-    (0, 1, 8),
-    (2, 3, 12),
-    (4, 5, 6, 12),
-    (7,),
+    (7, 8),
+    (0, 4, 8),
+    (6,),
+    (1, 3),
+    (4, 5, 7, 12),
     (9,),
-    (1, 10, 11),
+    (10, 11, 6),
     (),
-    (8, 2, 9, 3, 13, 4, 10, 5, 11, 13, 6, 7, 6, 8, 9, 10, 11, 7, 13, 8, 6, 9, 10, 13, 11, 7, 8, 9, 10, 13, 9, 11, 10, 11),
+    (9, 1, 13, 3, 10, 4, 8, 5, 11, 13, 7, 8, 6, 9, 4, 11, 10, 13, 8, 6, 9, 10, 11, 13, 8, 7, 10, 9, 11, 13, 7, 10, 9, 11),
 )
 
 
@@ -445,8 +449,10 @@
 class ForwardIn(NamedTuple):
     tok: object
     cot: object
-    meta: object
-    vecb: object
+    lengths: object
+    tags: object
+    key_mask: object
+    vectors: object
     masters: object
 
 
@@ -525,10 +531,8 @@
 class BackwardScratch(NamedTuple):
     g: object
     landing: object
-    half_y: object
-    half_x: object
-    quarter_x: object
-    quarter_y: object
+    half: object
+    quarter: object
     level: object
     total: object
     w: object
@@ -622,8 +626,8 @@
     results = pl.pallas_call(
         functools.partial(kernel, empty),
         out_shape=out_leaves,
-        in_specs=[spec] * len(leaves),
-        out_specs=[spec] * len(out_leaves),
+        in_specs=jax.tree.leaves(spec) if isinstance(spec, tuple) else [spec] * len(leaves),
+        out_specs=[pl.BlockSpec(memory_space=pl.ANY)] * len(out_leaves),
         scratch_shapes=() if scratch is None else jax.tree.leaves(scratch),
         compiler_params=pltpu.CompilerParams(**options),
     )(*leaves)
@@ -653,6 +657,10 @@
     return blocks[:, 0].reshape(half, rows.shape[1]), blocks[:, 1].reshape(half, rows.shape[1])
 
 
+def halves(cut, levels):
+    return pl.ds(0, cut), pl.ds(cut, levels - cut)
+
+
 def go_or_stay(stays, stay, go):
     @pl.when(stays)
     def _():
@@ -686,22 +694,14 @@
     shards = levels * 4
     S, D = R.A32.shape
     FF = R.G.shape[1]
-    ha = levels // 2
-    first, second = pl.ds(0, ha), pl.ds(ha, levels - ha)
     source = ((0, D), (0, 2 * D), (0, 0), (1, 0), (2, 0), (3, 0))
 
     half_loads = {}
     for l in range(2):
         for at, (master, stage) in enumerate(zip(R.masters, R.stages)):
-            rows = stage.shape[1]
-            cp = pltpu.make_async_copy(master.at[l, pl.ds(r * rows, rows)], stage.at[l], R.msem.at[l, at])
+            cp = pltpu.make_async_copy(master.at[l], stage.at[l], R.msem.at[l, at])
             cp.start()
             half_loads[(l, at)] = cp
-    vec_local = pltpu.make_async_copy(R.vecb, R.vecg.at[f], R.xsem.at[0])
-    vec_local.start()
-    meta_local = pltpu.make_async_copy(R.meta, R.metab.at[0], R.xsem.at[1])
-    meta_local.start()
-
     barrier = pltpu.get_barrier_semaphore()
     peers = [(r, lax.rem(f + s, shards)) for s in range(1, shards)] + [me.xn, me.dn]
     for peer in peers:
@@ -745,7 +745,8 @@
         if (l, at) not in loaded:
             half_loads[(l, at)].wait()
             loaded.add((l, at))
-        w[l, z, y, c, r, :, cols] = R.stages[at][l][:, offset + cols.start : offset + cols.stop].astype(BF)
+        rows = w.shape[5]
+        w[l, z, y, c, r, :, cols] = R.stages[at][l, pl.ds(r * rows, rows), offset + cols.start : offset + cols.stop].astype(BF)
         cps = []
         for s in range(1, levels):
             _, dev = me.zn(s, levels)
@@ -758,6 +759,7 @@
         w = R.w[kind]
         for cp in stage_copies[i]:
             cp.wait_recv()
+        first, second = halves(FORWARD_SPLIT[i], levels)
         a, b = w.at[l, first, y, c, r, :, cols], w.at[l, second, y, c, r, :, cols]
         stage_copies[i] = [
             start(remote(a, a, gs.at[i, levels - 1], gr.at[i, levels - 1], me.xn)),
@@ -769,6 +771,7 @@
         w = R.w[kind]
         for cp in stage_copies[i]:
             cp.wait_recv()
+        first, second = halves(FORWARD_SPLIT[i], levels)
         a, b = w.at[l, first, y, c, :, :, cols], w.at[l, second, :, c, r, :, cols]
         stage_copies[i] = [
             start(remote(a, a, gs.at[i, levels + 1], gr.at[i, levels + 1], me.yn)),
@@ -783,6 +786,28 @@
         a = w.at[l, :, :, c, :, :, cols]
         stage_copies[i] = [start(remote(a, a, gs.at[i, levels + 3], gr.at[i, levels + 3], me.cn))]
 
+    def h_y(i):
+        kind, l, cols = chunks[i]
+        w = R.w[kind]
+        at, offset = source[kind]
+        if (l, at) not in loaded:
+            half_loads[(l, at)].wait()
+            loaded.add((l, at))
+        whole = R.stages[at][l][:, offset + cols.start : offset + cols.stop].astype(BF)
+        w[l, z, y, c, :, :, cols] = whole.reshape(2, whole.shape[0] // 2, whole.shape[1])
+        spot = w.at[l, z, y, c, :, :, cols]
+        stage_copies[i] = [start(remote(spot, spot, gs.at[i, 0], gr.at[i, 0], me.yn))]
+
+    def h_z(i):
+        kind, l, cols = chunks[i]
+        w = R.w[kind]
+        for cp in stage_copies[i]:
+            cp.wait_recv()
+        spot = w.at[l, z, :, c, :, :, cols]
+        stage_copies[i] = [
+            start(remote(spot, spot, gs.at[i, s], gr.at[i, s], me.zn(s, levels)[1])) for s in range(1, levels)
+        ]
+
     def g_ready(i):
         kind, l, cols = chunks[i]
         for cp in stage_copies.pop(i):
@@ -791,32 +816,47 @@
             out(R.w[kind], R.w_o[kind].at[l], R.w[kind].at[l])
 
     steps = (g_z, g_1, g_2, g_core, g_ready)
+    other_steps = (h_y, h_z, g_core, g_ready)
     reached = [0] * len(chunks)
     turns = iter(FORWARD_TURNS)
 
     def turn():
         for i in next(turns):
-            steps[reached[i]](i)
+            (steps if FORWARD_SPLIT[i] else other_steps)[reached[i]](i)
             reached[i] += 1
 
     steps[0](0)
     reached[0] = 1
-    meta_cp = start(remote(R.meta, R.metab.at[1], R.xs.at[0], R.xr.at[0], me.cn))
+    tok_far = remote(R.tok.at[0], R.tokb, R.xs.at[1], R.xr.at[1], me.dn)
+    tok_near = pltpu.make_async_copy(R.tok.at[0], R.tokb, R.xsem.at[2])
+    stays = c == r
+
+    go_or_stay(stays, tok_near.start, tok_far.start)
+    length = R.lengths[0]
+    keys = R.key_mask[...]
+    key_pos = lax.broadcasted_iota(jnp.int32, keys.shape, 1)
+    valid = key_pos < length
+    bias = jnp.where(valid & ((keys == 1) | (key_pos == 0)), 0.0, masked_score)
+    place = lax.broadcasted_iota(jnp.int32, (128, 2 * S), 0)
+    columns = jnp.where(lax.rem(place, 64) == 0, bias, 0.0) + jnp.where((place == 1) & valid, 1.0, 0.0)
+    R.metab[0, : 2 * S] = columns.T.astype(BF)
+    R.metab[0, 2 * S :] = jnp.full((16, 128), R.tags[0].astype(F32)).astype(BF)
+    meta_cp = start(remote(R.metab.at[0], R.metab.at[1], R.xs.at[0], R.xr.at[0], me.cn))
+    wide = R.vectors.shape[2]
+    lane = lax.broadcasted_iota(jnp.int32, (R.vectors.shape[0], 128), 1)
+    R.vecg[f] = jnp.zeros((32, 128), BF)
+    for l in range(2):
+        block = jnp.concatenate([R.vectors[:, l]] * (128 // wide), axis=1)
+        block = jnp.where(lax.div(lane, wide) == lax.rem(f, 128 // wide), block, 0.0)
+        block = jnp.concatenate([block, jnp.zeros((16 - block.shape[0], 128), F32)], axis=0)
+        R.vecg[f, 16 * l : 16 * l + 16] = block.astype(BF)
     vec_cps = []
     for s in range(1, shards):
         spot = R.vecg.at[f]
-        vec_cps.append((s, remote(R.vecb, spot, R.vs.at[s - 1], R.vr.at[s - 1], (r, lax.rem(f + s, shards)))))
+        vec_cps.append((s, remote(spot, spot, R.vs.at[s - 1], R.vr.at[s - 1], (r, lax.rem(f + s, shards)))))
     for _, cp in vec_cps:
         start(cp)
-    tok_far = remote(R.tok.at[0], R.tokb, R.xs.at[1], R.xr.at[1], me.dn)
-    tok_near = pltpu.make_async_copy(R.tok.at[0], R.tokb, R.xsem.at[2])
-    stays = c == r
-
-    go_or_stay(stays, tok_near.start, tok_far.start)
-
     turn()
-    vec_local.wait()
-    meta_local.wait()
     meta_cp.wait_recv()
     for _, cp in vec_cps:
         cp.wait_recv()
@@ -840,7 +880,6 @@
         direction = e(0) * (1.0 - tag_row) + e(1) * tag_row
         if l == 1:
             turn()
-            go_or_stay(stays, cot_near.start, cot_far.start)
         A32, Ab, Q, K, V, CT = R.A32, R.Ab, R.Q, R.K, R.V, R.CT
         x_in = R.tokb if l == 0 else R.X
         summed = x_in[...].astype(F32) + direction
@@ -927,9 +966,6 @@
             return carry
 
         turn()
-        if l == 1:
-            go_or_stay(stays, cot_near.wait, cot_far.wait_recv)
-            out(R.cotb, R.cot_o)
         lax.fori_loop(0, S // T, norm_one, 0)
         out(R.N1, R.n1_o.at[l])
         out(R.r1, R.r1_o.at[l])
@@ -953,6 +989,8 @@
         for b in range(FF // D):
             if b % 2 == 0:
                 turn()
+            if l == 1 and b == COTANGENT_AT:
+                go_or_stay(stays, cot_near.start, cot_far.start)
             inner(b)
         out(R.G, R.g_o.at[l])
         out(R.Gp, R.gp_o.at[l])
@@ -981,6 +1019,8 @@
     out(R.Yb, R.y_o)
     out(vec, R.vec_o)
     out(msel, R.meta_o)
+    go_or_stay(stays, cot_near.wait, cot_far.wait_recv)
+    out(R.cotb, R.cot_o)
     for cp in out_copies.values():
         cp.wait()
     for cp in pending:
@@ -995,9 +1035,6 @@
     shards = levels * 4
     S, D = R.dy.shape
     FF = R.G.shape[1]
-    ha = levels // 2
-    hb = levels - ha
-    first, second = pl.ds(0, ha), pl.ds(ha, hb)
     saved = list(zip(R.w, R.w_o)) + [
         (R.AT, R.at_o), (R.Q, R.q_o), (R.K, R.k_o), (R.V, R.v_o), (R.lse, R.lse_o), (R.CT, R.ct_o), (R.CTp, R.ctp_o),
         (R.N1, R.n1_o), (R.r1, R.r1_o), (R.HT, R.ht_o), (R.G, R.g_o), (R.Gp, R.gp_o), (R.N2, R.n2_o), (R.r2, R.r2_o),
@@ -1022,8 +1059,9 @@
         cp.start()
         small.append(cp)
     wk, wv, wq, wo, wi, wf = R.w
-    for ref in (R.N2, R.r2, R.G, wf, R.Gp, R.HT, wi, R.N1, R.r1, R.CTp, wo, R.CT, R.K, R.V, R.Q, R.lse, R.AT, wq, wk, wv):
+    for ref in (R.N2, R.r2, R.G):
         load(ref, 1)
+    later = (wf, R.Gp, R.HT, wi, R.N1, R.r1, R.CTp, wo, R.CT, R.K, R.V, R.Q, R.lse, R.AT, wq, wk, wv)
 
     barrier = pltpu.get_barrier_semaphore()
     peers = [me.zn(s, levels)[1] for s in range(1, levels)] + [me.xn, me.yn, me.cn, me.dn]
@@ -1061,32 +1099,42 @@
     def rs_1(i):
         kind, l = chunks[i]
         g = R.g[kind]
+        first, second = halves(BACKWARD_SPLIT[i], levels)
+        half, quarter = R.half[kind], R.quarter[kind]
         g[l, c] = g[l, c] + (g[0, 0] if l == 1 else R.landing[kind][...])
         flight[i] = [
-            start(remote(g.at[l, c, first, 1 - y], R.half_y[kind].at[l], gs.at[i, 1], gr.at[i, 1], me.yn)),
-            start(remote(g.at[l, c, second, :, 1 - r], R.half_x[kind].at[l], gs.at[i, 2], gr.at[i, 2], me.xn)),
+            start(remote(g.at[l, c, first, 1 - y], half.at[l, first], gs.at[i, 1], gr.at[i, 1], me.yn)),
+            start(remote(g.at[l, c, second, :, 1 - r], half.at[l, second], gs.at[i, 2], gr.at[i, 2], me.xn)),
         ]
 
     def rs_2(i):
         kind, l = chunks[i]
         g = R.g[kind]
-        g[l, c, first, y] = g[l, c, first, y] + R.half_y[kind][l]
-        g[l, c, second, :, r] = g[l, c, second, :, r] + R.half_x[kind][l]
+        first, second = halves(BACKWARD_SPLIT[i], levels)
+        half, quarter = R.half[kind], R.quarter[kind]
+        g[l, c, first, y] = g[l, c, first, y] + half[l, first]
+        g[l, c, second, :, r] = g[l, c, second, :, r] + half[l, second]
         flight[i] = [
-            start(remote(g.at[l, c, first, y, 1 - r], R.quarter_x[kind].at[l], gs.at[i, 3], gr.at[i, 3], me.xn)),
-            start(remote(g.at[l, c, second, 1 - y, r], R.quarter_y[kind].at[l], gs.at[i, 4], gr.at[i, 4], me.yn)),
+            start(remote(g.at[l, c, first, y, 1 - r], quarter.at[l, first], gs.at[i, 3], gr.at[i, 3], me.xn)),
+            start(remote(g.at[l, c, second, 1 - y, r], quarter.at[l, second], gs.at[i, 4], gr.at[i, 4], me.yn)),
         ]
+
+    def level_spot(kind, l, s):
+        ref = R.level[kind]
+        return ref.at[l, s, 0, 0] if len(ref.shape) == 6 else ref.at[l, s]
 
     def rs_3(i):
         kind, l = chunks[i]
         g = R.g[kind]
-        g[l, c, first, y, r] = g[l, c, first, y, r] + R.quarter_x[kind][l]
-        g[l, c, second, y, r] = g[l, c, second, y, r] + R.quarter_y[kind][l]
+        first, second = halves(BACKWARD_SPLIT[i], levels)
+        half, quarter = R.half[kind], R.quarter[kind]
+        g[l, c, first, y, r] = g[l, c, first, y, r] + quarter[l, first]
+        g[l, c, second, y, r] = g[l, c, second, y, r] + quarter[l, second]
         flight[i] = []
         for s in range(1, levels):
             there, dev = me.zn(s, levels)
             flight[i].append(
-                start(remote(g.at[l, c, there, y, r], R.level[kind].at[l, s - 1], gs.at[i, 4 + s], gr.at[i, 4 + s], dev))
+                start(remote(g.at[l, c, there, y, r], level_spot(kind, l, s - 1), gs.at[i, 4 + s], gr.at[i, 4 + s], dev))
             )
 
     def rs_4(i):
@@ -1094,7 +1142,7 @@
         g, fin = R.g[kind], R.total[kind]
         total = g[l, c, z, y, r].astype(F32)
         for s in range(levels - 1):
-            total = total + R.level[kind][l, s].astype(F32)
+            total = total + level_spot(kind, l, s)[...].astype(F32)
         fin[l, r] = total.astype(BF)
         flight[i] = [start(remote(fin.at[l, r], fin.at[l, r], gs.at[i, 4 + levels], gr.at[i, 4 + levels], me.xn))]
 
@@ -1133,6 +1181,42 @@
             total = total + vb[l, s]
         vt[16 * l : 16 * l + 16] = total
 
+    def hs_z(i):
+        kind, l = chunks[i]
+        g = R.g[kind]
+        g[l, c] = g[l, c] + (g[0, 0] if l == 1 else R.landing[kind][...])
+        flight[i] = []
+        for s in range(1, levels):
+            there, dev = me.zn(s, levels)
+            flight[i].append(
+                start(remote(g.at[l, c, there], R.level[kind].at[l, s - 1], gs.at[i, s], gr.at[i, s], dev))
+            )
+
+    def hs_y(i):
+        kind, l = chunks[i]
+        g = R.g[kind]
+        whole = g[l, c, z].astype(F32)
+        for s in range(levels - 1):
+            whole = whole + R.level[kind][l, s].astype(F32)
+        g[l, c, z] = whole.astype(BF)
+        spot = R.half[kind].at[l, 0]
+        flight[i] = [start(remote(g.at[l, c, z, 1 - y], spot, gs.at[i, levels], gr.at[i, levels], me.yn))]
+
+    def hs_x(i):
+        kind, l = chunks[i]
+        g = R.g[kind]
+        g[l, c, z, y] = g[l, c, z, y] + R.half[kind][l, 0]
+        spot = R.quarter[kind].at[l, 0]
+        sems = gs.at[i, levels + 1], gr.at[i, levels + 1]
+        flight[i] = [start(remote(g.at[l, c, z, y, 1 - r], spot, *sems, me.xn))]
+
+    def hs_end(i):
+        kind, l = chunks[i]
+        g, fin = R.g[kind], R.total[kind]
+        fin[l, r] = g[l, c, z, y, r] + R.quarter[kind][l, 0]
+        flight[i] = [start(remote(fin.at[l, r], fin.at[l, r], gs.at[i, 4 + levels], gr.at[i, 4 + levels], me.xn))]
+
+    other_steps = (rs_core, hs_z, hs_y, hs_x, hs_end, rs_5)
     matrix_steps = (rs_core, rs_1, rs_2, rs_3, rs_4, rs_5)
     vec_steps = (vec_hop(0, me.cn), vec_hop(1, me.xn), vec_hop(2, me.yn), vec_level, vec_end)
     turns = iter(BACKWARD_TURNS)
@@ -1142,7 +1226,8 @@
             at = stage.get(i, 0)
             for cp in flight.pop(i, ()):
                 cp.wait_recv()
-            (matrix_steps if chunks[i][0] is not None else vec_steps)[at](i)
+            known = matrix_steps if i < len(BACKWARD_SPLIT) and BACKWARD_SPLIT[i] else other_steps
+            (vec_steps if chunks[i][0] is None else known)[at](i)
             stage[i] = at + 1
 
     for cp in small:
@@ -1153,7 +1238,7 @@
     low, high, spots = lane_masks()
     low32 = low.astype(F32)
     vg[...] = jnp.zeros_like(vg)
-    R.dy[...] = R.cotb[...].astype(F32)
+    R.dy[...] = R.cotb[...].astype(F32) * msel[pl.ds(c * S, S)][:, 1:2].astype(F32)
     T = 256
     dy, dpre, dF, dFT, dU, dZ = R.dy, R.dpre, R.dF, R.dFT, R.dU, R.dZ
 
@@ -1175,6 +1260,9 @@
 
         turn()
         N2, r2 = use(R.N2), use(R.r2)
+        if l == 1:
+            for ref in later:
+                load(ref, 1)
 
         def norm_two(t, carry):
             s7, s8, s9 = carry
@@ -1452,7 +1540,7 @@
     arrive(4, ())
     waits[1].wait()
     wide = masters[4].shape[2]
-    rows = masters[4].shape[1]
+    rows = masters[4].shape[0]
     span = 128 // wide
     slot = lax.rem(f, span)
     for l in range(2):
@@ -1460,7 +1548,7 @@
         grad = block[:, :wide]
         for s in range(1, span):
             grad = jnp.where(slot == s, block[:, s * wide : s * wide + wide], grad)
-        step(4, (l,), grad[:rows])
+        step(4, (slice(None), l), grad[:rows])
     done(4)
     waits[2].wait()
     leave(y, R.out.at[0])
@@ -1482,40 +1570,32 @@
     FF = master_in.shape[2]
     levels = shards // 4
     rows, cols = sizes_of(shards, D, FF)
-    f = lax.axis_index("fsdp")
-    key_count = key_mask.shape[1]
-    key_pos = jnp.arange(key_count, dtype=jnp.int32)
-    valid = key_pos < lengths[0]
-    key_valid = valid & ((key_mask[0] == 1) | (key_pos == 0))
-    lane = jnp.arange(128, dtype=jnp.int32)
-    bias = jnp.where(key_valid, 0.0, masked_score).astype(F32)
-    meta = jnp.where((lane % 64 == 0)[None, :], bias[:, None], 0.0)
-    tag_rows = jnp.full((16, 128), tags[0], F32)
-    meta = jnp.concatenate([meta, tag_rows], axis=0).astype(BF)
-    start_row = lax.axis_index("rep") * S
-    query_valid = (start_row + jnp.arange(S, dtype=jnp.int32)) < lengths[0]
-    cot = jnp.where(query_valid[None, :, None], cotangent, jnp.zeros_like(cotangent))
-    wide = master_vec.shape[2]
-    vec_rows = jnp.pad(master_vec, ((0, 0), (0, 16 - master_vec.shape[1]), (0, 0))).reshape(32, wide)
-    slot = (lane // wide) == lax.rem(f, 128 // wide)
-    vecb = jnp.where(slot[None, :], jnp.tile(vec_rows, (1, 128 // wide)), 0.0).astype(BF)
-
+    meta_shape = (2 * S + 16, 128)
+    by_row = lambda vectors: vectors.transpose(1, 0, 2)
     hbm = pl.BlockSpec(memory_space=pl.ANY)
     shape = jax.ShapeDtypeStruct
     V = pltpu.VMEM
     dma = pltpu.SemaphoreType.DMA
     w_tail = [(levels, 2, 2, 2, rows[k], cols[k]) for k in KINDS]
-    masters = (master_qkv, master_out, master_in, master_feed_output, master_vec)
-    firsts = (first_qkv, first_out, first_in, first_ffo, first_vec)
-    seconds = (second_qkv, second_out, second_in, second_ffo, second_moment_vector)
+    masters = (master_qkv, master_out, master_in, master_feed_output, by_row(master_vec))
+    firsts = (first_qkv, first_out, first_in, first_ffo, by_row(first_vec))
+    seconds = (second_qkv, second_out, second_in, second_ffo, by_row(second_moment_vector))
 
     saved = call_kernel(
         lambda parts, *refs: forward_kernel(parts, levels, norm_epsilon, *refs),
-        ForwardIn(tok=tokens, cot=cot, meta=meta, vecb=vecb, masters=masters[:4]),
+        ForwardIn(
+            tok=tokens,
+            cot=cotangent,
+            lengths=lengths,
+            tags=tags,
+            key_mask=key_mask,
+            vectors=by_row(master_vec),
+            masters=masters[:4],
+        ),
         Saved(
             w_o=tuple(shape((2,) + tail, BF) for tail in w_tail),
             vec_o=shape((32, D), F32),
-            meta_o=shape(meta.shape, BF),
+            meta_o=shape(meta_shape, BF),
             cot_o=shape((S, D), BF),
             y_o=shape((S, D), BF),
             at_o=shape((2, D, S), BF),
@@ -1535,11 +1615,11 @@
         ),
         ForwardScratch(
             w=tuple(V((2,) + tail, BF) for tail in w_tail),
-            stages=tuple(V((2, m.shape[1] // 2, m.shape[2]), F32) for m in masters[:4]),
+            stages=tuple(V(m.shape, F32) for m in masters[:4]),
             vecg=V((shards, 32, 128), BF),
             vec=V((32, D), F32),
-            metab=V((2,) + meta.shape, BF),
-            msel=V(meta.shape, BF),
+            metab=V((2,) + meta_shape, BF),
+            msel=V(meta_shape, BF),
             tokb=V((S, D), BF),
             cotb=V((S, D), BF),
             A32=V((S, D), F32),
@@ -1575,7 +1655,15 @@
             ks=dma((2, 2)),
             kr=dma((2, 2)),
         ),
-        hbm,
+        ForwardIn(
+            tok=hbm,
+            cot=hbm,
+            lengths=pl.BlockSpec(memory_space=pltpu.SMEM),
+            tags=pl.BlockSpec(memory_space=pltpu.SMEM),
+            key_mask=pl.BlockSpec(memory_space=pltpu.VMEM),
+            vectors=pl.BlockSpec(memory_space=pltpu.VMEM),
+            masters=(hbm,) * 4,
+        ),
         collective_id=0,
         has_side_effects=True,
         vmem_limit_bytes=VMEM_BYTES,
@@ -1583,7 +1671,6 @@
 
     tails = [(rows[k], cols[k]) for k in KINDS]
     tails[KIND_F] = (D // 2, FF // shards)
-    ha, hb = levels // 2, levels - levels // 2
     each = lambda *lead: tuple(V(lead + tail, BF) for tail in tails)
     grads = call_kernel(
         lambda parts, *refs: backward_kernel(parts, levels, *refs),
@@ -1597,11 +1684,11 @@
         BackwardScratch(
             g=each(2, 2, levels, 2, 2),
             landing=each(levels, 2, 2),
-            half_y=each(2, ha, 2),
-            half_x=each(2, hb, 2),
-            quarter_x=each(2, ha),
-            quarter_y=each(2, hb),
-            level=each(2, levels - 1),
+            half=each(2, levels, 2),
+            quarter=each(2, levels),
+            level=tuple(
+                V((2, levels - 1) + ((2, 2) if k in WHOLE_LEVEL_KINDS else ()) + tail, BF) for k, tail in zip(KINDS, tails)
+            ),
             total=each(2, 2),
             w=tuple(V(tail, BF) for tail in w_tail),
             AT=V((D, S), BF),
@@ -1619,7 +1706,7 @@
             N2=V((S, D), F32),
             r2=V((S, 128), F32),
             vec=V((32, D), F32),
-            msel=V(meta.shape, BF),
+            msel=V(meta_shape, BF),
             cotb=V((S, D), BF),
             dy=V((S, D), F32),
             dpre=V((S, D), F32),
@@ -1691,7 +1778,8 @@
         hbm,
         vmem_limit_bytes=VMEM_BYTES,
     )
-    return (new.out, new.grad, *new.new_masters, *new.new_firsts, *new.new_seconds)
+    trees = [(*tree[:4], by_row(tree[4])) for tree in (new.new_masters, new.new_firsts, new.new_seconds)]
+    return (new.out, new.grad, *trees[0], *trees[1], *trees[2])
 
 
 def solution(mesh):

time: 206 us -> 182 us (0.88)
  Pallas kernels: 192 us -> 180 us
  local copies, waits for them, and re-layouts: 6.74 us -> 0 us
  other arithmetic: 3.52 us -> 0 us
    pallas_call x3, Pallas kernels: 192 us -> 180 us  [call_kernel(): pl.pallas_call(functools.partial(kernel, empty), out_shape=out_leaves, in...]
    pallas_call x3 -> x0, local copies, waits for them, and re-layouts: 3.97 us -> none  [call_kernel(): pl.pallas_call(functools.partial(kernel, empty), out_shape=out_leaves, in...]
where the time goes in v3:
time: 182 us
  Pallas kernels  180 us (99%)
  between operations  2.21 us (1%)
    pallas_call x3, Pallas kernels, call_kernel(): pl.pallas_call(functools.partial(kernel, empty), out_shape=out_leaves, in...  180 us

profile of v3, /device:TPU:0, one launch (start us, length us, event | category | flops | bytes accessed | tf_op | source)
XLA Modules:
  0.0 181.9 jit_solution(9261799076132384053)
XLA Ops:
  1.9 85.8 %shard_map.323 = (bf16[2,4,2,2,2,16,512]{6,5,4,3,2,1,0:T(8,128)(2,1)}, bf16[2,4,2,2,2,16,512]{6,5,4,3,2,1,0:T(8,128)(2,1)}, bf16[2,4,2,2,2,16,512]{6,5,4,3,2,1,0...) custom-call(bf16[1,512,512]{2,1,0:T(8,128)(2,1)} %refs_0_.1, ...), custom_call_target="tpu_custom_call" | custom-call | tf_op jit(solution)/shard_map/pallas_call | solution.py:626
  87.8 87.6 %shard_map.324 = (bf16[2,2,16,512]{3,2,1,0:T(8,128)(2,1)}, bf16[2,2,16,512]{3,2,1,0:T(8,128)(2,1)}, bf16[2,2,16,512]{3,2,1,0:T(8,128)(2,1)}, bf16[2,2,16,512]{3,...) custom-call(bf16[2,4,2,2,2,16,512]{6,5,4,3,2,1,0:T(8,128)(2,1)} %get, ...), custom_call_target="tpu_custom_call" | custom-call | tf_op jit(solution)/shard_map/pallas_call | solution.py:626
  175.3 6.3 %shard_map.325 = (bf16[1,512,512]{2,1,0:T(8,128)(2,1)}, f32[1,512,512]{2,1,0:T(8,128)}, f32[2,32,1536]{2,1,0:T(8,128)}, f32[2,32,512]{2,1,0:T(8,128)}, f32[2,32,...) custom-call(bf16[2,2,16,512]{3,2,1,0:T(8,128)(2,1)} %get-tuple-eleme, ...), custom_call_target="tpu_custom_call" | custom-call | tf_op jit(solution)/shard_map/pallas_call | solution.py:626

commit v4 on v3

--- a/solution.py
+++ b/solution.py
@@ -355,38 +355,37 @@
 MESH = pl.DeviceIdType.MESH
 KIND_K, KIND_V, KIND_Q, KIND_O, KIND_I, KIND_F = KINDS = tuple(range(6))
 VMEM_BYTES = 60 << 20
-FORWARD_SPLIT = (2, 2, 1, 2, 2, 1, 3, 2, 0, 2, 1, 2, 3, 0, 2, 3)
-BACKWARD_SPLIT = (2, 2, 0, 1, 0, 3, 2, 2, 0, 3, 0, 2)
-WHOLE_LEVEL_KINDS = (KIND_O, KIND_K)
+FORWARD_SPLIT = (1, 1, 2, 1, 1, 1, 1, 1, 5, 5, 5, 1, 1, 2, 2, 5)
+BACKWARD_SPLIT = (1, 2, 5, 1, 1, 5, 2, 2, 5, 3, 1, 5)
 FORWARD_TURNS = (
-    (1, 2, 0, 3, 1, 4, 2),
-    (0, 3, 5, 1, 2, 4, 6, 0, 3, 5, 0, 1, 7),
-    (2, 1),
-    (6, 8, 4, 9, 2),
+    (1, 2, 0, 3, 4, 1, 2, 5),
+    (3, 0, 6, 1, 2, 4, 7, 3, 0, 5, 0, 1, 8),
+    (2, 6, 4, 1, 9),
+    (2,),
     (),
-    (3, 10, 5, 7),
-    (8, 3, 9, 6),
-    (10,),
-    (4,),
+    (7, 3, 5, 10),
+    (6,),
+    (11, 3, 8),
+    (4, 9, 12, 7),
+    (13,),
+    (),
+    (4, 10),
+    (5, 11, 14, 8, 12, 5, 15),
+    (6, 8, 13, 9, 6, 10, 14, 9, 7, 11, 10, 12, 7),
+    (13,),
+    (14, 15),
     (),
     (11,),
-    (4,),
-    (5, 8, 12, 7, 11, 9, 5, 13, 6, 14, 10, 8),
-    (12, 6, 15, 7, 11, 9, 14, 7),
-    (9, 10, 13),
-    (15,),
     (),
-    (12, 10),
     (),
     (11,),
-    (14,),
-    (11,),
-    (15,),
     (12,),
     (),
-    (14, 12),
-    (13, 14, 15, 13),
-    (15,),
+    (13, 12),
+    (),
+    (),
+    (13, 14),
+    (15, 14, 15),
     (),
 )
 COTANGENT_AT = 0
@@ -400,30 +399,30 @@
     (),
     (0,),
     (2,),
-    (1, 2),
+    (2, 1),
     (),
+    (2,),
     (0,),
-    (2,),
-    (1, 3),
+    (3,),
     (4, 5),
     (),
-    (12, 3),
-    (0, 2, 4, 5, 12),
-    (1, 3, 6),
-    (2,),
-    (5, 12),
-    (7,),
-    (2, 0, 3, 6, 5, 12),
+    (2, 3, 12),
+    (4, 5, 1, 12),
+    (6, 2, 0, 3),
     (),
-    (7, 8),
-    (0, 4, 8),
+    (),
+    (4, 5, 7),
     (6,),
-    (1, 3),
-    (4, 5, 7, 12),
+    (12, 1),
+    (3, 8),
+    (4, 0, 8, 7),
+    (6, 0, 5, 12),
+    (8, 1),
+    (4, 3, 12),
     (9,),
-    (10, 11, 6),
-    (),
-    (9, 1, 13, 3, 10, 4, 8, 5, 11, 13, 7, 8, 6, 9, 4, 11, 10, 13, 8, 6, 9, 10, 11, 13, 8, 7, 10, 9, 11, 13, 7, 10, 9, 11),
+    (11, 10),
+    (7, 5, 8, 9),
+    (11, 13, 1, 10, 4, 3, 6, 13, 7, 8, 9, 11, 6, 10, 13, 9, 7, 6, 10, 13, 11, 7, 9, 10, 11, 13, 9, 10),
 )
 
 
@@ -482,6 +481,7 @@
     w: object
     stages: object
     vecg: object
+    vecl: object
     vec: object
     metab: object
     msel: object
@@ -645,6 +645,7 @@
         self.yn = (self.r, self.f + 2 - 4 * self.y)
         self.cn = (self.r, self.f + 1 - 2 * self.c)
         self.dn = (1 - self.r, self.f + 1 - 2 * self.c)
+        self.en = (self.r, self.f + 3 - 4 * self.y - 2 * self.c)
 
     def zn(self, step, levels):
         other = lax.rem(self.z + step, levels)
@@ -703,7 +704,7 @@
             cp.start()
             half_loads[(l, at)] = cp
     barrier = pltpu.get_barrier_semaphore()
-    peers = [(r, lax.rem(f + s, shards)) for s in range(1, shards)] + [me.xn, me.dn]
+    peers = [me.zn(s, levels)[1] for s in range(1, levels)] + [me.xn, me.yn, me.cn, me.dn, me.en]
     for peer in peers:
         pl.semaphore_signal(barrier, inc=1, device_id=peer, device_id_type=MESH)
     pl.semaphore_wait(barrier, len(peers))
@@ -786,7 +787,7 @@
         a = w.at[l, :, :, c, :, :, cols]
         stage_copies[i] = [start(remote(a, a, gs.at[i, levels + 3], gr.at[i, levels + 3], me.cn))]
 
-    def h_y(i):
+    def h_z(i):
         kind, l, cols = chunks[i]
         w = R.w[kind]
         at, offset = source[kind]
@@ -796,33 +797,35 @@
         whole = R.stages[at][l][:, offset + cols.start : offset + cols.stop].astype(BF)
         w[l, z, y, c, :, :, cols] = whole.reshape(2, whole.shape[0] // 2, whole.shape[1])
         spot = w.at[l, z, y, c, :, :, cols]
-        stage_copies[i] = [start(remote(spot, spot, gs.at[i, 0], gr.at[i, 0], me.yn))]
-
-    def h_z(i):
+        stage_copies[i] = [
+            start(remote(spot, spot, gs.at[i, s], gr.at[i, s], me.zn(s, levels)[1])) for s in range(1, levels)
+        ]
+
+    def h_y(i):
         kind, l, cols = chunks[i]
         w = R.w[kind]
         for cp in stage_copies[i]:
             cp.wait_recv()
-        spot = w.at[l, z, :, c, :, :, cols]
-        stage_copies[i] = [
-            start(remote(spot, spot, gs.at[i, s], gr.at[i, s], me.zn(s, levels)[1])) for s in range(1, levels)
-        ]
+        spot = w.at[l, :, y, c, :, :, cols]
+        stage_copies[i] = [start(remote(spot, spot, gs.at[i, 0], gr.at[i, 0], me.yn))]
 
     def g_ready(i):
         kind, l, cols = chunks[i]
         for cp in stage_copies.pop(i):
             cp.wait_recv()
-        if cols.stop == R.w[kind].shape[-1]:
+        waiting.remove(i)
+        if not any(chunks[k][:2] == (kind, l) for k in waiting):
             out(R.w[kind], R.w_o[kind].at[l], R.w[kind].at[l])
 
     steps = (g_z, g_1, g_2, g_core, g_ready)
-    other_steps = (h_y, h_z, g_core, g_ready)
+    other_steps = (h_z, h_y, g_core, g_ready)
     reached = [0] * len(chunks)
+    waiting = list(range(len(chunks)))
     turns = iter(FORWARD_TURNS)
 
     def turn():
         for i in next(turns):
-            (steps if FORWARD_SPLIT[i] else other_steps)[reached[i]](i)
+            (other_steps if FORWARD_SPLIT[i] == 5 else steps)[reached[i]](i)
             reached[i] += 1
 
     steps[0](0)
@@ -844,28 +847,31 @@
     meta_cp = start(remote(R.metab.at[0], R.metab.at[1], R.xs.at[0], R.xr.at[0], me.cn))
     wide = R.vectors.shape[2]
     lane = lax.broadcasted_iota(jnp.int32, (R.vectors.shape[0], 128), 1)
-    R.vecg[f] = jnp.zeros((32, 128), BF)
+    spot = R.vecg.at[2 * y + c]
+    spot[...] = jnp.zeros((32, 128), BF)
     for l in range(2):
         block = jnp.concatenate([R.vectors[:, l]] * (128 // wide), axis=1)
         block = jnp.where(lax.div(lane, wide) == lax.rem(f, 128 // wide), block, 0.0)
         block = jnp.concatenate([block, jnp.zeros((16 - block.shape[0], 128), F32)], axis=0)
-        R.vecg[f, 16 * l : 16 * l + 16] = block.astype(BF)
+        spot[16 * l : 16 * l + 16] = block.astype(BF)
+    vec_cps = [start(remote(spot, spot, R.vs.at[at], R.vr.at[at], dev)) for at, dev in enumerate((me.yn, me.cn, me.en))]
+    for cp in vec_cps:
+        cp.wait_recv()
+    spot = R.vecl.at[z]
+    spot[...] = jnp.sum(R.vecg[...].astype(F32), axis=0).astype(BF)
     vec_cps = []
-    for s in range(1, shards):
-        spot = R.vecg.at[f]
-        vec_cps.append((s, remote(spot, spot, R.vs.at[s - 1], R.vr.at[s - 1], (r, lax.rem(f + s, shards)))))
-    for _, cp in vec_cps:
-        start(cp)
+    for s in range(1, levels):
+        vec_cps.append(start(remote(spot, spot, R.vs.at[2 + s], R.vr.at[2 + s], me.zn(s, levels)[1])))
     turn()
     meta_cp.wait_recv()
-    for _, cp in vec_cps:
+    for cp in vec_cps:
         cp.wait_recv()
     keep = stays.astype(F32)
     msel = R.msel
     msel[...] = (R.metab[0].astype(F32) * keep + R.metab[1].astype(F32) * (1.0 - keep)).astype(BF)
     vec = R.vec
     for zz in range(levels):
-        vec[:, 128 * zz : 128 * zz + 128] = jnp.sum(R.vecg[4 * zz : 4 * zz + 4].astype(F32), axis=0)
+        vec[:, 128 * zz : 128 * zz + 128] = R.vecl[zz].astype(F32)
     tag_row = msel[2 * S : 2 * S + 16].astype(F32)[:1]
     tag_row = jnp.concatenate([tag_row] * (D // 128), axis=1)
     low, high, spots = lane_masks()
@@ -938,6 +944,8 @@
 
         for j in range(D // 128):
             turn()
+            if l == 1 and j == COTANGENT_AT:
+                go_or_stay(stays, cot_near.start, cot_far.start)
             pair(j)
         turn()
         out(R.lse, R.lse_o.at[l])
@@ -989,8 +997,6 @@
         for b in range(FF // D):
             if b % 2 == 0:
                 turn()
-            if l == 1 and b == COTANGENT_AT:
-                go_or_stay(stays, cot_near.start, cot_far.start)
             inner(b)
         out(R.G, R.g_o.at[l])
         out(R.Gp, R.gp_o.at[l])
@@ -1067,7 +1073,6 @@
     peers = [me.zn(s, levels)[1] for s in range(1, levels)] + [me.xn, me.yn, me.cn, me.dn]
     for peer in peers:
         pl.semaphore_signal(barrier, inc=1, device_id=peer, device_id_type=MESH)
-    pl.semaphore_wait(barrier, len(peers))
 
     pending = []
 
@@ -1081,7 +1086,6 @@
     y_near = pltpu.make_async_copy(R.y_o, R.yo, R.ssem.at[3])
     dx_cps = []
 
-    go_or_stay(stays, y_near.start, y_far.start)
 
     gs, gr = R.gs, R.gr
     chunks = [(kind, l) for l in (1, 0) for kind in (KIND_F, KIND_I, KIND_O, KIND_Q, KIND_K, KIND_V)]
@@ -1119,10 +1123,6 @@
             start(remote(g.at[l, c, second, 1 - y, r], quarter.at[l, second], gs.at[i, 4], gr.at[i, 4], me.yn)),
         ]
 
-    def level_spot(kind, l, s):
-        ref = R.level[kind]
-        return ref.at[l, s, 0, 0] if len(ref.shape) == 6 else ref.at[l, s]
-
     def rs_3(i):
         kind, l = chunks[i]
         g = R.g[kind]
@@ -1134,7 +1134,7 @@
         for s in range(1, levels):
             there, dev = me.zn(s, levels)
             flight[i].append(
-                start(remote(g.at[l, c, there, y, r], level_spot(kind, l, s - 1), gs.at[i, 4 + s], gr.at[i, 4 + s], dev))
+                start(remote(g.at[l, c, there, y, r], R.level[kind].at[l, s - 1, 0], gs.at[i, 4 + s], gr.at[i, 4 + s], dev))
             )
 
     def rs_4(i):
@@ -1142,7 +1142,7 @@
         g, fin = R.g[kind], R.total[kind]
         total = g[l, c, z, y, r].astype(F32)
         for s in range(levels - 1):
-            total = total + level_spot(kind, l, s)[...].astype(F32)
+            total = total + R.level[kind][l, s, 0].astype(F32)
         fin[l, r] = total.astype(BF)
         flight[i] = [start(remote(fin.at[l, r], fin.at[l, r], gs.at[i, 4 + levels], gr.at[i, 4 + levels], me.xn))]
 
@@ -1181,42 +1181,40 @@
             total = total + vb[l, s]
         vt[16 * l : 16 * l + 16] = total
 
+    def hs_y(i):
+        kind, l = chunks[i]
+        g = R.g[kind]
+        g[l, c] = g[l, c] + (g[0, 0] if l == 1 else R.landing[kind][...])
+        spot = R.half[kind].at[l]
+        flight[i] = [start(remote(g.at[l, c, :, 1 - y], spot, gs.at[i, levels], gr.at[i, levels], me.yn))]
+
     def hs_z(i):
         kind, l = chunks[i]
         g = R.g[kind]
-        g[l, c] = g[l, c] + (g[0, 0] if l == 1 else R.landing[kind][...])
+        g[l, c, :, y] = g[l, c, :, y] + R.half[kind][l]
         flight[i] = []
         for s in range(1, levels):
             there, dev = me.zn(s, levels)
-            flight[i].append(
-                start(remote(g.at[l, c, there], R.level[kind].at[l, s - 1], gs.at[i, s], gr.at[i, s], dev))
-            )
-
-    def hs_y(i):
-        kind, l = chunks[i]
-        g = R.g[kind]
-        whole = g[l, c, z].astype(F32)
-        for s in range(levels - 1):
-            whole = whole + R.level[kind][l, s].astype(F32)
-        g[l, c, z] = whole.astype(BF)
-        spot = R.half[kind].at[l, 0]
-        flight[i] = [start(remote(g.at[l, c, z, 1 - y], spot, gs.at[i, levels], gr.at[i, levels], me.yn))]
+            spot = R.level[kind].at[l, s - 1]
+            flight[i].append(start(remote(g.at[l, c, there, y], spot, gs.at[i, s], gr.at[i, s], dev)))
 
     def hs_x(i):
         kind, l = chunks[i]
         g = R.g[kind]
-        g[l, c, z, y] = g[l, c, z, y] + R.half[kind][l, 0]
-        spot = R.quarter[kind].at[l, 0]
+        whole = g[l, c, z, y].astype(F32)
+        for s in range(levels - 1):
+            whole = whole + R.level[kind][l, s].astype(F32)
+        g[l, c, z, y] = whole.astype(BF)
+        spot = R.quarter[kind].at[l, pl.ds(0, 2)]
         sems = gs.at[i, levels + 1], gr.at[i, levels + 1]
-        flight[i] = [start(remote(g.at[l, c, z, y, 1 - r], spot, *sems, me.xn))]
+        flight[i] = [start(remote(g.at[l, c, z, y], spot, *sems, me.xn))]
 
     def hs_end(i):
         kind, l = chunks[i]
-        g, fin = R.g[kind], R.total[kind]
-        fin[l, r] = g[l, c, z, y, r] + R.quarter[kind][l, 0]
-        flight[i] = [start(remote(fin.at[l, r], fin.at[l, r], gs.at[i, 4 + levels], gr.at[i, 4 + levels], me.xn))]
-
-    other_steps = (rs_core, hs_z, hs_y, hs_x, hs_end, rs_5)
+        R.total[kind][l] = R.g[kind][l, c, z, y] + R.quarter[kind][l, :2]
+        rs_5(i)
+
+    other_steps = (rs_core, hs_y, hs_z, hs_x, hs_end)
     matrix_steps = (rs_core, rs_1, rs_2, rs_3, rs_4, rs_5)
     vec_steps = (vec_hop(0, me.cn), vec_hop(1, me.xn), vec_hop(2, me.yn), vec_level, vec_end)
     turns = iter(BACKWARD_TURNS)
@@ -1226,8 +1224,8 @@
             at = stage.get(i, 0)
             for cp in flight.pop(i, ()):
                 cp.wait_recv()
-            known = matrix_steps if i < len(BACKWARD_SPLIT) and BACKWARD_SPLIT[i] else other_steps
-            (vec_steps if chunks[i][0] is None else known)[at](i)
+            known = vec_steps if chunks[i][0] is None else other_steps if BACKWARD_SPLIT[i] == 5 else matrix_steps
+            known[at](i)
             stage[i] = at + 1
 
     for cp in small:
@@ -1282,6 +1280,9 @@
         put(7, jnp.sum(s7, axis=0, keepdims=True))
         put(8, jnp.sum(s8, axis=0, keepdims=True))
         put(9, jnp.sum(s9, axis=0, keepdims=True))
+        if l == 1:
+            pl.semaphore_wait(barrier, len(peers))
+            go_or_stay(stays, y_near.start, y_far.start)
         turn()
         G = use(R.G)
         gf = R.g[KIND_F]
@@ -1498,10 +1499,14 @@
     sources, _ = jax.tree.flatten((R.fin, R.fvec, R.y, R.dx, R.masters, R.firsts, R.seconds))
     places, tree = jax.tree.flatten(R.inside)
     copies = [pltpu.make_async_copy(s, p, R.isem.at[at]) for at, (s, p) in enumerate(zip(sources, places))]
-    for cp in copies:
-        cp.start()
     fin, fvec, y, dx, masters, firsts, seconds = R.inside
     waits = tree.unflatten(copies)
+    waits[3].start()
+    waits[2].start()
+    for at, kinds in ((2, (KIND_I,)), (3, (KIND_F,)), (1, (KIND_O,)), (0, (KIND_Q, KIND_K, KIND_V)), (4, ())):
+        for cp in [waits[0][k] for k in kinds] + [w[at] for w in waits[4:]]:
+            cp.start()
+    waits[1].start()
     finals = (R.new_masters, R.new_firsts, R.new_seconds)
     leaving = []
 
@@ -1523,6 +1528,11 @@
         for kept, final in zip((masters, firsts, seconds), finals):
             leave(kept[at], final[at])
 
+    waits[3].wait()
+    R.wide[...] = dx[...].astype(F32)
+    leave(R.wide, R.grad.at[0])
+    waits[2].wait()
+    leave(y, R.out.at[0])
     D = dx.shape[1]
     for at, kind in ((2, KIND_I), (3, KIND_F), (1, KIND_O)):
         arrive(at, (kind,))
@@ -1550,11 +1560,6 @@
             grad = jnp.where(slot == s, block[:, s * wide : s * wide + wide], grad)
         step(4, (slice(None), l), grad[:rows])
     done(4)
-    waits[2].wait()
-    leave(y, R.out.at[0])
-    waits[3].wait()
-    R.wide[...] = dx[...].astype(F32)
-    leave(R.wide, R.grad.at[0])
     for cp in leaving:
         cp.wait()
 
@@ -1616,7 +1621,8 @@
         ForwardScratch(
             w=tuple(V((2,) + tail, BF) for tail in w_tail),
             stages=tuple(V(m.shape, F32) for m in masters[:4]),
-            vecg=V((shards, 32, 128), BF),
+            vecg=V((4, 32, 128), BF),
+            vecl=V((levels, 32, 128), BF),
             vec=V((32, D), F32),
             metab=V((2,) + meta_shape, BF),
             msel=V(meta_shape, BF),
@@ -1648,8 +1654,8 @@
             osem=dma((48,)),
             gs=dma((16, levels + 4)),
             gr=dma((16, levels + 4)),
-            vs=dma((shards - 1,)),
-            vr=dma((shards - 1,)),
+            vs=dma((levels + 2,)),
+            vr=dma((levels + 2,)),
             xs=dma((3,)),
             xr=dma((3,)),
             ks=dma((2, 2)),
@@ -1686,9 +1692,7 @@
             landing=each(levels, 2, 2),
             half=each(2, levels, 2),
             quarter=each(2, levels),
-            level=tuple(
-                V((2, levels - 1) + ((2, 2) if k in WHOLE_LEVEL_KINDS else ()) + tail, BF) for k, tail in zip(KINDS, tails)
-            ),
+            level=each(2, levels - 1, 2),
             total=each(2, 2),
             w=tuple(V(tail, BF) for tail in w_tail),
             AT=V((D, S), BF),

time: 182 us -> 180 us (0.989)
  Pallas kernels: 180 us -> 177 us
    pallas_call x3, Pallas kernels: 180 us -> 177 us  [call_kernel(): pl.pallas_call(functools.partial(kernel, empty), out_shape=out_leaves, in...]
where the time goes in v4:
time: 180 us; the launch traced here: 179 us
  Pallas kernels  177 us (98%)
  between operations  2.21 us (1%)
    pallas_call x3, Pallas kernels, call_kernel(): pl.pallas_call(functools.partial(kernel, empty), out_shape=out_leaves, in...  177 us

profile of v4, /device:TPU:0, one launch (start us, length us, event | category | flops | bytes accessed | tf_op | source)
XLA Modules:
  0.0 179.3 jit_solution(4160476785813489128)
XLA Ops:
  1.9 88.0 %shard_map.323 = (bf16[2,4,2,2,2,16,512]{6,5,4,3,2,1,0:T(8,128)(2,1)}, bf16[2,4,2,2,2,16,512]{6,5,4,3,2,1,0:T(8,128)(2,1)}, bf16[2,4,2,2,2,16,512]{6,5,4,3,2,1,0...) custom-call(bf16[1,512,512]{2,1,0:T(8,128)(2,1)} %refs_0_.1, ...), custom_call_target="tpu_custom_call" | custom-call | tf_op jit(solution)/shard_map/pallas_call | solution.py:626
  89.9 83.3 %shard_map.324 = (bf16[2,2,16,512]{3,2,1,0:T(8,128)(2,1)}, bf16[2,2,16,512]{3,2,1,0:T(8,128)(2,1)}, bf16[2,2,16,512]{3,2,1,0:T(8,128)(2,1)}, bf16[2,2,16,512]{3,...) custom-call(bf16[2,4,2,2,2,16,512]{6,5,4,3,2,1,0:T(8,128)(2,1)} %get, ...), custom_call_target="tpu_custom_call" | custom-call | tf_op jit(solution)/shard_map/pallas_call | solution.py:626
  173.3 5.7 %shard_map.325 = (bf16[1,512,512]{2,1,0:T(8,128)(2,1)}, f32[1,512,512]{2,1,0:T(8,128)}, f32[2,32,1536]{2,1,0:T(8,128)}, f32[2,32,512]{2,1,0:T(8,128)}, f32[2,32,...) custom-call(bf16[2,2,16,512]{3,2,1,0:T(8,128)(2,1)} %get-tuple-eleme, ...), custom_call_target="tpu_custom_call" | custom-call | tf_op jit(solution)/shard_map/pallas_call | solution.py:626

commit v5 on v4

--- a/solution.py
+++ b/solution.py
@@ -355,74 +355,74 @@
 MESH = pl.DeviceIdType.MESH
 KIND_K, KIND_V, KIND_Q, KIND_O, KIND_I, KIND_F = KINDS = tuple(range(6))
 VMEM_BYTES = 60 << 20
-FORWARD_SPLIT = (1, 1, 2, 1, 1, 1, 1, 1, 5, 5, 5, 1, 1, 2, 2, 5)
-BACKWARD_SPLIT = (1, 2, 5, 1, 1, 5, 2, 2, 5, 3, 1, 5)
+FORWARD_SPLIT = (1, 1, 1, 2, 1, 1, 1, 1, 5, 5, 1, 1, 1, 1, 5, 5)
+BACKWARD_SPLIT = (1, 2, 1, 2, 5, 1, 5, 2, 5, 1, 1, 1, 5, 2, 5, 5)
 FORWARD_TURNS = (
     (1, 2, 0, 3, 4, 1, 2, 5),
-    (3, 0, 6, 1, 2, 4, 7, 3, 0, 5, 0, 1, 8),
-    (2, 6, 4, 1, 9),
-    (2,),
+    (3, 0, 6, 1, 2, 4, 3, 0, 7, 5, 0, 1, 8),
+    (6, 2, 9, 1),
+    (4, 7, 2, 3),
+    (10, 5),
+    (6, 11),
+    (3, 8, 12),
     (),
-    (7, 3, 5, 10),
-    (6,),
-    (11, 3, 8),
-    (4, 9, 12, 7),
+    (4, 9, 10, 13, 7),
+    (11, 14),
+    (4,),
+    (),
+    (5, 8, 12, 9, 13, 5, 15),
+    (6, 9, 8, 10, 6, 7, 14, 11, 12, 13, 7),
+    (10,),
+    (),
+    (),
+    (15, 10),
+    (),
+    (),
+    (11, 14),
+    (12,),
+    (11, 14),
+    (12,),
     (13,),
     (),
-    (4, 10),
-    (5, 11, 14, 8, 12, 5, 15),
-    (6, 8, 13, 9, 6, 10, 14, 9, 7, 11, 10, 12, 7),
-    (13,),
-    (14, 15),
-    (),
-    (11,),
-    (),
-    (),
-    (11,),
-    (12,),
-    (),
-    (13, 12),
-    (),
-    (),
-    (13, 14),
-    (15, 14, 15),
+    (15, 13),
+    (15,),
     (),
 )
-COTANGENT_AT = 0
+COTANGENT_AT = 2
 BACKWARD_TURNS = (
     (),
     (),
-    (0,),
+    (0, 1),
     (),
     (),
+    (2, 0, 3),
+    (),
+    (1,),
+    (2, 4),
+    (3, 4, 0),
     (1,),
     (),
-    (0,),
-    (2,),
-    (2, 1),
+    (2, 4),
+    (5,),
+    (7, 3, 0, 6),
     (),
-    (2,),
-    (0,),
-    (3,),
-    (4, 5),
+    (5, 1, 16, 7),
+    (2, 6, 4, 16),
+    (0, 8, 3, 5, 7, 9),
+    (4,),
+    (16, 1, 6, 8, 0),
+    (5, 7, 10, 11, 9, 2, 16, 1),
     (),
-    (2, 3, 12),
-    (4, 5, 1, 12),
-    (6, 2, 0, 3),
-    (),
-    (),
-    (4, 5, 7),
-    (6,),
-    (12, 1),
-    (3, 8),
-    (4, 0, 8, 7),
-    (6, 0, 5, 12),
-    (8, 1),
-    (4, 3, 12),
-    (9,),
-    (11, 10),
-    (7, 5, 8, 9),
-    (11, 13, 1, 10, 4, 3, 6, 13, 7, 8, 9, 11, 6, 10, 13, 9, 7, 6, 10, 13, 11, 7, 9, 10, 11, 13, 9, 10),
+    (10,),
+    (3, 12, 11),
+    (8, 12, 2, 5, 6, 9),
+    (7, 16),
+    (3, 12, 10),
+    (8, 5, 11),
+    (13, 6, 9),
+    (7, 12, 14, 10, 15),
+    (13,),
+    (8, 17, 14, 11, 15, 12, 17, 9, 10, 13, 14, 11, 15, 17, 9, 10, 14, 13, 11, 17, 15, 14, 13, 17, 15, 13),
 )
 
 
@@ -1088,67 +1088,82 @@
 
 
     gs, gr = R.gs, R.gr
-    chunks = [(kind, l) for l in (1, 0) for kind in (KIND_F, KIND_I, KIND_O, KIND_Q, KIND_K, KIND_V)]
+    chunks = []
+    for l in (1, 0):
+        for kind in (KIND_F, KIND_I, KIND_O, KIND_Q, KIND_K, KIND_V):
+            rows, cols = R.g[kind].shape[-2:]
+            if kind == KIND_F:
+                spans = [(slice(0, rows // 2), slice(0, cols)), (slice(rows // 2, rows), slice(0, cols))]
+            elif kind == KIND_I:
+                spans = [(slice(0, rows), slice(0, cols // 2)), (slice(0, rows), slice(cols // 2, cols))]
+            else:
+                spans = [(slice(0, rows), slice(0, cols))]
+            chunks += [(kind, l, *span) for span in spans]
     chunks += [(None, 1), (None, 0)]
     flight = {}
     stage = {}
     fin_copies = []
 
     def rs_core(i):
-        kind, l = chunks[i]
+        kind, l, rs, cs = chunks[i]
         g = R.g[kind]
-        spot = g.at[0, 0] if l == 1 else R.landing[kind]
-        flight[i] = [start(remote(g.at[l, 1 - c], spot, gs.at[i, 0], gr.at[i, 0], me.cn))]
+        spot = g.at[0, 0, :, :, :, rs, cs] if l == 1 else R.landing[kind].at[:, :, :, rs, cs]
+        mine = g.at[l, 1 - c, :, :, :, rs, cs]
+        flight[i] = [start(remote(mine, spot, gs.at[i, 0], gr.at[i, 0], me.cn))]
+
+    def add_landed(i):
+        kind, l, rs, cs = chunks[i]
+        g = R.g[kind]
+        landed = g[0, 0, :, :, :, rs, cs] if l == 1 else R.landing[kind][:, :, :, rs, cs]
+        g[l, c, :, :, :, rs, cs] = g[l, c, :, :, :, rs, cs] + landed
 
     def rs_1(i):
-        kind, l = chunks[i]
-        g = R.g[kind]
+        kind, l, rs, cs = chunks[i]
+        g, half = R.g[kind], R.half[kind]
         first, second = halves(BACKWARD_SPLIT[i], levels)
-        half, quarter = R.half[kind], R.quarter[kind]
-        g[l, c] = g[l, c] + (g[0, 0] if l == 1 else R.landing[kind][...])
+        add_landed(i)
+        a, b = g.at[l, c, first, 1 - y, :, rs, cs], g.at[l, c, second, :, 1 - r, rs, cs]
         flight[i] = [
-            start(remote(g.at[l, c, first, 1 - y], half.at[l, first], gs.at[i, 1], gr.at[i, 1], me.yn)),
-            start(remote(g.at[l, c, second, :, 1 - r], half.at[l, second], gs.at[i, 2], gr.at[i, 2], me.xn)),
+            start(remote(a, half.at[l, first, :, rs, cs], gs.at[i, 1], gr.at[i, 1], me.yn)),
+            start(remote(b, half.at[l, second, :, rs, cs], gs.at[i, 2], gr.at[i, 2], me.xn)),
         ]
 
     def rs_2(i):
-        kind, l = chunks[i]
-        g = R.g[kind]
+        kind, l, rs, cs = chunks[i]
+        g, half, quarter = R.g[kind], R.half[kind], R.quarter[kind]
         first, second = halves(BACKWARD_SPLIT[i], levels)
-        half, quarter = R.half[kind], R.quarter[kind]
-        g[l, c, first, y] = g[l, c, first, y] + half[l, first]
-        g[l, c, second, :, r] = g[l, c, second, :, r] + half[l, second]
+        g[l, c, first, y, :, rs, cs] = g[l, c, first, y, :, rs, cs] + half[l, first, :, rs, cs]
+        g[l, c, second, :, r, rs, cs] = g[l, c, second, :, r, rs, cs] + half[l, second, :, rs, cs]
+        a, b = g.at[l, c, first, y, 1 - r, rs, cs], g.at[l, c, second, 1 - y, r, rs, cs]
         flight[i] = [
-            start(remote(g.at[l, c, first, y, 1 - r], quarter.at[l, first], gs.at[i, 3], gr.at[i, 3], me.xn)),
-            start(remote(g.at[l, c, second, 1 - y, r], quarter.at[l, second], gs.at[i, 4], gr.at[i, 4], me.yn)),
+            start(remote(a, quarter.at[l, first, rs, cs], gs.at[i, 3], gr.at[i, 3], me.xn)),
+            start(remote(b, quarter.at[l, second, rs, cs], gs.at[i, 4], gr.at[i, 4], me.yn)),
         ]
 
     def rs_3(i):
-        kind, l = chunks[i]
-        g = R.g[kind]
+        kind, l, rs, cs = chunks[i]
+        g, quarter = R.g[kind], R.quarter[kind]
         first, second = halves(BACKWARD_SPLIT[i], levels)
-        half, quarter = R.half[kind], R.quarter[kind]
-        g[l, c, first, y, r] = g[l, c, first, y, r] + quarter[l, first]
-        g[l, c, second, y, r] = g[l, c, second, y, r] + quarter[l, second]
+        g[l, c, first, y, r, rs, cs] = g[l, c, first, y, r, rs, cs] + quarter[l, first, rs, cs]
+        g[l, c, second, y, r, rs, cs] = g[l, c, second, y, r, rs, cs] + quarter[l, second, rs, cs]
         flight[i] = []
         for s in range(1, levels):
             there, dev = me.zn(s, levels)
-            flight[i].append(
-                start(remote(g.at[l, c, there, y, r], R.level[kind].at[l, s - 1, 0], gs.at[i, 4 + s], gr.at[i, 4 + s], dev))
-            )
+            mine, spot = g.at[l, c, there, y, r, rs, cs], R.level[kind].at[l, s - 1, 0, rs, cs]
+            flight[i].append(start(remote(mine, spot, gs.at[i, 4 + s], gr.at[i, 4 + s], dev)))
 
     def rs_4(i):
-        kind, l = chunks[i]
-        g, fin = R.g[kind], R.total[kind]
-        total = g[l, c, z, y, r].astype(F32)
+        kind, l, rs, cs = chunks[i]
+        total = R.g[kind][l, c, z, y, r, rs, cs].astype(F32)
         for s in range(levels - 1):
-            total = total + R.level[kind][l, s, 0].astype(F32)
-        fin[l, r] = total.astype(BF)
-        flight[i] = [start(remote(fin.at[l, r], fin.at[l, r], gs.at[i, 4 + levels], gr.at[i, 4 + levels], me.xn))]
+            total = total + R.level[kind][l, s, 0, rs, cs].astype(F32)
+        R.total[kind][l, r, rs, cs] = total.astype(BF)
+        spot = R.total[kind].at[l, r, rs, cs]
+        flight[i] = [start(remote(spot, spot, gs.at[i, 4 + levels], gr.at[i, 4 + levels], me.xn))]
 
     def rs_5(i):
-        kind, l = chunks[i]
-        cp = pltpu.make_async_copy(R.total[kind].at[l], R.fin[kind].at[l], R.fsem.at[i])
+        kind, l, rs, cs = chunks[i]
+        cp = pltpu.make_async_copy(R.total[kind].at[l, :, rs, cs], R.fin[kind].at[l, :, rs, cs], R.fsem.at[i])
         cp.start()
         fin_copies.append(cp)
 
@@ -1182,36 +1197,35 @@
         vt[16 * l : 16 * l + 16] = total
 
     def hs_y(i):
-        kind, l = chunks[i]
+        kind, l, rs, cs = chunks[i]
+        add_landed(i)
+        mine, spot = R.g[kind].at[l, c, :, 1 - y, :, rs, cs], R.half[kind].at[l, :, :, rs, cs]
+        flight[i] = [start(remote(mine, spot, gs.at[i, levels], gr.at[i, levels], me.yn))]
+
+    def hs_z(i):
+        kind, l, rs, cs = chunks[i]
         g = R.g[kind]
-        g[l, c] = g[l, c] + (g[0, 0] if l == 1 else R.landing[kind][...])
-        spot = R.half[kind].at[l]
-        flight[i] = [start(remote(g.at[l, c, :, 1 - y], spot, gs.at[i, levels], gr.at[i, levels], me.yn))]
-
-    def hs_z(i):
-        kind, l = chunks[i]
-        g = R.g[kind]
-        g[l, c, :, y] = g[l, c, :, y] + R.half[kind][l]
+        g[l, c, :, y, :, rs, cs] = g[l, c, :, y, :, rs, cs] + R.half[kind][l, :, :, rs, cs]
         flight[i] = []
         for s in range(1, levels):
             there, dev = me.zn(s, levels)
-            spot = R.level[kind].at[l, s - 1]
-            flight[i].append(start(remote(g.at[l, c, there, y], spot, gs.at[i, s], gr.at[i, s], dev)))
+            mine, spot = g.at[l, c, there, y, :, rs, cs], R.level[kind].at[l, s - 1, :, rs, cs]
+            flight[i].append(start(remote(mine, spot, gs.at[i, s], gr.at[i, s], dev)))
 
     def hs_x(i):
-        kind, l = chunks[i]
+        kind, l, rs, cs = chunks[i]
         g = R.g[kind]
-        whole = g[l, c, z, y].astype(F32)
+        whole = g[l, c, z, y, :, rs, cs].astype(F32)
         for s in range(levels - 1):
-            whole = whole + R.level[kind][l, s].astype(F32)
-        g[l, c, z, y] = whole.astype(BF)
-        spot = R.quarter[kind].at[l, pl.ds(0, 2)]
+            whole = whole + R.level[kind][l, s, :, rs, cs].astype(F32)
+        g[l, c, z, y, :, rs, cs] = whole.astype(BF)
+        mine, spot = g.at[l, c, z, y, :, rs, cs], R.quarter[kind].at[l, pl.ds(0, 2), rs, cs]
         sems = gs.at[i, levels + 1], gr.at[i, levels + 1]
-        flight[i] = [start(remote(g.at[l, c, z, y], spot, *sems, me.xn))]
+        flight[i] = [start(remote(mine, spot, *sems, me.xn))]
 
     def hs_end(i):
-        kind, l = chunks[i]
-        R.total[kind][l] = R.g[kind][l, c, z, y] + R.quarter[kind][l, :2]
+        kind, l, rs, cs = chunks[i]
+        R.total[kind][l, :, rs, cs] = R.g[kind][l, c, z, y, :, rs, cs] + R.quarter[kind][l, :2, rs, cs]
         rs_5(i)
 
     other_steps = (rs_core, hs_y, hs_z, hs_x, hs_end)
@@ -1732,9 +1746,9 @@
             vt=V((32, 128), F32),
             lsem=dma((2, 20)),
             ssem=dma((7,)),
-            fsem=dma((12,)),
-            gs=dma((12, levels + 5)),
-            gr=dma((12, levels + 5)),
+            fsem=dma((16,)),
+            gs=dma((16, levels + 5)),
+            gr=dma((16, levels + 5)),
             xs=dma((3,)),
             xr=dma((3,)),
             ks=dma((2, 2, 2)),

time: 180 us -> 179 us (level)
  no operation moved by 1% of the time
where the time goes in v5:
time: 179 us
  Pallas kernels  177 us (99%)
  between operations  2.21 us (1%)
    pallas_call x3, Pallas kernels, call_kernel(): pl.pallas_call(functools.partial(kernel, empty), out_shape=out_leaves, in...  177 us

profile of v5, /device:TPU:0, one launch (start us, length us, event | category | flops | bytes accessed | tf_op | source)
XLA Modules:
  0.0 178.8 jit_solution(3595102943948781952)
XLA Ops:
  1.9 85.8 %shard_map.323 = (bf16[2,4,2,2,2,16,512]{6,5,4,3,2,1,0:T(8,128)(2,1)}, bf16[2,4,2,2,2,16,512]{6,5,4,3,2,1,0:T(8,128)(2,1)}, bf16[2,4,2,2,2,16,512]{6,5,4,3,2,1,0...) custom-call(bf16[1,512,512]{2,1,0:T(8,128)(2,1)} %refs_0_.1, ...), custom_call_target="tpu_custom_call" | custom-call | tf_op jit(solution)/shard_map/pallas_call | solution.py:626
  87.8 85.1 %shard_map.324 = (bf16[2,2,16,512]{3,2,1,0:T(8,128)(2,1)}, bf16[2,2,16,512]{3,2,1,0:T(8,128)(2,1)}, bf16[2,2,16,512]{3,2,1,0:T(8,128)(2,1)}, bf16[2,2,16,512]{3,...) custom-call(bf16[2,4,2,2,2,16,512]{6,5,4,3,2,1,0:T(8,128)(2,1)} %get, ...), custom_call_target="tpu_custom_call" | custom-call | tf_op jit(solution)/shard_map/pallas_call | solution.py:626
  172.9 5.7 %shard_map.325 = (bf16[1,512,512]{2,1,0:T(8,128)(2,1)}, f32[1,512,512]{2,1,0:T(8,128)}, f32[2,32,1536]{2,1,0:T(8,128)}, f32[2,32,512]{2,1,0:T(8,128)}, f32[2,32,...) custom-call(bf16[2,2,16,512]{3,2,1,0:T(8,128)(2,1)} %get-tuple-eleme, ...), custom_call_target="tpu_custom_call" | custom-call | tf_op jit(solution)/shard_map/pallas_call | solution.py:626

commit v6 on v5

--- a/solution.py
+++ b/solution.py
@@ -482,6 +482,7 @@
     stages: object
     vecg: object
     vecl: object
+    vecs: object
     vec: object
     metab: object
     msel: object
@@ -697,6 +698,9 @@
     FF = R.G.shape[1]
     source = ((0, D), (0, 2 * D), (0, 0), (1, 0), (2, 0), (3, 0))
 
+    R.vecs[...] = jnp.zeros(R.vecs.shape, F32)
+    vec_load = pltpu.make_async_copy(R.vectors, R.vecs.at[pl.ds(0, R.vectors.shape[0])], R.xsem.at[0])
+    vec_load.start()
     half_loads = {}
     for l in range(2):
         for at, (master, stage) in enumerate(zip(R.masters, R.stages)):
@@ -846,13 +850,13 @@
     R.metab[0, 2 * S :] = jnp.full((16, 128), R.tags[0].astype(F32)).astype(BF)
     meta_cp = start(remote(R.metab.at[0], R.metab.at[1], R.xs.at[0], R.xr.at[0], me.cn))
     wide = R.vectors.shape[2]
-    lane = lax.broadcasted_iota(jnp.int32, (R.vectors.shape[0], 128), 1)
+    lane = lax.broadcasted_iota(jnp.int32, (16, 128), 1)
+    vec_load.wait()
     spot = R.vecg.at[2 * y + c]
     spot[...] = jnp.zeros((32, 128), BF)
     for l in range(2):
-        block = jnp.concatenate([R.vectors[:, l]] * (128 // wide), axis=1)
+        block = jnp.concatenate([R.vecs[:, l]] * (128 // wide), axis=1)
         block = jnp.where(lax.div(lane, wide) == lax.rem(f, 128 // wide), block, 0.0)
-        block = jnp.concatenate([block, jnp.zeros((16 - block.shape[0], 128), F32)], axis=0)
         spot[16 * l : 16 * l + 16] = block.astype(BF)
     vec_cps = [start(remote(spot, spot, R.vs.at[at], R.vr.at[at], dev)) for at, dev in enumerate((me.yn, me.cn, me.en))]
     for cp in vec_cps:
@@ -1512,7 +1516,12 @@
     f = lax.axis_index("fsdp")
     sources, _ = jax.tree.flatten((R.fin, R.fvec, R.y, R.dx, R.masters, R.firsts, R.seconds))
     places, tree = jax.tree.flatten(R.inside)
-    copies = [pltpu.make_async_copy(s, p, R.isem.at[at]) for at, (s, p) in enumerate(zip(sources, places))]
+    copies = []
+    for at, (s, p) in enumerate(zip(sources, places)):
+        if s.shape != p.shape:
+            p[...] = jnp.zeros(p.shape, p.dtype)
+            p = p.at[pl.ds(0, s.shape[0])]
+        copies.append(pltpu.make_async_copy(s, p, R.isem.at[at]))
     fin, fvec, y, dx, masters, firsts, seconds = R.inside
     waits = tree.unflatten(copies)
     waits[3].start()
@@ -1540,7 +1549,8 @@
 
     def done(at):
         for kept, final in zip((masters, firsts, seconds), finals):
-            leave(kept[at], final[at])
+            src = kept[at]
+            leave(src if src.shape == final[at].shape else src.at[pl.ds(0, final[at].shape[0])], final[at])
 
     waits[3].wait()
     R.wide[...] = dx[...].astype(F32)
@@ -1564,7 +1574,6 @@
     arrive(4, ())
     waits[1].wait()
     wide = masters[4].shape[2]
-    rows = masters[4].shape[0]
     span = 128 // wide
     slot = lax.rem(f, span)
     for l in range(2):
@@ -1572,7 +1581,7 @@
         grad = block[:, :wide]
         for s in range(1, span):
             grad = jnp.where(slot == s, block[:, s * wide : s * wide + wide], grad)
-        step(4, (slice(None), l), grad[:rows])
+        step(4, (slice(None), l), grad)
     done(4)
     for cp in leaving:
         cp.wait()
@@ -1637,6 +1646,7 @@
             stages=tuple(V(m.shape, F32) for m in masters[:4]),
             vecg=V((4, 32, 128), BF),
             vecl=V((levels, 32, 128), BF),
+            vecs=V((16,) + masters[4].shape[1:], F32),
             vec=V((32, D), F32),
             metab=V((2,) + meta_shape, BF),
             msel=V(meta_shape, BF),
@@ -1681,7 +1691,7 @@
             lengths=pl.BlockSpec(memory_space=pltpu.SMEM),
             tags=pl.BlockSpec(memory_space=pltpu.SMEM),
             key_mask=pl.BlockSpec(memory_space=pltpu.VMEM),
-            vectors=pl.BlockSpec(memory_space=pltpu.VMEM),
+            vectors=hbm,
             masters=(hbm,) * 4,
         ),
         collective_id=0,
@@ -1787,7 +1797,7 @@
                 V((32, 128), F32),
                 V((S, D), BF),
                 V((S, D), BF),
-                *(tuple(V(p.shape, F32) for p in masters) for _ in range(3)),
+                *((*(V(p.shape, F32) for p in masters[:4]), V((16,) + masters[4].shape[1:], F32)) for _ in range(3)),
             ),
             wide=V((S, D), F32),
             isem=dma((24,)),

time: 179 us -> 178 us (level)
  no operation moved by 1% of the time
where the time goes in v6:
time: 178 us; the launch traced here: 179 us
  Pallas kernels  177 us (99%)
  between operations  2.21 us (1%)
    pallas_call x3, Pallas kernels, call_kernel(): pl.pallas_call(functools.partial(kernel, empty), out_shape=out_leaves, in...  177 us

profile of v6, /device:TPU:0, one launch (start us, length us, event | category | flops | bytes accessed | tf_op | source)
XLA Modules:
  0.0 178.8 jit_solution(298423588593138431)
XLA Ops:
  1.9 85.8 %shard_map.323 = (bf16[2,4,2,2,2,16,512]{6,5,4,3,2,1,0:T(8,128)(2,1)}, bf16[2,4,2,2,2,16,512]{6,5,4,3,2,1,0:T(8,128)(2,1)}, bf16[2,4,2,2,2,16,512]{6,5,4,3,2,1,0...) custom-call(bf16[1,512,512]{2,1,0:T(8,128)(2,1)} %refs_0_.1, ...), custom_call_target="tpu_custom_call" | custom-call | tf_op jit(solution)/shard_map/pallas_call | solution.py:627
  87.7 85.1 %shard_map.324 = (bf16[2,2,16,512]{3,2,1,0:T(8,128)(2,1)}, bf16[2,2,16,512]{3,2,1,0:T(8,128)(2,1)}, bf16[2,2,16,512]{3,2,1,0:T(8,128)(2,1)}, bf16[2,2,16,512]{3,...) custom-call(bf16[2,4,2,2,2,16,512]{6,5,4,3,2,1,0:T(8,128)(2,1)} %get, ...), custom_call_target="tpu_custom_call" | custom-call | tf_op jit(solution)/shard_map/pallas_call | solution.py:627
  172.8 5.7 %shard_map.325 = (bf16[1,512,512]{2,1,0:T(8,128)(2,1)}, f32[1,512,512]{2,1,0:T(8,128)}, f32[2,32,1536]{2,1,0:T(8,128)}, f32[2,32,512]{2,1,0:T(8,128)}, f32[2,32,...) custom-call(bf16[2,2,16,512]{3,2,1,0:T(8,128)(2,1)} %get-tuple-eleme, ...), custom_call_target="tpu_custom_call" | custom-call | tf_op jit(solution)/shard_map/pallas_call | solution.py:627
